TPU v7x, 32 devices: a whole 2x2x4 slice. The times are simulated.
32 devices in a mesh: dom: 32 (over z, y, x, core).
Axes of the slice: x: 2, y: 2, z: 4, core: 2. Of those that a mesh axis runs over, the one named last changes fastest.
Arguments:
- positions: float32 [1024, 3, 128], P('dom'), may hold values from 0 to 6
- velocities: float32 [1024, 3, 128], P('dom'), may hold values from -6 to 6
- masses: float32 [1024, 128], P('dom'), may hold values from 0.035 to 0.13
- smoothing: float32 [1024, 128], P('dom'), may hold values from 0.8 to 1.4
- entropy: float32 [1024, 128], P('dom'), may hold values from 0.5 to 2
- export_blocks: int32 [32, 32, 32], P('dom'), may hold values from -1 to 31, as said below
- partner_slots: int32 [1024, 16], P('dom'), may hold values from 0 to 1023, as said below
- active: int32 [1024], P('dom'), may hold values from 0 to 1, as said below
Outputs:
- density: float32 [1024, 128], P('dom')
- divergence: float32 [1024, 128], P('dom')
- acceleration: float32 [1024, 3, 128], P('dom')
Inputs may be any that keep to these rules, and one draw needn't show every extreme that they name: `export_blocks`: entry [p, d, c] is the index within segment p of the block that p sends to segment d in slot c, or -1 for an empty slot. Filled slots come first; each segment receives 32 filled slots from a quarter of the segments, 16 from half of them and none from the rest. `partner_slots`: for a block of segment d, each entry is p * 32 + c for a filled slot c from segment p to d; every filled slot to d is named exactly once over d's blocks. Every segment has 1 to 32 active blocks, and some segment has all of them active.
All inputs are finite; a program needn't handle non-finite values.
Results may differ from a plain program's by a relative error of at most 0.00002.
Values sent between devices are 32-bit elements; how exact they have to be, the bound alone decides.
No kernel may reach another device: no remote copies, remote signals or barrier semaphores. Data moves between devices by JAX's collectives and lax.ppermute only.
A program may use at most 64 MiB of HBM per device.

v0:
```python
import jax
import jax.numpy as jnp
from jax import lax
from jax.sharding import PartitionSpec as P

kernel_norm = 3.3422538049298023


def kernel_parts(radius, smooth):
    ratio = radius / smooth
    tail = jnp.maximum(1.0 - ratio, 0.0)
    value = kernel_norm * tail**4 * (1.0 + 4.0 * ratio) / smooth**3
    slope = -20.0 * kernel_norm * tail**3 / smooth**5
    return (value, slope)


def separation(own_pos, near_pos):
    offset = own_pos[None, :, None, :] - near_pos[:, :, :, None]
    radius = jnp.sqrt(jnp.sum(offset * offset, axis=1))
    return (offset, radius)


def density_block(own_pos, own_vel, own_smooth, near_pos, near_vel, near_mass):
    offset, radius = separation(own_pos, near_pos)
    value, slope = kernel_parts(radius, own_smooth[None, None, :])
    weight = near_mass[:, :, None]
    density = jnp.sum(weight * value, axis=(0, 1))
    moving = own_vel[None, :, None, :] - near_vel[:, :, :, None]
    approach = jnp.sum(moving * offset, axis=1)
    divergence = -jnp.sum(weight * slope * approach, axis=(0, 1)) / density
    return (density, divergence)


def force_block(own_pos, own_smooth, own_press, near_pos, near_smooth, near_mass, near_press):
    offset, radius = separation(own_pos, near_pos)
    _, slope_own = kernel_parts(radius, own_smooth[None, None, :])
    _, slope_near = kernel_parts(radius, near_smooth[:, :, None])
    factor = near_mass[:, :, None] * (
        own_press[None, None, :] * slope_own + near_press[:, :, None] * slope_near
    )
    return -jnp.sum(factor[:, None] * offset, axis=(0, 2))


def per_device(
    positions, velocities, masses, smoothing, entropy, export_blocks, partner_slots, active
):
    blocks_here = positions.shape[0]
    capacity = export_blocks.shape[2]
    fields = jnp.concatenate(
        [positions, velocities, masses[:, None, :], smoothing[:, None, :]], axis=1
    )
    everything = lax.all_gather(fields, "dom", axis=0, tiled=True)
    tables = lax.all_gather(export_blocks, "dom", axis=0, tiled=True)
    column = lax.dynamic_index_in_dim(tables, lax.axis_index("dom"), axis=1, keepdims=False)
    senders = partner_slots // capacity
    remote_ids = senders * blocks_here + column[senders, partner_slots % capacity]
    remote = everything[remote_ids]
    local = jnp.broadcast_to(fields[None], (blocks_here,) + fields.shape)
    near = jnp.concatenate([local, remote], axis=1)

    def first_pass(member):
        own_fields, near_fields = member
        return density_block(
            own_fields[0:3],
            own_fields[3:6],
            own_fields[7],
            near_fields[:, 0:3],
            near_fields[:, 3:6],
            near_fields[:, 6],
        )

    density, divergence = lax.map(first_pass, (fields, near))
    pressure_term = entropy * jnp.power(density, -1.0 / 3.0)
    remote_press = lax.all_gather(pressure_term, "dom", axis=0, tiled=True)[remote_ids]
    local_press = jnp.broadcast_to(pressure_term[None], (blocks_here,) + pressure_term.shape)
    near_press = jnp.concatenate([local_press, remote_press], axis=1)

    def second_pass(own_fields, near_fields, own_press, other_press):
        return force_block(
            own_fields[0:3],
            own_fields[7],
            own_press,
            near_fields[:, 0:3],
            near_fields[:, 7],
            near_fields[:, 6],
            other_press,
        )

    def masked_pass(member):
        own_fields, near_fields, own_press, other_press = member
        return second_pass(own_fields, near_fields, own_press, other_press)

    acceleration = lax.map(masked_pass, (fields, near, pressure_term, near_press))
    acceleration = jnp.where(active[:, None, None] > 0, acceleration, 0.0)
    return (density, divergence, acceleration)


def solution(mesh):
    in_specs = (
        P("dom", None, None),
        P("dom", None, None),
        P("dom", None),
        P("dom", None),
        P("dom", None),
        P("dom", None, None),
        P("dom", None),
        P("dom"),
    )
    out_specs = (P("dom", None), P("dom", None), P("dom", None, None))
    return jax.shard_map(
        per_device, mesh=mesh, in_specs=in_specs, out_specs=out_specs, check_vma=False
    )
```

profile of v0, /device:TPU:0, one launch (start us, length us, event | category | flops | bytes accessed | tf_op | source)
XLA Modules:
  0.0 894.9 jit_solution(6234024082564609196)
XLA Ops:
  12.2 45.5 %all_gather.10 = s32[32,32,32]{2,1,0:T(8,128)S(1)} all-gather(s32[1,32,32]{2,1,0:T(8,128)} %param.17), channel_id=1, replica_groups=mesh['dom'=32] {'dom'}, dimensions={0}, use_global_device_ids=true | all-gather | bytes 135168 | tf_op jit(solution)/shard_map/all_gather | solution.py:53
  57.7 3.8 gather_fusion
  61.7 14.7 %all-gather.2.cloned.1.call-done = f32[1024,8,128]{2,1,0:T(8,128)} async-done(((f32[32,8,128]{2,1,0:T(8,128)}), f32[1024,8,128]{2,1,0:T(8,128)}) %all-gather.2.cloned.1.call-update) | async-done | bytes 4194320 | tf_op jit(solution)/shard_map/all_gather | solution.py:52
  83.8 389.5 %while.24 = (s32[]{:T(128)}, f32[32,128]{1,0:T(8,128)S(1)}, f32[32,128]{1,0:T(8,128)}, f32[32,48,8,128]{3,1,2,0:T(8,128)}, f32[32,8,128]{2,1,0:T(8,128)}) while((s32[]{:T(128)}, f32[32,128]{1,0:T(8,128)S(1)}, f32[32,128]{1,0:T(8,128)}, f32[32,48,8,128]{3,1,2,0:T(8,128)}, f32[32,8,128]{2,1,0:T(8,128)}) %tuple.74), condition=%wide.region_5.6_spmd.clone, body=%wide.region_0.5_spmd.sunk.clone | while | flops 26739200 | bytes 13812821 | solution.py:72
  85.6 6.3 fusion.51
  97.8 6.3 fusion.51
  110.0 6.3 fusion.51
  122.1 6.3 fusion.51
  134.3 6.3 fusion.51
  146.5 6.3 fusion.51
  158.7 6.3 fusion.51
  170.8 6.3 fusion.51
  183.0 6.3 fusion.51
  195.2 6.3 fusion.51
  207.3 6.3 fusion.51
  219.5 6.3 fusion.51
  231.7 6.3 fusion.51
  243.8 6.3 fusion.51
  256.0 6.3 fusion.51
  268.2 6.3 fusion.51
  280.4 6.3 fusion.51
  292.5 6.3 fusion.51
  304.7 6.3 fusion.51
  316.9 6.3 fusion.51
  329.0 6.3 fusion.51
  341.2 6.3 fusion.51
  353.4 6.3 fusion.51
  365.6 6.3 fusion.51
  377.7 6.3 fusion.51
  389.9 6.3 fusion.51
  402.1 6.3 fusion.51
  414.3 6.3 fusion.51
  426.4 6.3 fusion.51
  438.6 6.3 fusion.51
  450.8 6.3 fusion.51
  462.9 6.3 fusion.51
  473.4 40.5 %all_gather.11 = f32[1024,128]{1,0:T(8,128)S(1)} all-gather(f32[32,128]{1,0:T(8,128)S(1)} %power_multiply_fusion), channel_id=1, replica_groups=mesh['dom'=32] {'dom'}, dimensions={0}, use_global_device_ids=true | all-gather | bytes 540672 | tf_op jit(solution)/shard_map/all_gather | solution.py:74
  515.0 372.3 %while.25 = (s32[]{:T(128)}, f32[32,3,128]{2,0,1:T(8,128)S(1)}, f32[32,48,8,128]{3,1,2,0:T(8,128)}, f32[32,128]{1,0:T(8,128)S(1)}, f32[32,8,128]{2,1,0:T(8,128)}, /*index=5*/f32[32,48,128]{2,1,0:T(8,128)S(1)}) while((s32[]{:T(128)}, f32[32,3,128]{2,0,1:T(8,128)S(1)}, f32[32,48,8,128]{3,1,2,0:T(8,128)}, f32[32,128]{1,0:T(8,128)S(1)}, ...), condition=%wide.region_9.10_spmd.clone, body=%wide.region_6.9_spmd.sunk.clone | while | flops 27543936 | bytes 13742689 | solution.py:93
  519.9 3.7 fusion.56
  531.6 3.7 fusion.56
  543.2 3.7 fusion.56
  554.8 3.7 fusion.56
  566.5 3.7 fusion.56
  578.1 3.7 fusion.56
  589.8 3.7 fusion.56
  601.4 3.7 fusion.56
  613.0 3.7 fusion.56
  624.7 3.7 fusion.56
  636.3 3.7 fusion.56
  647.9 3.7 fusion.56
  659.6 3.7 fusion.56
  671.2 3.7 fusion.56
  682.8 3.7 fusion.56
  694.5 3.7 fusion.56
  706.1 3.7 fusion.56
  717.8 3.7 fusion.56
  729.4 3.7 fusion.56
  741.0 3.7 fusion.56
  764.3 3.7 fusion.56
  787.6 3.7 fusion.56
  810.8 3.7 fusion.56
  822.5 3.7 fusion.56
  834.1 3.7 fusion.56
  845.7 3.7 fusion.56
  (903 shorter events, 473.2 us)
Async XLA Ops:
  7.2 69.3 %all-gather.2.cloned.1.call-start = ((), (), s32[]{:S(2)}) async-start(), calls=%async_computation | async-start | bytes 4325376 | tf_op jit(solution)/shard_map/all_gather | solution.py:52
  57.7 4.0 copy-start.2
  83.8 389.5 %copy-start = (f32[32,128]{1,0:T(8,128)S(1)}, f32[32,128]{1,0:T(8,128)}, u32[]{:S(2)}) copy-start(f32[32,128]{1,0:T(8,128)} %param.16) | copy-start | bytes 49156
  473.3 41.7 %copy-start.1 = (f32[32,128]{1,0:T(8,128)}, f32[32,128]{1,0:T(8,128)S(1)}, u32[]{:S(2)}) copy-start(f32[32,128]{1,0:T(8,128)S(1)} %get-tuple-element.60) | copy-start | bytes 49156
Sparse Core Ops, SparseCore 0:
  10.9 65.5 all-gather.1
where the time goes:
time: 900 us; the launch traced here: 895 us
  other arithmetic  608 us (68%)
  local copies, waits for them, and re-layouts  166 us (18%)
  blocking collectives  86 us (10%)
  waiting for transfers between devices  14.7 us (2%)
  between operations  14.2 us (2%)
    reduce_sum x32, other arithmetic, density_block(): approach = jnp.sum(moving * offset, axis=1)  202 us
    mul x32, other arithmetic, force_block(): near_mass[:, :, None]  118 us
    reduce_sum x32, other arithmetic, separation(): radius = jnp.sqrt(jnp.sum(offset * offset, axis=1))  99.9 us
    reduce_sum x32, other arithmetic, force_block(): return -jnp.sum(factor[:, None] * offset, axis=(0, 2))  93.8 us
    reduce_sum x32, other arithmetic, density_block(): divergence = -jnp.sum(weight * slope * approach, axis=(0, 1)) / density  87.8 us
    squeeze x64, local copies, waits for them, and re-layouts, per_device(): density, divergence = lax.map(first_pass, (fields, near))  60.5 us
    all_gather x1, blocking collectives, per_device(): tables = lax.all_gather(export_blocks, 'dom', axis=0, tiled=True)  45.5 us
    dynamic_slice x64, local copies, waits for them, and re-layouts, per_device(): density, divergence = lax.map(first_pass, (fields, near))  43.6 us
  transfers between devices with their start and end apart: 1, of which 1 were waited for; matrix products, arithmetic and copies ran while one was open for 1% of the time, Pallas kernels for 0%

commit v1 on v0

v1 whole, which is shorter than its diff:
```python
import functools

import jax
import jax.numpy as jnp
import numpy as np
from jax import lax
from jax.experimental import pallas as pl
from jax.experimental.pallas import tpu as pltpu
from jax.sharding import PartitionSpec as P

kernel_norm = 3.3422538049298023
LANES = 128
FEATS = 96
ROWS = 512
CHUNK = 1024
bf16 = jnp.bfloat16
f32 = jnp.float32
NT = (((1,), (1,)), ((), ()))


def split3(value):
    high = value.astype(bf16).astype(f32)
    rest = value - high
    middle = rest.astype(bf16).astype(f32)
    return high, middle, rest - middle


def near_rows(value, extra):
    high, middle, low = split3(value)
    first = [high, middle]
    last = [low, extra]
    return jnp.concatenate(first * 3 + last * 3, axis=0).astype(bf16)


def own_rows(value, extra):
    parts = split3(value)
    rows = []
    for part in parts:
        rows += [part, part]
    for part, more in zip(parts, extra):
        rows += [part, more]
    rows.append(jnp.zeros((LANES - FEATS, LANES), f32))
    return jnp.concatenate(rows, axis=0).T[:, :FEATS].astype(bf16)


def particle_rows(fields, centre):
    shifted = fields - centre
    pos = shifted[0:3]
    vel = shifted[3:6]
    square = jnp.sum(pos * pos, axis=0, keepdims=True)
    cross = jnp.sum(pos * vel, axis=0, keepdims=True)
    return pos, vel, square, cross


def moment_rows(pos, vel, square, cross):
    one = jnp.ones_like(square)
    value = jnp.concatenate([pos, vel, one, cross], axis=0)
    parts = split3(square)
    extra = jnp.concatenate(list(parts) + [jnp.zeros((5, LANES), f32)], axis=0)
    return value, extra


def slope_rows(pos, square, scale, smooth):
    sigma = scale / smooth
    sigma = sigma * sigma
    return jnp.concatenate([pos * sigma, sigma, square * sigma, jnp.zeros((3, LANES), f32)], axis=0)


def prepare_kernel(fields_ref, near_ref, own_ref, own2_ref, mass_ref, centre_ref):
    blocks = fields_ref.shape[0]
    total = jnp.sum(fields_ref[...], axis=0)
    mean = jnp.sum(total, axis=1, keepdims=True) / (blocks * LANES)
    rows = lax.broadcasted_iota(jnp.int32, (8, LANES), 0)
    centre = jnp.where(rows < 6, jnp.broadcast_to(mean, (8, LANES)), 0.0)
    centre_ref[...] = centre
    zero = jnp.zeros((8, LANES), f32)

    @pl.loop(0, blocks)
    def _(index):
        fields = fields_ref[index]
        at = pl.ds(pl.multiple_of(index * LANES, LANES), LANES)
        pos, vel, square, cross = particle_rows(fields, centre)
        value, extra = moment_rows(pos, vel, square, cross)
        near_ref[:, at] = near_rows(value, extra)
        mass_ref[:, at] = fields[6:7]
        smooth = fields[7:8]
        sigma = 16.0 / (smooth * smooth)
        blank = jnp.zeros((3, LANES), f32)
        coefficient = jnp.concatenate(
            [pos * (-2.0 * sigma), blank, square * sigma, blank[0:1]], axis=0
        )
        more = [
            jnp.concatenate([part] * 3 + [jnp.zeros((5, LANES), f32)], axis=0)
            for part in split3(sigma)
        ]
        own_ref[at, :] = own_rows(coefficient, more)
        coefficient = jnp.concatenate(
            [pos * -2.0, square, jnp.ones_like(square), blank], axis=0
        )
        own2_ref[at, :] = own_rows(coefficient, [zero] * 3)


def first_chunk(own, near, mass, moments):
    square = jnp.maximum(jnp.dot(own, near, preferred_element_type=f32), 1e-12)
    tail = jnp.maximum(4.0 - square * lax.rsqrt(square), 0.0)
    fourth = tail * tail
    slope = fourth * tail * mass
    value = slope * (tail * (5.0 - tail))
    width = value.shape[1]
    lanes = value[:, 0:LANES]
    for part in range(LANES, width, LANES):
        lanes = lanes + value[:, part : part + LANES]
    return lanes, reduce_slope(slope, moments)


def second_chunk(own, near, scale, moments):
    square = jnp.maximum(jnp.dot(own, near, preferred_element_type=f32), 1e-12)
    tail = jnp.maximum(scale - square * lax.rsqrt(square), 0.0)
    return reduce_slope(tail * tail * tail, moments)


def reduce_slope(slope, moments):
    high = slope.astype(bf16)
    low = (slope - high.astype(f32)).astype(bf16)
    return lax.dot_general(moments, high, NT, preferred_element_type=f32) + lax.dot_general(
        moments, low, NT, preferred_element_type=f32
    )


def fold_parts(moments):
    return moments[0:8] + (moments[8:16] + moments[16:24])


def lane_sums(lanes):
    return jnp.concatenate(
        [
            jnp.sum(lanes[part : part + LANES].T, axis=0, keepdims=True)
            for part in range(0, lanes.shape[0], LANES)
        ],
        axis=1,
    )


def local_first_kernel(own_ref, near_ref, mass_ref, out_ref, density_ref):
    rows = own_ref.shape[0]
    own = own_ref[...]

    def step(index, carry):
        lanes, moments = carry
        at = pl.ds(pl.multiple_of(index * CHUNK, CHUNK), CHUNK)
        more_lanes, more = first_chunk(
            own, near_ref[:, at], mass_ref[:, at], near_ref[32:64, at]
        )
        return lanes + more_lanes, moments + more

    start = (jnp.zeros((rows, LANES), f32), jnp.zeros((32, rows), f32))
    lanes, moments = lax.fori_loop(0, near_ref.shape[1] // CHUNK, step, start)
    out_ref[...] = fold_parts(moments)
    density_ref[...] = lane_sums(lanes)


def local_second_kernel(own_ref, near_ref, scale_ref, moment_ref, out_ref):
    rows = own_ref.shape[0]
    own = own_ref[...]

    def step(index, moments):
        at = pl.ds(pl.multiple_of(index * CHUNK, CHUNK), CHUNK)
        return moments + second_chunk(
            own, near_ref[:, at], scale_ref[:, at], moment_ref[32:64, at]
        )

    moments = lax.fori_loop(
        0, near_ref.shape[1] // CHUNK, step, jnp.zeros((32, rows), f32)
    )
    out_ref[...] = fold_parts(moments)


def slot_place(slot, column_ref, place_ref, me, capacity, blocks, extra):
    sender = slot // capacity
    block = column_ref[sender * capacity + slot % capacity]
    apart = sender ^ me
    half = blocks // 2
    first = place_ref[0, apart]
    second = place_ref[1, apart]
    devices = place_ref.shape[1]
    row = jnp.where(
        block < half,
        first * (half + extra) + block,
        devices * (half + extra) + second * half + block - half,
    )
    return row, first * blocks + block


def fetch(pieces, gathered, semaphore):
    start = 0
    copies = []
    for number, piece in enumerate(pieces):
        count = piece.shape[0]
        copy = pltpu.make_async_copy(
            piece, gathered.at[pl.ds(start, count)], semaphore.at[number]
        )
        copy.start()
        copies.append(copy)
        start += count
    for copy in copies:
        copy.wait()


def remote_first_kernel(
    capacity,
    extra,
    slots_ref,
    column_ref,
    place_ref,
    me_ref,
    piece0,
    piece1,
    piece2,
    piece3,
    own_ref,
    fields_ref,
    centre_ref,
    entropy_ref,
    moments_ref,
    lanes_ref,
    density_ref,
    divergence_ref,
    scale_ref,
    gradient_ref,
    near2_ref,
    scale_row_ref,
    gathered,
    near,
    mass,
    semaphore,
):
    blocks = fields_ref.shape[0]
    partners = slots_ref.shape[1]
    fetch((piece0, piece1, piece2, piece3), gathered, semaphore)
    centre = centre_ref[...]
    me = me_ref[0]

    @pl.loop(0, blocks)
    def _(index):
        at = pl.ds(pl.multiple_of(index * LANES, LANES), LANES)
        for k in range(partners):
            row, _ = slot_place(
                slots_ref[index, k], column_ref, place_ref, me, capacity, blocks, extra
            )
            fields = gathered[row]
            value, more = moment_rows(*particle_rows(fields, centre))
            near[:, k * LANES : (k + 1) * LANES] = near_rows(value, more)
            mass[:, k * LANES : (k + 1) * LANES] = fields[6:7]
        lanes, moments = first_chunk(own_ref[at, :], near[...], mass[...], near[32:64, :])
        moments = fold_parts(moments) + moments_ref[:, at]
        total = lane_sums(lanes) + lanes_ref[:, at]
        fields = fields_ref[index]
        pos, vel, square, cross = particle_rows(fields, centre)
        smooth = fields[7:8]
        inverse = 1.0 / smooth
        cube = inverse * inverse * inverse
        density = total * cube * (kernel_norm / 256.0)
        factor = cube * inverse * inverse * (20.0 * kernel_norm / 64.0)
        approach = (
            cross * moments[6:7]
            + moments[7:8]
            - jnp.sum(vel * moments[0:3], axis=0, keepdims=True)
            - jnp.sum(pos * moments[3:6], axis=0, keepdims=True)
        )
        press = entropy_ref[pl.ds(index, 1), :] * inverse_cube_root(density)
        weight = (20.0 * kernel_norm) * fields[6:7] * press * cube * inverse * inverse
        root = inverse_cube_root(weight)
        scale = weight * root * root
        density_ref[pl.ds(index, 1), :] = density
        divergence_ref[pl.ds(index, 1), :] = factor * approach / density
        scale_ref[pl.ds(index, 1), :] = scale
        gradient = (pos * moments[6:7] - moments[0:3]) * (factor * press)
        gradient_ref[:, at] = jnp.concatenate(
            [gradient, jnp.zeros((5, LANES), f32)], axis=0
        )
        near2_ref[:, at] = near_rows(
            slope_rows(pos, square, scale, smooth), jnp.zeros((8, LANES), f32)
        )
        scale_row_ref[:, at] = scale


def inverse_cube_root(value):
    guess = jnp.exp(jnp.log(value) * (-1.0 / 3.0))
    guess = guess * (4.0 - value * guess * guess * guess) * (1.0 / 3.0)
    return guess * (4.0 - value * guess * guess * guess) * (1.0 / 3.0)


def remote_second_kernel(
    capacity,
    extra,
    slots_ref,
    column_ref,
    place_ref,
    me_ref,
    active_ref,
    piece0,
    piece1,
    piece2,
    piece3,
    scale0,
    scale1,
    own_ref,
    fields_ref,
    centre_ref,
    moments_ref,
    gradient_ref,
    out_ref,
    gathered,
    scales,
    near,
    moment,
    scale_row,
    semaphore,
    scale_semaphore,
):
    blocks = fields_ref.shape[0]
    partners = slots_ref.shape[1]
    fetch((piece0, piece1, piece2, piece3), gathered, semaphore)
    fetch((scale0, scale1), scales, scale_semaphore)
    centre = centre_ref[...]
    me = me_ref[0]

    @pl.loop(0, blocks)
    def _(index):
        at = pl.ds(pl.multiple_of(index * LANES, LANES), LANES)

        @pl.when(active_ref[index] > 0)
        def _():
            for k in range(partners):
                row, scale_at = slot_place(
                    slots_ref[index, k], column_ref, place_ref, me, capacity, blocks, extra
                )
                fields = gathered[row]
                scale = scales[pl.ds(scale_at, 1), :]
                pos, vel, square, cross = particle_rows(fields, centre)
                value = jnp.concatenate([pos, vel, jnp.ones_like(square), cross], axis=0)
                high, middle, low = split3(value)
                here = slice(k * LANES, (k + 1) * LANES)
                moment[:, here] = jnp.concatenate(
                    [high, middle, low, jnp.zeros_like(low)], axis=0
                ).astype(bf16)
                near[:, here] = near_rows(
                    slope_rows(pos, square, scale, fields[7:8]), jnp.zeros((8, LANES), f32)
                )
                scale_row[:, here] = scale
            moments = second_chunk(own_ref[at, :], near[...], scale_row[...], moment[...])
            moments = fold_parts(moments) + moments_ref[:, at]
            pos, _, _, _ = particle_rows(fields_ref[index], centre)
            out_ref[index] = gradient_ref[0:3, at] + (pos * moments[6:7] - moments[0:3])

        @pl.when(active_ref[index] <= 0)
        def _():
            out_ref[index] = jnp.zeros((3, LANES), f32)


def in_vmem(count):
    return [pl.BlockSpec(memory_space=pltpu.VMEM)] * count


def in_smem(count):
    return [pl.BlockSpec(memory_space=pltpu.SMEM)] * count


def in_any(count):
    return [pl.BlockSpec(memory_space=pl.ANY)] * count


def shape(*dims, dtype=f32):
    return jax.ShapeDtypeStruct(dims, dtype)


params = pltpu.CompilerParams(vmem_limit_bytes=48 * 2**20)


def prepare(fields):
    particles = fields.shape[0] * LANES
    return pl.pallas_call(
        prepare_kernel,
        out_shape=[
            shape(FEATS, particles, dtype=bf16),
            shape(particles, FEATS, dtype=bf16),
            shape(particles, FEATS, dtype=bf16),
            shape(1, particles),
            shape(8, LANES),
        ],
        in_specs=in_vmem(1),
        out_specs=in_vmem(5),
        compiler_params=params,
    )(fields)


def local_first(part, parts, own, near, mass):
    particles = near.shape[1]
    share = particles // parts
    steps = share // ROWS
    whole = lambda index: (0, 0)
    return pl.pallas_call(
        local_first_kernel,
        grid=(steps,),
        in_specs=[
            pl.BlockSpec((ROWS, FEATS), lambda index: (part * steps + index, 0)),
            pl.BlockSpec(near.shape, whole),
            pl.BlockSpec(mass.shape, whole),
        ],
        out_specs=[
            pl.BlockSpec((8, ROWS), lambda index: (0, index)),
            pl.BlockSpec((1, ROWS), lambda index: (0, index)),
        ],
        out_shape=[shape(8, share), shape(1, share)],
        cost_estimate=pl.CostEstimate(
            flops=share * particles * 400, bytes_accessed=2**20, transcendentals=0
        ),
        compiler_params=params,
    )(own, near, mass)


def local_second(part, parts, own, near, scale, moments):
    particles = near.shape[1]
    share = particles // parts
    steps = share // ROWS
    whole = lambda index: (0, 0)
    return pl.pallas_call(
        local_second_kernel,
        grid=(steps,),
        in_specs=[
            pl.BlockSpec((ROWS, FEATS), lambda index: (part * steps + index, 0)),
            pl.BlockSpec(near.shape, whole),
            pl.BlockSpec(scale.shape, whole),
            pl.BlockSpec(moments.shape, whole),
        ],
        out_specs=pl.BlockSpec((8, ROWS), lambda index: (0, index)),
        out_shape=shape(8, share),
        cost_estimate=pl.CostEstimate(
            flops=share * particles * 400, bytes_accessed=2**20, transcendentals=0
        ),
        compiler_params=params,
    )(own, near, scale, moments)


def doubling(value, order, devices):
    for number, bit in enumerate(order):
        other = lax.ppermute(value, "dom", [(i, i ^ bit) for i in range(devices)])
        if number == len(order) - 1:
            return value, other
        value = jnp.concatenate([value, other], axis=0)


def places(order, devices):
    table = np.zeros((devices,), np.int32)
    for apart in range(devices):
        table[apart] = sum(1 << k for k, bit in enumerate(order) if apart & bit)
    return table


def per_device(
    devices,
    positions,
    velocities,
    masses,
    smoothing,
    entropy,
    export_blocks,
    partner_slots,
    active,
):
    blocks = positions.shape[0]
    particles = blocks * LANES
    capacity = export_blocks.shape[2]
    half = blocks // 2
    me = lax.axis_index("dom")
    fields = jnp.concatenate(
        [positions, velocities, masses[:, None, :], smoothing[:, None, :]], axis=1
    )
    words = devices * capacity
    extra = -(-words // (8 * LANES))
    table = export_blocks.astype(f32).reshape(words)
    table = jnp.pad(table, (0, extra * 8 * LANES - words)).reshape(extra, 8, LANES)
    bits = [1 << k for k in reversed(range(devices.bit_length() - 1))]
    order0 = list(bits)
    order1 = list(bits)
    order1[-3:-1] = reversed(order1[-3:-1])
    first = doubling(jnp.concatenate([fields[:half], table], axis=0), order0, devices)
    second = doubling(fields[half:], order1, devices)
    pieces = (*first, *second)
    place0 = places(order0, devices)
    place = jnp.asarray(np.stack([place0, places(order1, devices)]))

    near, own, own2, mass, centre = prepare(fields)
    parts = 4
    sums = [local_first(part, parts, own, near, mass) for part in range(parts)]
    moments = jnp.concatenate([item[0] for item in sums], axis=1)
    lanes = jnp.concatenate([item[1] for item in sums], axis=1)

    step = half + extra
    tables = jnp.concatenate(
        [item.reshape(devices // 2, step, 8, LANES)[:, half:] for item in first], axis=0
    )
    tables = tables.reshape(devices, extra * 8 * LANES)[:, :words]
    tables = tables.reshape(devices, devices, capacity)
    column = lax.dynamic_index_in_dim(tables, me, axis=1, keepdims=False)
    senders = jnp.arange(devices, dtype=jnp.int32) ^ me
    column = column[jnp.asarray(place0)[senders]].astype(jnp.int32).reshape(words)
    me_array = me.astype(jnp.int32).reshape(1)

    rows = sum(piece.shape[0] for piece in pieces)
    partners = partner_slots.shape[1] * LANES
    density, divergence, scale, gradient, near2, scale_row = pl.pallas_call(
        functools.partial(remote_first_kernel, capacity, extra),
        out_shape=[
            shape(blocks, LANES),
            shape(blocks, LANES),
            shape(blocks, LANES),
            shape(8, particles),
            shape(FEATS, particles, dtype=bf16),
            shape(1, particles),
        ],
        in_specs=in_smem(4) + in_any(4) + in_vmem(6),
        out_specs=in_vmem(6),
        scratch_shapes=[
            pltpu.VMEM((rows, 8, LANES), f32),
            pltpu.VMEM((FEATS, partners), bf16),
            pltpu.VMEM((1, partners), f32),
            pltpu.SemaphoreType.DMA((4,)),
        ],
        compiler_params=params,
    )(
        partner_slots, column, place, me_array, *pieces, own, fields, centre, entropy,
        moments, lanes,
    )

    scales = doubling(scale, order0, devices)
    sums = [
        local_second(part, parts, own2, near2, scale_row, near) for part in range(parts)
    ]
    moments = jnp.concatenate(sums, axis=1)
    acceleration = pl.pallas_call(
        functools.partial(remote_second_kernel, capacity, extra),
        out_shape=shape(blocks, 3, LANES),
        in_specs=in_smem(5) + in_any(6) + in_vmem(5),
        out_specs=pl.BlockSpec(memory_space=pltpu.VMEM),
        scratch_shapes=[
            pltpu.VMEM((rows, 8, LANES), f32),
            pltpu.VMEM((devices * blocks, LANES), f32),
            pltpu.VMEM((FEATS, partners), bf16),
            pltpu.VMEM((32, partners), bf16),
            pltpu.VMEM((1, partners), f32),
            pltpu.SemaphoreType.DMA((4,)),
            pltpu.SemaphoreType.DMA((2,)),
        ],
        compiler_params=params,
    )(
        partner_slots, column, place, me_array, active, *pieces, *scales, own2, fields,
        centre, moments, gradient,
    )
    return (density, divergence, acceleration)


def solution(mesh):
    in_specs = (
        P("dom", None, None),
        P("dom", None, None),
        P("dom", None),
        P("dom", None),
        P("dom", None),
        P("dom", None, None),
        P("dom", None),
        P("dom"),
    )
    out_specs = (P("dom", None), P("dom", None), P("dom", None, None))
    return jax.shard_map(
        functools.partial(per_device, mesh.shape["dom"]),
        mesh=mesh,
        in_specs=in_specs,
        out_specs=out_specs,
        check_vma=False,
    )
```

time: 900 us -> 253 us (0.28)
  the two profiles are of different devices: /device:TPU:0 before, /device:TPU:11 now
where the time goes in v1:
time: 253 us
  Pallas kernels  184 us (73%)
  starting transfers between devices  25.6 us (10%)
  local copies, waits for them, and re-layouts  23.2 us (9%)
  waiting for transfers between devices  10.2 us (4%)
  other arithmetic  8.64 us (3%)
    pallas_call x4, Pallas kernels, local_first(): pl.pallas_call(local_first_kernel, grid=(steps,), in_specs=[pl.BlockSpec(...  56.6 us
    pallas_call x4, Pallas kernels, local_second(): pl.pallas_call(local_second_kernel, grid=(steps,), in_specs=[pl.BlockSpec...  44.3 us
    pallas_call x1, Pallas kernels, per_device(): pl.pallas_call(functools.partial(remote_first_kernel, capacity, extra), o...  41.9 us
    pallas_call x1, Pallas kernels, per_device(): pl.pallas_call(functools.partial(remote_second_kernel, capacity, extra),...  37.6 us
    ppermute x15, starting transfers between devices, doubling(): other = lax.ppermute(value, 'dom', [(i, i ^ bit) for i in range(devices)])  25.6 us
    unnamed x68, local copies, waits for them, and re-layouts  14.5 us
    ppermute x15, waiting for transfers between devices, doubling(): other = lax.ppermute(value, 'dom', [(i, i ^ bit) for i in range(devices)])  10.2 us
  transfers between devices with their start and end apart: 15, of which 6 were waited for; matrix products, arithmetic and copies ran while one was open for 8% of the time, Pallas kernels for 28%

profile of v1, /device:TPU:11, one launch (start us, length us, event | category | flops | bytes accessed | tf_op | source)
XLA Modules:
  0.0 253.0 jit_solution(7908640776438438759)
XLA Ops:
  0.6 0.8 copy.19
  1.5 0.8 copy.20
  2.3 0.8 pad_maximum_fusion.4.fields_ref
  3.1 0.7 fusion.2
  3.8 2.3 collective-permute-start.5
  6.1 0.7 convert_element_type.10
  6.9 0.6 pad_maximum_fusion.10
  7.6 3.9 %shard_map.121 = (bf16[96,4096]{1,0:T(8,128)(2,1)S(1)}, bf16[4096,96]{1,0:T(8,128)(2,1)S(1)}, bf16[4096,96]{1,0:T(8,128)(2,1)S(1)}, f32[1,4096]{1,0:T(1,128)S(1)}, f32[8,128]{1,0:T(8,128)S(1)}) custom-call(f32[32,8,128]{2,1,0:T(8,128)S(1)} %pad_maximum_fusion.4.fields_ref), custom_call_target="tpu_custom_call" | custom-call | tf_op jit(solution)/shard_map/pallas_call | solution.py:382
  11.5 1.0 copy-done.2
  12.4 0.6 copy-done.11
  13.0 14.1 %shard_map.125 = (f32[8,1024]{1,0:T(8,128)S(1)}, f32[1,1024]{1,0:T(1,128)S(1)}) custom-call(bf16[4096,96]{1,0:T(8,128)(2,1)S(1)} %get-tuple-element.22.own_ref, bf16[96,4096]{1,0:T(8,128)(2,1)S(1)} %get-tuple-element.24.near_ref.moment_ref, f32[1,4096]{1,0:T(1,128)S(1)} %get-tuple-element.25.mass_ref), custom_call_target="tpu_custom_call" | custom-call | flops 1677721600 | bytes 1048576 | tf_op jit(solution)/shard_map/pallas_call | solution.py:402
  27.2 14.2 %shard_map.124 = (f32[8,1024]{1,0:T(8,128)S(1)}, f32[1,1024]{1,0:T(1,128)S(1)}) custom-call(bf16[4096,96]{1,0:T(8,128)(2,1)S(1)} %get-tuple-element.22.own_ref, bf16[96,4096]{1,0:T(8,128)(2,1)S(1)} %get-tuple-element.24.near_ref.moment_ref, f32[1,4096]{1,0:T(1,128)S(1)} %get-tuple-element.25.mass_ref), custom_call_target="tpu_custom_call" | custom-call | flops 1677721600 | bytes 1048576 | tf_op jit(solution)/shard_map/pallas_call | solution.py:402
  41.4 0.6 copy-done.4
  42.0 0.7 gather_fusion
  42.7 1.1 copy-done.16
  43.9 14.2 %shard_map.123 = (f32[8,1024]{1,0:T(8,128)S(1)}, f32[1,1024]{1,0:T(1,128)S(1)}) custom-call(bf16[4096,96]{1,0:T(8,128)(2,1)S(1)} %get-tuple-element.22.own_ref, bf16[96,4096]{1,0:T(8,128)(2,1)S(1)} %copy-done.16, f32[1,4096]{1,0:T(1,128)S(1)} %get-tuple-element.25.mass_ref), custom_call_target="tpu_custom_call" | custom-call | flops 1677721600 | bytes 1048576 | tf_op jit(solution)/shard_map/pallas_call | solution.py:402
  58.1 0.9 pad_maximum_fusion.3
  59.2 0.6 constant_dynamic-update-slice_fusion.3
  59.8 0.8 pad_maximum_fusion.6
  60.6 1.4 collective-permute-start.6
  62.0 0.9 collective-permute-done.1
  62.9 0.9 pad_maximum_fusion.1
  63.8 1.3 collective-permute-start.2
  65.1 1.5 constant_dynamic-update-slice_fusion.2
  66.7 0.9 pad_maximum_fusion.2
  67.9 0.7 constant_dynamic-update-slice_fusion.1
  68.6 0.7 collective-permute-done.2
  69.3 0.7 constant_dynamic-update-slice_fusion
  70.6 14.1 %shard_map.122 = (f32[8,1024]{1,0:T(8,128)S(1)}, f32[1,1024]{1,0:T(1,128)S(1)}) custom-call(bf16[4096,96]{1,0:T(8,128)(2,1)S(1)} %get-tuple-element.22.own_ref, bf16[96,4096]{1,0:T(8,128)(2,1)S(1)} %copy-done.16, f32[1,4096]{1,0:T(1,128)S(1)} %get-tuple-element.25.mass_ref), custom_call_target="tpu_custom_call" | custom-call | flops 1677721600 | bytes 1048576 | tf_op jit(solution)/shard_map/pallas_call | solution.py:402
  84.7 0.6 copy-done.8
  85.4 0.9 pad_maximum_fusion
  86.3 1.0 collective-permute-start.8
  87.4 0.6 pad_clamp_fusion
  88.0 0.8 constant_dynamic-update-slice_fusion.14
  88.9 0.9 constant_dynamic-update-slice_fusion.13
  89.9 1.1 constant_dynamic-update-slice_fusion.5.piece0
  91.0 5.5 %collective-permute-start.4 = (f32[272,8,128]{2,1,0:T(8,128)S(1)}, f32[272,8,128]{2,1,0:T(8,128)S(1)}, u32[]{:S(2)}, u32[]{:S(2)}) collective-permute-start(f32[272,8,128]{2,1,0:T(8,128)S(1)} %constant_dynamic-update-slice_fusion.5.piece0), channel_id=1, source_target_pairs={{0,1},{1,0},{2,3},{3,2},{4,5},{5,4},{6,7},{7,6},{8,9},{9,8},{10,11... | collective-permute-start | bytes 3342344 | tf_op jit(solution)/shard_map/ppermute | solution.py:447
  96.6 1.1 constant_dynamic-update-slice_fusion.11.piece2
  97.6 4.4 %collective-permute-start.9 = (f32[256,8,128]{2,1,0:T(8,128)S(1)}, f32[256,8,128]{2,1,0:T(8,128)S(1)}, u32[]{:S(2)}, u32[]{:S(2)}) collective-permute-start(f32[256,8,128]{2,1,0:T(8,128)S(1)} %constant_dynamic-update-slice_fusion.11.piece2), channel_id=1, source_target_pairs={{0,1},{1,0},{2,3},{3,2},{4,5},{5,4},{6,7},{7,6},{8,9},{9,8},{10,11... | collective-permute-start | bytes 3145736 | tf_op jit(solution)/shard_map/ppermute | solution.py:447
  102.1 1.0 copy-done.19
  103.1 0.7 pad_maximum_fusion.5
  103.8 1.9 reshape_reshape.3
  105.7 0.9 constant_dynamic-slice_fusion
  106.6 0.7 gather_fusion.1
  107.3 0.6 convert_element_type.11
  107.9 0.8 convert_element_type.12.column_ref
  108.7 1.2 copy-done.1
  109.9 0.7 copy-done.12
  110.6 0.7 copy-done.13
  111.3 41.9 %shard_map.126 = (f32[32,128]{1,0:T(8,128)}, f32[32,128]{1,0:T(8,128)}, f32[32,128]{1,0:T(8,128)S(1)}, f32[8,4096]{1,0:T(8,128)S(1)}, bf16[96,4096]{1,0:T(8,128)(2,1)S(1)}, /*index=5*/f32[1,4096]{1,0:T(1,128)S(1)}) custom-call(s32[32,16]{1,0:T(8,128)S(1)} %copy.22.slots_ref, s32[1024]{0:T(1024)S(1)} %convert_element_type.12.column_ref, ...), custom_call_target="tpu_custom_call" | custom-call | tf_op jit(solution)/shard_map/pallas_call | solution.py:512
  153.2 11.0 %shard_map.130 = f32[8,1024]{1,0:T(8,128)S(1)} custom-call(bf16[4096,96]{1,0:T(8,128)(2,1)S(1)} %copy-done.3, bf16[96,4096]{1,0:T(8,128)(2,1)S(1)} %get-tuple-element.38.near_ref, f32[1,4096]{1,0:T(1,128)S(1)} %get-tuple-element.39.scale_ref, bf16[96,4096]{1,0:T(8,128)(2,1)S(1)} %copy-done.17), custom_call_target="tpu_custom_call" | custom-call | flops 1677721600 | bytes 1048576 | tf_op jit(solution)/shard_map/pallas_call | solution.py:427
  164.3 11.0 %shard_map.129 = f32[8,1024]{1,0:T(8,128)S(1)} custom-call(bf16[4096,96]{1,0:T(8,128)(2,1)S(1)} %copy-done.3, bf16[96,4096]{1,0:T(8,128)(2,1)S(1)} %get-tuple-element.38.near_ref, f32[1,4096]{1,0:T(1,128)S(1)} %get-tuple-element.39.scale_ref, bf16[96,4096]{1,0:T(8,128)(2,1)S(1)} %copy-done.17), custom_call_target="tpu_custom_call" | custom-call | flops 1677721600 | bytes 1048576 | tf_op jit(solution)/shard_map/pallas_call | solution.py:427
  175.3 11.2 %shard_map.128 = f32[8,1024]{1,0:T(8,128)S(1)} custom-call(bf16[4096,96]{1,0:T(8,128)(2,1)S(1)} %copy-done.3, bf16[96,4096]{1,0:T(8,128)(2,1)S(1)} %get-tuple-element.38.near_ref, f32[1,4096]{1,0:T(1,128)S(1)} %get-tuple-element.39.scale_ref, bf16[96,4096]{1,0:T(8,128)(2,1)S(1)} %copy-done.17), custom_call_target="tpu_custom_call" | custom-call | flops 1677721600 | bytes 1048576 | tf_op jit(solution)/shard_map/pallas_call | solution.py:427
  186.5 2.4 collective-permute-start.10
  188.9 11.0 %shard_map.127 = f32[8,1024]{1,0:T(8,128)S(1)} custom-call(bf16[4096,96]{1,0:T(8,128)(2,1)S(1)} %copy-done.3, bf16[96,4096]{1,0:T(8,128)(2,1)S(1)} %get-tuple-element.38.near_ref, f32[1,4096]{1,0:T(1,128)S(1)} %get-tuple-element.39.scale_ref, bf16[96,4096]{1,0:T(8,128)(2,1)S(1)} %copy-done.17), custom_call_target="tpu_custom_call" | custom-call | flops 1677721600 | bytes 1048576 | tf_op jit(solution)/shard_map/pallas_call | solution.py:427
  200.2 2.6 %collective-permute-done.11 = f32[64,128]{1,0:T(8,128)S(1)} collective-permute-done((f32[64,128]{1,0:T(8,128)S(1)}, f32[64,128]{1,0:T(8,128)S(1)}, u32[]{:S(2)}, u32[]{:S(2)}) %collective-permute-start.11) | collective-permute-done | bytes 32800 | tf_op jit(solution)/shard_map/ppermute | solution.py:447
  202.8 1.0 collective-permute-start.12
  203.8 2.1 collective-permute-done.12
  205.9 1.1 collective-permute-start.13
  207.0 2.8 %collective-permute-done.13 = f32[256,128]{1,0:T(8,128)S(1)} collective-permute-done((f32[256,128]{1,0:T(8,128)S(1)}, f32[256,128]{1,0:T(8,128)S(1)}, u32[]{:S(2)}, u32[]{:S(2)}) %collective-permute-start.13) | collective-permute-done | bytes 131104 | tf_op jit(solution)/shard_map/ppermute | solution.py:447
  209.8 3.8 %collective-permute-start.14 = (f32[512,128]{1,0:T(8,128)S(1)}, f32[512,128]{1,0:T(8,128)S(1)}, u32[]{:S(2)}, u32[]{:S(2)}) collective-permute-start(f32[512,128]{1,0:T(8,128)S(1)} %constant_dynamic-update-slice_fusion.16.scale0), channel_id=1, source_target_pairs={{0,1},{1,0},{2,3},{3,2},{4,5},{5,4},{6,7},{7,6},{8,9},{9,8},{10,11... | collective-permute-start | bytes 786440 | tf_op jit(solution)/shard_map/ppermute | solution.py:447
  213.6 1.1 collective-permute-done.14.scale1
  214.8 37.6 %shard_map.131 = f32[32,3,128]{2,1,0:T(4,128)S(1)} custom-call(s32[32,16]{1,0:T(8,128)S(1)} %copy.22.slots_ref, s32[1024]{0:T(1024)S(1)} %convert_element_type.12.column_ref, s32[2,32]{1,0:T(2,128)S(1)} %copy-done.13, s32[1]{0:T(128)} %bitcast.8.me_ref, s32[32]{0:T(128)S(1)} %copy-done.14, f32[272,8,128]{2,1,0:T(8,128)S(1)} %constant_dynamic-update-slice_fusion.5.piece0, ...), custom_call_target="tpu_custom_call" | custom-call | tf_op jit(solution)/shard_map/pallas_call | solution.py:541
  252.4 0.6 copy.24
  (78 shorter events, 1.8 us)
Async XLA Ops:
  3.8 54.3 %copy-start.21 = (f32[16,8,128]{2,1,0:T(8,128)}, f32[16,8,128]{2,1,0:T(8,128)S(1)}, u32[]{:S(2)}) copy-start(f32[16,8,128]{2,1,0:T(8,128)S(1)} %get-tuple-element.55) | copy-start | bytes 196612
  3.8 56.0 %copy-start.24 = (f32[16,8,128]{2,1,0:T(8,128)}, f32[16,8,128]{2,1,0:T(8,128)S(1)}, u32[]{:S(2)}) copy-start(f32[16,8,128]{2,1,0:T(8,128)S(1)} %get-tuple-element.51) | copy-start | bytes 196612
  3.8 56.0 %collective-permute-start.5 = (f32[16,8,128]{2,1,0:T(8,128)S(1)}, f32[16,8,128]{2,1,0:T(8,128)}, u32[]{:S(2)}, u32[]{:S(2)}) collective-permute-start(f32[16,8,128]{2,1,0:T(8,128)S(1)} %get-tuple-element.51), channel_id=1, source_target_pairs={{0,16},{1,17},{2,18},{3,19},{4,20},{5,21},{6,22},{7,23},{8,24},{9,... | collective-permute-start | bytes 196616 | tf_op jit(solution)/shard_map/ppermute | solution.py:447
  7.5 50.5 %collective-permute-start = (f32[17,8,128]{2,1,0:T(8,128)}, f32[17,8,128]{2,1,0:T(8,128)}, u32[]{:S(2)}, u32[]{:S(2)}) collective-permute-start(f32[17,8,128]{2,1,0:T(8,128)} %pad_maximum_fusion.10), channel_id=1, source_target_pairs={{0,16},{1,17},{2,18},{3,19},{4,20},{5,21},{6,22},{7,23},{8,24},{9,... | collective-permute-start | bytes 208904 | tf_op jit(solution)/shard_map/ppermute | solution.py:447
  11.4 1.0 copy-start.2
  12.4 0.6 copy-start.11
  13.0 14.2 %copy-start.15 = (bf16[96,4096]{1,0:T(8,128)(2,1)}, bf16[96,4096]{1,0:T(8,128)(2,1)S(1)}, u32[]{:S(2)}) copy-start(bf16[96,4096]{1,0:T(8,128)(2,1)S(1)} %get-tuple-element.24.near_ref.moment_ref) | copy-start | bytes 2359300
  13.0 57.5 %copy-start = (bf16[4096,96]{1,0:T(8,128)(2,1)}, bf16[4096,96]{1,0:T(8,128)(2,1)S(1)}, u32[]{:S(2)}) copy-start(bf16[4096,96]{1,0:T(8,128)(2,1)S(1)} %get-tuple-element.22.own_ref) | copy-start | bytes 2359300
  27.2 14.8 %copy-start.18 = (s32[32]{0:T(128)S(1)}, s32[32]{0:T(128)}, u32[]{:S(2)}) copy-start(s32[32]{0:T(128)} %constant.18.clone) | copy-start | bytes 388
  41.4 0.6 copy-start.4
  42.7 1.1 copy-start.16
  58.0 10.6 %copy-start.6 = (f32[8,1024]{1,0:T(8,128)}, f32[8,1024]{1,0:T(8,128)S(1)}, u32[]{:S(2)}) copy-start(f32[8,1024]{1,0:T(8,128)S(1)} %get-tuple-element.27) | copy-start | bytes 98308
  59.0 4.0 %collective-permute-start.1 = (f32[34,8,128]{2,1,0:T(8,128)S(1)}, f32[34,8,128]{2,1,0:T(8,128)S(1)}, u32[]{:S(2)}, u32[]{:S(2)}) collective-permute-start(f32[34,8,128]{2,1,0:T(8,128)S(1)} %pad_maximum_fusion.3), channel_id=1, source_target_pairs={{0,8},{1,9},{2,10},{3,11},{4,12},{5,13},{6,14},{7,15},{8,0},{9,1},... | collective-permute-start | bytes 417800 | tf_op jit(solution)/shard_map/ppermute | solution.py:447
  60.6 6.0 %collective-permute-start.6 = (f32[32,8,128]{2,1,0:T(8,128)S(1)}, f32[32,8,128]{2,1,0:T(8,128)S(1)}, u32[]{:S(2)}, u32[]{:S(2)}) collective-permute-start(f32[32,8,128]{2,1,0:T(8,128)S(1)} %pad_maximum_fusion.6), channel_id=1, source_target_pairs={{0,8},{1,9},{2,10},{3,11},{4,12},{5,13},{6,14},{7,15},{8,0},{9,1},... | collective-permute-start | bytes 393224 | tf_op jit(solution)/shard_map/ppermute | solution.py:447
  63.8 5.5 %collective-permute-start.2 = (f32[68,8,128]{2,1,0:T(8,128)S(1)}, f32[68,8,128]{2,1,0:T(8,128)S(1)}, u32[]{:S(2)}, u32[]{:S(2)}) collective-permute-start(f32[68,8,128]{2,1,0:T(8,128)S(1)} %pad_maximum_fusion.1), channel_id=1, source_target_pairs={{0,4},{1,5},{2,6},{3,7},{4,0},{5,1},{6,2},{7,3},{8,12},{9,13},{10,... | collective-permute-start | bytes 835592 | tf_op jit(solution)/shard_map/ppermute | solution.py:447
  66.7 18.7 %copy-start.20 = (f32[32,8,128]{2,1,0:T(8,128)}, f32[32,8,128]{2,1,0:T(8,128)S(1)}, u32[]{:S(2)}) copy-start(f32[32,8,128]{2,1,0:T(8,128)S(1)} %collective-permute-done.6) | copy-start | bytes 393220
  67.6 17.7 %collective-permute-start.7 = (f32[64,8,128]{2,1,0:T(8,128)S(1)}, f32[64,8,128]{2,1,0:T(8,128)S(1)}, u32[]{:S(2)}, u32[]{:S(2)}) collective-permute-start(f32[64,8,128]{2,1,0:T(8,128)S(1)} %pad_maximum_fusion.2), channel_id=1, source_target_pairs={{0,2},{1,3},{2,0},{3,1},{4,6},{5,7},{6,4},{7,5},{8,10},{9,11},{10,... | collective-permute-start | bytes 786440 | tf_op jit(solution)/shard_map/ppermute | solution.py:447
  70.0 15.3 %copy-start.25 = (f32[16,8,128]{2,1,0:T(8,128)S(1)}, f32[16,8,128]{2,1,0:T(8,128)}, u32[]{:S(2)}) copy-start(f32[16,8,128]{2,1,0:T(8,128)} %copy-done.24) | copy-start | bytes 196612
  70.0 17.9 %copy-start.26 = (s32[32,16]{0,1:T(8,128)S(1)}, s32[32,16]{0,1:T(8,128)}, u32[]{:S(2)}) copy-start(s32[32,16]{0,1:T(8,128)} %param.16) | copy-start | bytes 6148
  70.0 19.8 %collective-permute-start.3 = (f32[136,8,128]{2,1,0:T(8,128)}, f32[136,8,128]{2,1,0:T(8,128)}, u32[]{:S(2)}, u32[]{:S(2)}) collective-permute-start(f32[136,8,128]{2,1,0:T(8,128)} %get-tuple-element.47), channel_id=1, source_target_pairs={{0,2},{1,3},{2,0},{3,1},{4,6},{5,7},{6,4},{7,5},{8,10},{9,11},{10,... | collective-permute-start | bytes 1671176 | tf_op jit(solution)/shard_map/ppermute | solution.py:447
  84.7 0.6 copy-start.8
  85.4 1.0 copy-start.22
  86.3 10.2 %collective-permute-start.8 = (f32[128,8,128]{2,1,0:T(8,128)S(1)}, f32[128,8,128]{2,1,0:T(8,128)}, u32[]{:S(2)}, u32[]{:S(2)}) collective-permute-start(f32[128,8,128]{2,1,0:T(8,128)S(1)} %pad_maximum_fusion), channel_id=1, source_target_pairs={{0,4},{1,5},{2,6},{3,7},{4,0},{5,1},{6,2},{7,3},{8,12},{9,13},{10,... | collective-permute-start | bytes 1572872 | tf_op jit(solution)/shard_map/ppermute | solution.py:447
  87.4 9.1 %copy-start.23 = (f32[64,8,128]{2,1,0:T(8,128)S(1)}, f32[64,8,128]{2,1,0:T(8,128)}, u32[]{:S(2)}) copy-start(f32[64,8,128]{2,1,0:T(8,128)} %copy-done.22) | copy-start | bytes 786436
  89.8 12.2 %copy-start.5 = (f32[8,1024]{1,0:T(8,128)S(1)}, f32[8,1024]{1,0:T(8,128)}, u32[]{:S(2)}) copy-start(f32[8,1024]{1,0:T(8,128)} %copy-done.4) | copy-start | bytes 98308
  89.8 12.2 %copy-start.7 = (f32[8,1024]{1,0:T(8,128)S(1)}, f32[8,1024]{1,0:T(8,128)}, u32[]{:S(2)}) copy-start(f32[8,1024]{1,0:T(8,128)} %copy-done.6) | copy-start | bytes 98308
  89.8 12.2 %copy-start.9 = (f32[8,1024]{1,0:T(8,128)S(1)}, f32[8,1024]{1,0:T(8,128)}, u32[]{:S(2)}) copy-start(f32[8,1024]{1,0:T(8,128)} %copy-done.8) | copy-start | bytes 98308
  91.0 11.1 %collective-permute-start.4 = (f32[272,8,128]{2,1,0:T(8,128)S(1)}, f32[272,8,128]{2,1,0:T(8,128)S(1)}, u32[]{:S(2)}, u32[]{:S(2)}) collective-permute-start(f32[272,8,128]{2,1,0:T(8,128)S(1)} %constant_dynamic-update-slice_fusion.5.piece0), channel_id=1, source_target_pairs={{0,1},{1,0},{2,3},{3,2},{4,5},{5,4},{6,7},{7,6},{8,9},{9,8},{10,11... | collective-permute-start | bytes 3342344 | tf_op jit(solution)/shard_map/ppermute | solution.py:447
  97.6 11.1 %copy-start.10 = (f32[32,128]{1,0:T(8,128)S(1)}, f32[32,128]{1,0:T(8,128)}, u32[]{:S(2)}) copy-start(f32[32,128]{1,0:T(8,128)} %entropy_ref.1) | copy-start | bytes 49156
  97.6 11.0 %collective-permute-start.9 = (f32[256,8,128]{2,1,0:T(8,128)S(1)}, f32[256,8,128]{2,1,0:T(8,128)S(1)}, u32[]{:S(2)}, u32[]{:S(2)}) collective-permute-start(f32[256,8,128]{2,1,0:T(8,128)S(1)} %constant_dynamic-update-slice_fusion.11.piece2), channel_id=1, source_target_pairs={{0,1},{1,0},{2,3},{3,2},{4,5},{5,4},{6,7},{7,6},{8,9},{9,8},{10,11... | collective-permute-start | bytes 3145736 | tf_op jit(solution)/shard_map/ppermute | solution.py:447
  102.1 1.0 copy-start.19
  108.7 1.2 copy-start.1
  109.9 0.7 copy-start.12
  110.6 0.7 copy-start.13
  111.3 41.9 %copy-start.3 = (bf16[4096,96]{1,0:T(8,128)(2,1)S(1)}, bf16[4096,96]{1,0:T(8,128)(2,1)}, u32[]{:S(2)}) copy-start(bf16[4096,96]{1,0:T(8,128)(2,1)} %copy-done.2) | copy-start | bytes 2359300
  111.3 41.9 %copy-start.17 = (bf16[96,4096]{1,0:T(8,128)(2,1)S(1)}, bf16[96,4096]{1,0:T(8,128)(2,1)}, u32[]{:S(2)}) copy-start(bf16[96,4096]{1,0:T(8,128)(2,1)} %copy-done.15) | copy-start | bytes 2359300
  186.5 13.4 %collective-permute-start.10 = (f32[32,128]{1,0:T(8,128)S(1)}, f32[32,128]{1,0:T(8,128)S(1)}, u32[]{:S(2)}, u32[]{:S(2)}) collective-permute-start(f32[32,128]{1,0:T(8,128)S(1)} %get-tuple-element.36), channel_id=1, source_target_pairs={{0,16},{1,17},{2,18},{3,19},{4,20},{5,21},{6,22},{7,23},{8,24},{9,... | collective-permute-start | bytes 49160 | tf_op jit(solution)/shard_map/ppermute | solution.py:447
  199.9 14.9 %copy-start.14 = (s32[32]{0:T(128)S(1)}, s32[32]{0:T(128)}, u32[]{:S(2)}) copy-start(s32[32]{0:T(128)} %active_ref.1) | copy-start | bytes 388
  199.9 2.8 %collective-permute-start.11 = (f32[64,128]{1,0:T(8,128)S(1)}, f32[64,128]{1,0:T(8,128)S(1)}, u32[]{:S(2)}, u32[]{:S(2)}) collective-permute-start(f32[64,128]{1,0:T(8,128)S(1)} %pad_maximum_fusion.12), channel_id=1, source_target_pairs={{0,8},{1,9},{2,10},{3,11},{4,12},{5,13},{6,14},{7,15},{8,0},{9,1},... | collective-permute-start | bytes 98312 | tf_op jit(solution)/shard_map/ppermute | solution.py:447
  202.8 3.1 %collective-permute-start.12 = (f32[128,128]{1,0:T(8,128)S(1)}, f32[128,128]{1,0:T(8,128)S(1)}, u32[]{:S(2)}, u32[]{:S(2)}) collective-permute-start(f32[128,128]{1,0:T(8,128)S(1)} %pad_maximum_fusion.11), channel_id=1, source_target_pairs={{0,4},{1,5},{2,6},{3,7},{4,0},{5,1},{6,2},{7,3},{8,12},{9,13},{10,... | collective-permute-start | bytes 196616 | tf_op jit(solution)/shard_map/ppermute | solution.py:447
  205.9 3.9 %collective-permute-start.13 = (f32[256,128]{1,0:T(8,128)S(1)}, f32[256,128]{1,0:T(8,128)S(1)}, u32[]{:S(2)}, u32[]{:S(2)}) collective-permute-start(f32[256,128]{1,0:T(8,128)S(1)} %pad_maximum_fusion.8), channel_id=1, source_target_pairs={{0,2},{1,3},{2,0},{3,1},{4,6},{5,7},{6,4},{7,5},{8,10},{9,11},{10,... | collective-permute-start | bytes 393224 | tf_op jit(solution)/shard_map/ppermute | solution.py:447
  209.8 5.0 %collective-permute-start.14 = (f32[512,128]{1,0:T(8,128)S(1)}, f32[512,128]{1,0:T(8,128)S(1)}, u32[]{:S(2)}, u32[]{:S(2)}) collective-permute-start(f32[512,128]{1,0:T(8,128)S(1)} %constant_dynamic-update-slice_fusion.16.scale0), channel_id=1, source_target_pairs={{0,1},{1,0},{2,3},{3,2},{4,5},{5,4},{6,7},{7,6},{8,9},{9,8},{10,11... | collective-permute-start | bytes 786440 | tf_op jit(solution)/shard_map/ppermute | solution.py:447

commit v2 on v0

v2 whole, which is shorter than its diff:
```python
import functools

import jax
import jax.numpy as jnp
import numpy as np
from jax import lax
from jax.experimental import pallas as pl
from jax.experimental.pallas import tpu as pltpu
from jax.sharding import PartitionSpec as P

kernel_norm = 3.3422538049298023
LANES = 128
FEATS = 48
TILE = 256
bf16 = jnp.bfloat16
f32 = jnp.float32


def split3(value):
    high = value.astype(bf16).astype(f32)
    rest = value - high
    middle = rest.astype(bf16).astype(f32)
    return high, middle, rest - middle


def near_rows(four, last):
    high, middle, low = split3(jnp.concatenate([four, four], axis=0))
    upper = lax.broadcasted_iota(jnp.int32, high.shape, 0) < 4
    mixed = jnp.where(upper, high, middle)
    blank = jnp.zeros((FEATS - 35, LANES), f32)
    rows = jnp.concatenate([high, middle, low, mixed, *last, blank], axis=0)
    return rows.T.astype(bf16)


def own_rows(four, last):
    high, middle, low = split3(four)
    pair = [high, middle]
    blank = jnp.zeros((FEATS - 35, LANES), f32)
    rows = pair * 3 + [low, low, *last, blank]
    return jnp.concatenate(rows, axis=0).astype(bf16)


def split_rows(value):
    parts = list(split3(value))
    if value.shape[0] % 8 == 0:
        parts.append(jnp.zeros_like(value))
    else:
        parts.append(jnp.zeros((16 - 3 * value.shape[0], LANES), f32))
    return jnp.concatenate(parts, axis=0).astype(bf16)


def fold_rows(moments, count):
    return moments[0:count] + (moments[count : 2 * count] + moments[2 * count : 3 * count])


def particle_rows(fields, centre):
    shifted = fields - centre
    pos = shifted[0:3]
    vel = shifted[3:6]
    square = jnp.sum(pos * pos, axis=0, keepdims=True)
    return pos, vel, square


def first_near(fields, centre):
    pos, vel, square = particle_rows(fields, centre)
    one = jnp.ones_like(square)
    cross = jnp.sum(pos * vel, axis=0, keepdims=True)
    near = near_rows(jnp.concatenate([pos, square], axis=0), [one] * 3)
    moments = split_rows(jnp.concatenate([pos, vel, one, cross], axis=0))
    return near, moments


def second_near(fields, centre, weight):
    pos, _, square = particle_rows(fields, centre)
    inverse = 1.0 / fields[7:8]
    inverse = inverse * inverse
    last = split3(square * inverse)
    near = near_rows(jnp.concatenate([pos * inverse, inverse], axis=0), last)
    moments = split_rows(jnp.concatenate([pos * weight, weight], axis=0))
    return near, moments


def spread(row):
    return jnp.broadcast_to(row, (LANES, LANES)).T


def prepare_kernel(fields_ref, near_ref, moment_ref, mass_ref, own_ref, own2_ref, centre_ref):
    blocks = fields_ref.shape[0]
    total = jnp.sum(fields_ref[...], axis=0)
    mean = jnp.sum(total, axis=1, keepdims=True) / (blocks * LANES)
    rows = lax.broadcasted_iota(jnp.int32, (8, LANES), 0)
    centre = jnp.where(rows < 6, jnp.broadcast_to(mean, (8, LANES)), 0.0)
    centre_ref[...] = centre

    def block(index):
        fields = fields_ref[index]
        at = pl.ds(pl.multiple_of(index * LANES, LANES), LANES)
        near_ref[at, :], moment_ref[:, at] = first_near(fields, centre)
        mass_ref[at, :] = spread(fields[6:7])
        pos, _, square = particle_rows(fields, centre)
        smooth = fields[7:8]
        sigma = 16.0 / (smooth * smooth)
        four = jnp.concatenate([pos * (-2.0 * sigma), sigma], axis=0)
        own_ref[:, at] = own_rows(four, split3(square * sigma))
        one = jnp.ones_like(square)
        four = jnp.concatenate([pos * -2.0, square], axis=0)
        own2_ref[:, at] = own_rows(four, [one] * 3)

    @pl.loop(0, blocks // 4)
    def _(group):
        for part in range(4):
            block(group * 4 + part)


def halves(slope):
    high = slope.astype(bf16)
    low = (slope - high.astype(f32)).astype(bf16)
    return jnp.concatenate([high, low], axis=0)


def pair_sums(own, near_ref, moment_ref, mass_ref, start, chunk, steps):
    width = own.shape[1]
    dense = None
    total = None

    def place(step):
        if isinstance(start, int):
            return pl.ds(start + step * chunk, chunk)
        return pl.ds(pl.multiple_of(start + step * chunk, chunk), chunk)

    def product(step):
        return jnp.dot(near_ref[place(step), :], own, preferred_element_type=f32)

    def moment(step, slope):
        fields = moment_ref[:, place(step)]
        both = jnp.concatenate([fields, fields], axis=1)
        return jnp.dot(both, slope, preferred_element_type=f32)

    square = product(0)
    slope = None
    for step in range(steps):
        following = product(step + 1) if step + 1 < steps else None
        square = jnp.maximum(square, 1e-12)
        radius = square * lax.rsqrt(square)
        if mass_ref is None:
            tail = jnp.maximum(1.0 - radius, 0.0)
            cube = tail * tail * tail
        else:
            mass = mass_ref[place(step), :]
            mass = jnp.concatenate([mass] * (width // LANES), axis=1)
            tail = jnp.maximum(4.0 - radius, 0.0)
            cube = tail * tail * tail * mass
            value = cube * (tail * (5.0 - tail))
            value = jnp.sum(value.reshape(chunk // 8, 8, width), axis=0)
            dense = value if dense is None else dense + value
        if slope is not None:
            more = moment(step - 1, slope)
            total = more if total is None else total + more
        slope = halves(cube)
        square = following
    more = moment(steps - 1, slope)
    total = more if total is None else total + more
    return dense, total


def local_first_kernel(own_ref, near_ref, moment_ref, mass_ref, *refs):
    out_ref, dense_ref = refs[-2:]
    own = own_ref[...]
    width = own.shape[1]
    particles = near_ref.shape[0]
    chunk, steps = 256, 16
    steps = min(steps, particles // chunk)

    def step(index, carry):
        dense, total = pair_sums(
            own, near_ref, moment_ref, mass_ref, index * (chunk * steps), chunk, steps
        )
        return carry[0] + dense, carry[1] + total

    zero = (jnp.zeros((8, width), f32), jnp.zeros((32, width), f32))
    dense, total = lax.fori_loop(0, particles // (chunk * steps), step, zero)
    out_ref[...] = fold_rows(total, 8)
    dense_ref[...] = dense


def local_second_kernel(own_ref, near_ref, moment_ref, *refs):
    out_ref = refs[-1]
    own = own_ref[...]
    width = own.shape[1]
    particles = near_ref.shape[0]
    chunk, steps = 256, 16
    steps = min(steps, particles // chunk)

    def step(index, carry):
        _, total = pair_sums(
            own, near_ref, moment_ref, None, index * (chunk * steps), chunk, steps
        )
        return carry + total

    zero = jnp.zeros((16, width), f32)
    total = lax.fori_loop(0, particles // (chunk * steps), step, zero)
    out_ref[...] = jnp.concatenate([fold_rows(total, 4), jnp.zeros((4, width), f32)], axis=0)


def slot_place(slot, tables_ref, place_ref, me, capacity, blocks, extra):
    sender = slot // capacity
    apart = sender ^ me
    first = place_ref[0, apart]
    second = place_ref[1, apart]
    block = tables_ref[first, (me * capacity) % LANES + slot % capacity]
    half = blocks // 2
    devices = place_ref.shape[1]
    row = jnp.where(
        block < half,
        first * (half + extra) + block,
        devices * (half + extra) + second * half + block - half,
    )
    return row, first * blocks + block


def fetch(pieces, gathered, semaphore):
    start = 0
    copies = []
    for number, piece in enumerate(pieces):
        count = piece.shape[0]
        copy = pltpu.make_async_copy(
            piece, gathered.at[pl.ds(start, count)], semaphore.at[number]
        )
        copy.start()
        copies.append(copy)
        start += count
    return copies


def in_turn(blocks, build, sums):
    build(0, 0)

    @pl.loop(0, blocks // 2)
    def _(pair):
        build(pair * 2 + 1, 1)
        sums(pair * 2, 0)
        build(jnp.minimum(pair * 2 + 2, blocks - 1), 0)
        sums(pair * 2 + 1, 1)


def remote_first_kernel(
    capacity,
    extra,
    slots_ref,
    tables_ref,
    place_ref,
    me_ref,
    piece0,
    piece1,
    piece2,
    piece3,
    own_ref,
    fields_ref,
    centre_ref,
    entropy_ref,
    moments_ref,
    dense_ref,
    density_ref,
    divergence_ref,
    weight_ref,
    gradient_ref,
    gathered,
    near0,
    near1,
    moment0,
    moment1,
    mass0,
    mass1,
    sums_ref,
    semaphore,
):
    blocks = fields_ref.shape[0]
    partners = slots_ref.shape[1]
    copies = fetch((piece0, piece1, piece2, piece3), gathered, semaphore)
    for copy in copies:
        copy.wait()
    centre = centre_ref[...]
    me = me_ref[0]
    sides = ((near0, moment0, mass0), (near1, moment1, mass1))

    def build(index, side):
        near, moment, mass = sides[side]
        for k in range(partners):
            row, _ = slot_place(
                slots_ref[index, k], tables_ref, place_ref, me, capacity, blocks, extra
            )
            fields = gathered[row]
            at = slice(k * LANES, (k + 1) * LANES)
            near[at, :], moment[:, at] = first_near(fields, centre)
            mass[at, :] = spread(fields[6:7])

    def sums(index, side):
        near, moment, mass = sides[side]
        at = pl.ds(pl.multiple_of(index * LANES, LANES), LANES)
        dense, total = pair_sums(
            own_ref[:, at], near, moment, mass, 0, 512, partners * LANES // 512
        )
        sums_ref[index, 0:8, :] = fold_rows(total, 8) + moments_ref[:, at]
        sums_ref[index, 8:16, :] = dense + dense_ref[:, at]

    in_turn(blocks, build, sums)
    total = sums_ref[:, 8, :]
    for row in range(9, 16):
        total = total + sums_ref[:, row, :]
    moments = [sums_ref[:, row, :] for row in range(8)]
    own = [fields_ref[:, row, :] - centre[row : row + 1, :] for row in range(8)]
    inverse = 1.0 / own[7]
    cube = inverse * inverse * inverse
    density = total * cube * (kernel_norm / 256.0)
    factor = cube * inverse * inverse * (20.0 * kernel_norm / 64.0)
    cross = own[0] * own[3] + own[1] * own[4] + own[2] * own[5]
    approach = cross * moments[6] + moments[7]
    for row in range(3):
        approach = approach - own[row + 3] * moments[row] - own[row] * moments[row + 3]
    press = entropy_ref[...] * inverse_cube_root(density)
    density_ref[...] = density
    divergence_ref[...] = factor * approach / density
    weight_ref[...] = (20.0 * kernel_norm) * own[6] * press * (cube * inverse * inverse)
    for row in range(3):
        gradient = (own[row] * moments[6] - moments[row]) * (factor * press)
        gradient_ref[row] = gradient


def inverse_cube_root(value):
    guess = jnp.exp(jnp.log(value) * (-1.0 / 3.0))
    guess = guess * (4.0 - value * guess * guess * guess) * (1.0 / 3.0)
    return guess * (4.0 - value * guess * guess * guess) * (1.0 / 3.0)


def prepare_second_kernel(fields_ref, centre_ref, weight_ref, near_ref, moment_ref):
    blocks = fields_ref.shape[0]
    centre = centre_ref[...]

    @pl.loop(0, blocks // 4)
    def _(group):
        for part in range(4):
            index = group * 4 + part
            at = pl.ds(pl.multiple_of(index * LANES, LANES), LANES)
            near_ref[at, :], moment_ref[:, at] = second_near(
                fields_ref[index], centre, weight_ref[pl.ds(index, 1), :]
            )


def remote_second_kernel(
    capacity,
    extra,
    slots_ref,
    tables_ref,
    place_ref,
    me_ref,
    active_ref,
    piece0,
    piece1,
    piece2,
    piece3,
    weight0,
    weight1,
    own_ref,
    fields_ref,
    centre_ref,
    moments_ref,
    gradient_ref,
    out_ref,
    gathered,
    weights,
    near0,
    near1,
    moment0,
    moment1,
    semaphore,
    weight_semaphore,
):
    blocks = fields_ref.shape[0]
    partners = slots_ref.shape[1]
    copies = fetch((piece0, piece1, piece2, piece3), gathered, semaphore)
    copies += fetch((weight0, weight1), weights, weight_semaphore)
    for copy in copies:
        copy.wait()
    centre = centre_ref[...]
    me = me_ref[0]
    sides = ((near0, moment0), (near1, moment1))

    def build(index, side):
        near, moment = sides[side]
        for k in range(partners):
            row, weight_row = slot_place(
                slots_ref[index, k], tables_ref, place_ref, me, capacity, blocks, extra
            )
            at = slice(k * LANES, (k + 1) * LANES)
            near[at, :], moment[:, at] = second_near(
                gathered[row], centre, weights[pl.ds(weight_row, 1), :]
            )

    def sums(index, side):
        near, moment = sides[side]
        at = pl.ds(pl.multiple_of(index * LANES, LANES), LANES)
        _, total = pair_sums(
            own_ref[:, at], near, moment, None, 0, 512, partners * LANES // 512
        )
        total = fold_rows(total, 4) + moments_ref[0:4, at]
        pos, _, _ = particle_rows(fields_ref[index], centre)
        out = gradient_ref[:, index, :] + (pos * total[3:4] - total[0:3])
        out_ref[index] = jnp.where(active_ref[index] > 0, out, 0.0)

    in_turn(blocks, build, sums)


def join_kernel(*refs):
    count = (len(refs) - 1) // 3
    copies = []
    for number in range(count):
        out = refs[2 * count + number]
        start = 0
        for part in range(2):
            piece = refs[2 * number + part]
            copy = pltpu.make_async_copy(
                piece, out.at[pl.ds(start, piece.shape[0])], refs[-1].at[2 * number + part]
            )
            copy.start()
            copies.append(copy)
            start += piece.shape[0]
    for copy in copies:
        copy.wait()


def in_vmem(count):
    return [pl.BlockSpec(memory_space=pltpu.VMEM)] * count


def in_smem(count):
    return [pl.BlockSpec(memory_space=pltpu.SMEM)] * count


def in_any(count):
    return [pl.BlockSpec(memory_space=pl.ANY)] * count


def shape(*dims, dtype=f32):
    return jax.ShapeDtypeStruct(dims, dtype)


params = pltpu.CompilerParams(vmem_limit_bytes=48 * 2**20)


def join(*pairs):
    flat = [item for pair in pairs for item in pair]
    outs = [shape(2 * pair[0].shape[0], *pair[0].shape[1:]) for pair in pairs]
    return pl.pallas_call(
        join_kernel,
        out_shape=outs,
        in_specs=in_any(len(flat)),
        out_specs=in_any(len(outs)),
        scratch_shapes=[pltpu.SemaphoreType.DMA((len(flat),))],
        compiler_params=params,
    )(*flat)


def prepare(fields):
    particles = fields.shape[0] * LANES
    return pl.pallas_call(
        prepare_kernel,
        out_shape=[
            shape(particles, FEATS, dtype=bf16),
            shape(32, particles, dtype=bf16),
            shape(particles, LANES),
            shape(FEATS, particles, dtype=bf16),
            shape(FEATS, particles, dtype=bf16),
            shape(8, LANES),
        ],
        in_specs=in_vmem(1),
        out_specs=in_vmem(6),
        compiler_params=params,
    )(fields)


def prepare_second(fields, centre, weight):
    particles = fields.shape[0] * LANES
    return pl.pallas_call(
        prepare_second_kernel,
        out_shape=[
            shape(particles, FEATS, dtype=bf16),
            shape(16, particles, dtype=bf16),
        ],
        in_specs=in_vmem(3),
        out_specs=in_vmem(2),
        compiler_params=params,
    )(fields, centre, weight)


def local_pass(kernel, first, count, own, whole, sums):
    particles = own.shape[1]
    fixed = lambda index: (0, 0)
    here = lambda index: (0, first + index)
    height = 2 if kernel is local_first_kernel else 1
    outs = [shape(8, particles)] * height
    aliases = {}
    operands = [own, *whole]
    in_specs = [pl.BlockSpec((FEATS, TILE), here)]
    in_specs += [pl.BlockSpec(item.shape, fixed) for item in whole]
    if sums is not None:
        aliases = {len(operands) + number: number for number in range(height)}
        operands += list(sums)
        in_specs += in_any(height)
    return pl.pallas_call(
        kernel,
        grid=(count,),
        in_specs=in_specs,
        out_specs=[pl.BlockSpec((8, TILE), here)] * height,
        out_shape=outs,
        input_output_aliases=aliases,
        cost_estimate=pl.CostEstimate(
            flops=count * TILE * particles * 2000, bytes_accessed=2**20, transcendentals=0
        ),
        compiler_params=params,
    )(*operands)


def swap(value, bit, devices):
    return lax.ppermute(value, "dom", [(i, i ^ bit) for i in range(devices)])


def places(order, devices):
    table = np.zeros((devices,), np.int32)
    for apart in range(devices):
        table[apart] = sum(1 << k for k, bit in enumerate(order) if apart & bit)
    return table


def shares(tiles, stages):
    cuts = [round(tiles * k / stages) for k in range(stages + 1)]
    return list(zip(cuts[:-1], cuts[1:]))


def per_device(
    devices,
    positions,
    velocities,
    masses,
    smoothing,
    entropy,
    export_blocks,
    partner_slots,
    active,
):
    blocks = positions.shape[0]
    particles = blocks * LANES
    capacity = export_blocks.shape[2]
    half = blocks // 2
    me = lax.axis_index("dom")
    fields = jnp.concatenate(
        [positions, velocities, masses[:, None, :], smoothing[:, None, :]], axis=1
    )
    words = devices * capacity
    extra = -(-words // (8 * LANES))
    table = export_blocks.astype(f32).reshape(words)
    table = jnp.pad(table, (0, extra * 8 * LANES - words)).reshape(extra, 8, LANES)
    bits = [1 << k for k in reversed(range(devices.bit_length() - 1))]
    order0 = list(bits)
    order1 = list(bits)
    order1[-3:-1] = reversed(order1[-3:-1])
    place = jnp.asarray(np.stack([places(order0, devices), places(order1, devices)]))
    tiles = particles // TILE
    stages = len(bits)

    near, moment, mass, own, own2, centre = prepare(fields)
    first = jnp.concatenate([fields[:half], table], axis=0)
    second = fields[half:]
    sums = None
    for number, (start, stop) in enumerate(shares(tiles, stages)):
        first_in = swap(first, order0[number], devices)
        second_in = swap(second, order1[number], devices)
        if stop > start:
            sums = local_pass(
                local_first_kernel, start, stop - start, own, (near, moment, mass), sums
            )
        if number < stages - 1:
            first, first_in, second, second_in, near, sums = lax.optimization_barrier(
                (first, first_in, second, second_in, near, sums)
            )
            first, second = join((first, first_in), (second, second_in))
    pieces = (first, first_in, second, second_in)

    step = half + extra
    line = (me * capacity) // LANES
    tables = [
        lax.dynamic_slice(
            item.reshape(devices // 2, step, 8, LANES),
            (0, half + line // 8, line % 8, 0),
            (devices // 2, 1, 1, LANES),
        ).reshape(devices // 2, LANES)
        for item in (first, first_in)
    ]
    tables = jnp.concatenate(tables, axis=0).astype(jnp.int32)
    me_array = me.astype(jnp.int32).reshape(1)

    rows = sum(piece.shape[0] for piece in pieces)
    partners = partner_slots.shape[1] * LANES
    near_side = [pltpu.VMEM((partners, FEATS), bf16)] * 2
    density, divergence, weight, gradient = pl.pallas_call(
        functools.partial(remote_first_kernel, capacity, extra),
        out_shape=[
            shape(blocks, LANES),
            shape(blocks, LANES),
            shape(blocks, LANES),
            shape(3, blocks, LANES),
        ],
        in_specs=in_smem(4) + in_any(4) + in_vmem(6),
        out_specs=in_vmem(4),
        scratch_shapes=[
            pltpu.VMEM((rows, 8, LANES), f32),
            *near_side,
            pltpu.VMEM((32, partners), bf16),
            pltpu.VMEM((32, partners), bf16),
            pltpu.VMEM((partners, LANES), f32),
            pltpu.VMEM((partners, LANES), f32),
            pltpu.VMEM((blocks, 16, LANES), f32),
            pltpu.SemaphoreType.DMA((4,)),
        ],
        compiler_params=params,
    )(
        partner_slots, tables, place, me_array, *pieces, own, fields, centre, entropy, *sums
    )

    near2, moment2 = prepare_second(fields, centre, weight)
    sums = None
    for number, (start, stop) in enumerate(shares(tiles, stages)):
        weight_in = swap(weight, order0[number], devices)
        if stop > start:
            sums = local_pass(
                local_second_kernel, start, stop - start, own2, (near2, moment2), sums
            )
        if number < stages - 1:
            weight, weight_in, near2, sums = lax.optimization_barrier(
                (weight, weight_in, near2, sums)
            )
            (weight,) = join((weight, weight_in))

    acceleration = pl.pallas_call(
        functools.partial(remote_second_kernel, capacity, extra),
        out_shape=shape(blocks, 3, LANES),
        in_specs=in_smem(5) + in_any(6) + in_vmem(5),
        out_specs=pl.BlockSpec(memory_space=pltpu.VMEM),
        scratch_shapes=[
            pltpu.VMEM((rows, 8, LANES), f32),
            pltpu.VMEM((devices * blocks, LANES), f32),
            *near_side,
            pltpu.VMEM((16, partners), bf16),
            pltpu.VMEM((16, partners), bf16),
            pltpu.SemaphoreType.DMA((4,)),
            pltpu.SemaphoreType.DMA((2,)),
        ],
        compiler_params=params,
    )(
        partner_slots, tables, place, me_array, active, *pieces, weight, weight_in, own2,
        fields, centre, *sums, gradient,
    )
    return (density, divergence, acceleration)


def solution(mesh):
    in_specs = (
        P("dom", None, None),
        P("dom", None, None),
        P("dom", None),
        P("dom", None),
        P("dom", None),
        P("dom", None, None),
        P("dom", None),
        P("dom"),
    )
    out_specs = (P("dom", None), P("dom", None), P("dom", None, None))
    return jax.shard_map(
        functools.partial(per_device, mesh.shape["dom"]),
        mesh=mesh,
        in_specs=in_specs,
        out_specs=out_specs,
        check_vma=False,
    )
```

time: 900 us -> 170 us (0.19)
  other arithmetic: 608 us -> 1.54 us
  local copies, waits for them, and re-layouts: 166 us -> 10.3 us
  Pallas kernels: 0 us -> 136 us
  blocking collectives: 86 us -> 0 us
  starting transfers between devices: 0.04 us -> 17 us
  between operations: 14.2 us -> 0.95 us
  waiting for transfers between devices: 14.7 us -> 3.81 us
    reduce_sum x128 -> x0, other arithmetic: 483 us -> none  [the longest x32 202 us: density_block(): approach = jnp.sum(moving * offset, axis=1)]
    pallas_call x0 -> x22, Pallas kernels: none -> 136 us  [the longest x10 69.3 us: local_pass(): pl.pallas_call(kernel, grid=(count,), in_specs=in_specs, out_specs=[pl.Bl...]
    mul x65 -> x0, other arithmetic: 119 us -> none  [the longest x32 118 us: force_block(): near_mass[:, :, None]]
    all_gather x2 -> x0, blocking collectives: 86 us -> none  [the longest x1 45.5 us: per_device(): tables = lax.all_gather(export_blocks, 'dom', axis=0, tiled=True)]
    squeeze x64 -> x0, local copies, waits for them, and re-layouts: 60.5 us -> none  [per_device(): density, divergence = lax.map(first_pass, (fields, near))]
    dynamic_update_slice x128 -> x0, local copies, waits for them, and re-layouts: 44.4 us -> none  [the longest x64 42.8 us: per_device(): density, divergence = lax.map(first_pass, (fields, near))]
    dynamic_slice x65 -> x2, local copies, waits for them, and re-layouts: 43.6 us -> 0.03 us  [per_device(): lax.dynamic_slice(item.reshape(devices // 2, step, 8, LANES), (0, half +...]
    ppermute x0 -> x15, starting transfers between devices: none -> 17 us  [swap(): return lax.ppermute(value, 'dom', [(i, i ^ bit) for i in range(devices)])]
  transfers between devices with their start and end apart: 1 -> 15, of which waited for: 1 -> 2; matrix products, arithmetic and copies ran while one was open for 1% -> 0% of each run, Pallas kernels for 0% -> 42%
where the time goes in v2:
time: 170 us; the launch traced here: 169 us
  Pallas kernels  136 us (80%)
  starting transfers between devices  17 us (10%)
  local copies, waits for them, and re-layouts  10.3 us (6%)
  waiting for transfers between devices  3.81 us (2%)
    pallas_call x10, Pallas kernels, local_pass(): pl.pallas_call(kernel, grid=(count,), in_specs=in_specs, out_specs=[pl.Bl...  69.3 us
    pallas_call x1, Pallas kernels, per_device(): pl.pallas_call(functools.partial(remote_first_kernel, capacity, extra), o...  35.1 us
    pallas_call x1, Pallas kernels, per_device(): pl.pallas_call(functools.partial(remote_second_kernel, capacity, extra),...  26.2 us
    ppermute x15, starting transfers between devices, swap(): return lax.ppermute(value, 'dom', [(i, i ^ bit) for i in range(devices)])  17 us
    unnamed x38, local copies, waits for them, and re-layouts  10.2 us
    ppermute x15, waiting for transfers between devices, swap(): return lax.ppermute(value, 'dom', [(i, i ^ bit) for i in range(devices)])  3.81 us
  transfers between devices with their start and end apart: 15, of which 2 were waited for; matrix products, arithmetic and copies ran while one was open for 0% of the time, Pallas kernels for 42%

profile of v2, /device:TPU:0, one launch (start us, length us, event | category | flops | bytes accessed | tf_op | source)
XLA Modules:
  0.0 169.3 jit_solution(3310071026527116830)
XLA Ops:
  0.6 0.8 copy.24
  1.5 0.8 copy.25
  2.3 0.8 pad_maximum_fusion.fields_ref
  3.1 0.7 convert_element_type.6
  3.9 0.1 reshape.26
  3.9 4.1 %collective-permute-start = (f32[17,8,128]{2,1,0:T(8,128)S(1)}, f32[17,8,128]{2,1,0:T(8,128)S(1)}, u32[]{:S(2)}, u32[]{:S(2)}) collective-permute-start(f32[17,8,128]{2,1,0:T(8,128)S(1)} %pad_maximum_fusion.1.refs_0_), channel_id=1, source_target_pairs={{0,16},{1,17},{2,18},{3,19},{4,20},{5,21},{6,22},{7,23},{8,24},{9,... | collective-permute-start | bytes 208904 | tf_op jit(solution)/shard_map/ppermute | solution.py:524
  8.0 0.1 collective-permute-start.1
  8.1 1.7 shard_map.112
  9.8 0.8 copy-done
  10.5 7.5 %shard_map.113 = (f32[8,4096]{1,0:T(8,128)S(1)}, f32[8,4096]{1,0:T(8,128)S(1)}) custom-call(bf16[48,4096]{1,0:T(8,128)(2,1)S(1)} %get-tuple-element.78.own_ref, bf16[4096,48]{1,0:T(8,128)(2,1)S(1)} %get-tuple-element.123.near_ref, bf16[32,4096]{1,0:T(8,128)(2,1)S(1)} %get-tuple-element.79.moment_ref, f32[4096,128]{1,0:T(8,128)S(1)} %get-tuple-element.80.mass_ref), custom_call_target="tpu_custom_call" | custom-call | flops 6291456000 | bytes 1048576 | tf_op jit(solution)/shard_map/pallas_call | solution.py:509
  18.1 0.0 collective-permute-done.1.refs_3_
  18.1 0.0 collective-permute-done.refs_1_
  18.1 0.4 shard_map.114
  18.5 1.9 %collective-permute-start.2 = (f32[34,8,128]{2,1,0:T(8,128)S(1)}, f32[34,8,128]{2,1,0:T(8,128)S(1)}, u32[]{:S(2)}, u32[]{:S(2)}) collective-permute-start(f32[34,8,128]{2,1,0:T(8,128)S(1)} %get-tuple-element.94.refs_0_), channel_id=1, source_target_pairs={{0,8},{1,9},{2,10},{3,11},{4,12},{5,13},{6,14},{7,15},{8,0},{9,1},... | collective-permute-start | bytes 417800 | tf_op jit(solution)/shard_map/ppermute | solution.py:524
  20.4 0.2 collective-permute-start.3
  20.6 7.5 %shard_map.115 = (f32[8,4096]{1,0:T(8,128)S(1)}, f32[8,4096]{1,0:T(8,128)S(1)}) custom-call(bf16[48,4096]{1,0:T(8,128)(2,1)S(1)} %get-tuple-element.78.own_ref, bf16[4096,48]{1,0:T(8,128)(2,1)S(1)} %get-tuple-element.123.near_ref, bf16[32,4096]{1,0:T(8,128)(2,1)S(1)} %get-tuple-element.79.moment_ref, ...), custom_call_target="tpu_custom_call", output_to_operand_aliasing={{0}: (4, {}), {1}: (5, {})} | custom-call | flops 6291456000 | bytes 1048576 | tf_op jit(solution)/shard_map/pallas_call | solution.py:509
  28.1 0.0 collective-permute-done.3.refs_3_
  28.1 0.0 collective-permute-done.2.refs_1_
  28.2 0.7 shard_map.116
  28.9 1.8 %collective-permute-start.4 = (f32[68,8,128]{2,1,0:T(8,128)S(1)}, f32[68,8,128]{2,1,0:T(8,128)S(1)}, u32[]{:S(2)}, u32[]{:S(2)}) collective-permute-start(f32[68,8,128]{2,1,0:T(8,128)S(1)} %get-tuple-element.105.refs_0_), channel_id=1, source_target_pairs={{0,4},{1,5},{2,6},{3,7},{4,0},{5,1},{6,2},{7,3},{8,12},{9,13},{10,... | collective-permute-start | bytes 835592 | tf_op jit(solution)/shard_map/ppermute | solution.py:524
  30.7 1.5 collective-permute-start.5
  32.2 10.0 %shard_map.117 = (f32[8,4096]{1,0:T(8,128)S(1)}, f32[8,4096]{1,0:T(8,128)S(1)}) custom-call(bf16[48,4096]{1,0:T(8,128)(2,1)S(1)} %get-tuple-element.78.own_ref, bf16[4096,48]{1,0:T(8,128)(2,1)S(1)} %get-tuple-element.123.near_ref, bf16[32,4096]{1,0:T(8,128)(2,1)S(1)} %get-tuple-element.79.moment_ref, ...), custom_call_target="tpu_custom_call", output_to_operand_aliasing={{0}: (4, {}), {1}: (5, {})} | custom-call | flops 8388608000 | bytes 1048576 | tf_op jit(solution)/shard_map/pallas_call | solution.py:509
  42.3 0.0 collective-permute-done.4.refs_1_
  42.3 0.2 shard_map.118
  42.4 0.6 collective-permute-start.6
  43.0 0.3 collective-permute-start.7
  43.3 7.5 %shard_map.119 = (f32[8,4096]{1,0:T(8,128)S(1)}, f32[8,4096]{1,0:T(8,128)S(1)}) custom-call(bf16[48,4096]{1,0:T(8,128)(2,1)S(1)} %get-tuple-element.78.own_ref, bf16[4096,48]{1,0:T(8,128)(2,1)S(1)} %get-tuple-element.123.near_ref, bf16[32,4096]{1,0:T(8,128)(2,1)S(1)} %get-tuple-element.79.moment_ref, ...), custom_call_target="tpu_custom_call", output_to_operand_aliasing={{0}: (4, {}), {1}: (5, {})} | custom-call | flops 6291456000 | bytes 1048576 | tf_op jit(solution)/shard_map/pallas_call | solution.py:509
  50.9 0.7 copy-done.4
  51.5 3.3 %collective-permute-done.7.refs_3_ = f32[128,8,128]{2,1,0:T(8,128)S(1)} collective-permute-done((f32[128,8,128]{2,1,0:T(8,128)S(1)}, f32[128,8,128]{2,1,0:T(8,128)S(1)}, u32[]{:S(2)}, u32[]{:S(2)}) %collective-permute-start.7) | collective-permute-done | bytes 524320 | tf_op jit(solution)/shard_map/ppermute | solution.py:524
  54.8 0.4 collective-permute-done.6.refs_1_
  55.2 0.3 shard_map.120
  55.5 0.1 collective-permute-start.8
  55.6 0.5 collective-permute-start.9
  56.1 0.8 copy.27.slots_ref
  56.9 1.0 copy-done.3
  57.9 0.9 copy-done.5
  58.8 1.6 copy-done.12
  60.4 1.2 copy-done.14
  61.6 0.9 copy-done.16
  62.5 7.5 %shard_map.121 = (f32[8,4096]{1,0:T(8,128)S(1)}, f32[8,4096]{1,0:T(8,128)S(1)}) custom-call(bf16[48,4096]{1,0:T(8,128)(2,1)S(1)} %copy-done.3, bf16[4096,48]{1,0:T(8,128)(2,1)S(1)} %copy-done.14, bf16[32,4096]{1,0:T(8,128)(2,1)S(1)} %copy-done.16, f32[4096,128]{1,0:T(8,128)S(1)} %copy-done.12, ...), custom_call_target="tpu_custom_call", output_to_operand_aliasing={{0}: (4, {}), {1}: (5, {})} | custom-call | flops 6291456000 | bytes 1048576 | tf_op jit(solution)/shard_map/pallas_call | solution.py:509
  70.2 35.1 %shard_map.122 = (f32[32,128]{1,0:T(8,128)}, f32[32,128]{1,0:T(8,128)}, f32[32,128]{1,0:T(8,128)S(1)}, f32[3,32,128]{2,1,0:T(8,128)S(1)}) custom-call(s32[32,16]{1,0:T(8,128)S(1)} %copy.27.slots_ref, s32[32,128]{1,0:T(8,128)S(1)} %maximum_convert_fusion.tables_ref, s32[2,32]{1,0:T(2,128)S(1)} %copy-done.9, s32[1]{0:T(128)} %bitcast.6.me_ref, ...), custom_call_target="tpu_custom_call" | custom-call | tf_op jit(solution)/shard_map/pallas_call | solution.py:604
  105.2 1.1 shard_map.123
  106.3 2.6 %collective-permute-start.10 = (f32[32,128]{1,0:T(8,128)S(1)}, f32[32,128]{1,0:T(8,128)S(1)}, u32[]{:S(2)}, u32[]{:S(2)}) collective-permute-start(f32[32,128]{1,0:T(8,128)S(1)} %get-tuple-element.134.weight_ref.refs_0_), channel_id=1, source_target_pairs={{0,16},{1,17},{2,18},{3,19},{4,20},{5,21},{6,22},{7,23},{8,24},{9,... | collective-permute-start | bytes 49160 | tf_op jit(solution)/shard_map/ppermute | solution.py:524
  109.0 5.5 %shard_map.124.refs_0_ = f32[8,4096]{1,0:T(8,128)S(1)} custom-call(bf16[48,4096]{1,0:T(8,128)(2,1)S(1)} %copy-done.1, bf16[4096,48]{1,0:T(8,128)(2,1)S(1)} %get-tuple-element.148.near_ref, bf16[16,4096]{1,0:T(8,128)(2,1)S(1)} %get-tuple-element.133.moment_ref), custom_call_target="tpu_custom_call" | custom-call | flops 6291456000 | bytes 1048576 | tf_op jit(solution)/shard_map/pallas_call | solution.py:509
  114.4 0.0 collective-permute-done.10.refs_1_
  114.4 0.1 shard_map.125.refs_0_
  114.5 1.7 collective-permute-start.11
  116.2 5.5 %shard_map.126.refs_0_ = f32[8,4096]{1,0:T(8,128)S(1)} custom-call(bf16[48,4096]{1,0:T(8,128)(2,1)S(1)} %copy-done.1, bf16[4096,48]{1,0:T(8,128)(2,1)S(1)} %get-tuple-element.148.near_ref, bf16[16,4096]{1,0:T(8,128)(2,1)S(1)} %get-tuple-element.133.moment_ref, f32[8,4096]{1,0:T(8,128)S(1)} %shard_map.124.refs_0_), custom_call_target="tpu_custom_call", output_to_operand_aliasing={{}: (3, {})} | custom-call | flops 6291456000 | bytes 1048576 | tf_op jit(solution)/shard_map/pallas_call | solution.py:509
  121.6 0.0 collective-permute-done.11.refs_1_
  121.7 0.1 shard_map.127.refs_0_
  121.8 0.6 collective-permute-start.12
  122.3 7.3 %shard_map.128.refs_0_ = f32[8,4096]{1,0:T(8,128)S(1)} custom-call(bf16[48,4096]{1,0:T(8,128)(2,1)S(1)} %copy-done.1, bf16[4096,48]{1,0:T(8,128)(2,1)S(1)} %get-tuple-element.148.near_ref, bf16[16,4096]{1,0:T(8,128)(2,1)S(1)} %get-tuple-element.133.moment_ref, f32[8,4096]{1,0:T(8,128)S(1)} %shard_map.126.refs_0_), custom_call_target="tpu_custom_call", output_to_operand_aliasing={{}: (3, {})} | custom-call | flops 8388608000 | bytes 1048576 | tf_op jit(solution)/shard_map/pallas_call | solution.py:509
  129.6 0.0 collective-permute-done.12.refs_1_
  129.7 0.2 shard_map.129.refs_0_
  129.9 1.1 collective-permute-start.13
  131.0 5.5 %shard_map.130.refs_0_ = f32[8,4096]{1,0:T(8,128)S(1)} custom-call(bf16[48,4096]{1,0:T(8,128)(2,1)S(1)} %copy-done.1, bf16[4096,48]{1,0:T(8,128)(2,1)S(1)} %get-tuple-element.148.near_ref, bf16[16,4096]{1,0:T(8,128)(2,1)S(1)} %get-tuple-element.133.moment_ref, f32[8,4096]{1,0:T(8,128)S(1)} %shard_map.128.refs_0_), custom_call_target="tpu_custom_call", output_to_operand_aliasing={{}: (3, {})} | custom-call | flops 6291456000 | bytes 1048576 | tf_op jit(solution)/shard_map/pallas_call | solution.py:509
  136.4 0.0 collective-permute-done.13.refs_1_
  136.4 0.4 shard_map.131.weight0
  136.8 0.0 copy-start.10
  136.8 0.1 collective-permute-start.14
  136.9 5.5 %shard_map.132.moments_ref = f32[8,4096]{1,0:T(8,128)S(1)} custom-call(bf16[48,4096]{1,0:T(8,128)(2,1)S(1)} %copy-done.1, bf16[4096,48]{1,0:T(8,128)(2,1)S(1)} %get-tuple-element.148.near_ref, bf16[16,4096]{1,0:T(8,128)(2,1)S(1)} %get-tuple-element.133.moment_ref, f32[8,4096]{1,0:T(8,128)S(1)} %shard_map.130.refs_0_), custom_call_target="tpu_custom_call", output_to_operand_aliasing={{}: (3, {})} | custom-call | flops 6291456000 | bytes 1048576 | tf_op jit(solution)/shard_map/pallas_call | solution.py:509
  142.4 0.0 collective-permute-done.14.weight1
  142.4 26.2 %shard_map.133 = f32[32,3,128]{2,1,0:T(4,128)S(1)} custom-call(s32[32,16]{1,0:T(8,128)S(1)} %copy.27.slots_ref, s32[32,128]{1,0:T(8,128)S(1)} %maximum_convert_fusion.tables_ref, s32[2,32]{1,0:T(2,128)S(1)} %copy-done.9, s32[1]{0:T(128)} %bitcast.6.me_ref, s32[32]{0:T(128)S(1)} %copy-done.10, f32[272,8,128]{2,1,0:T(8,128)S(1)} %get-tuple-element.120.piece0, ...), custom_call_target="tpu_custom_call" | custom-call | tf_op jit(solution)/shard_map/pallas_call | solution.py:643
  168.7 0.6 copy.29
  (34 shorter events, 0.1 us)
Async XLA Ops:
  3.9 14.2 %collective-permute-start = (f32[17,8,128]{2,1,0:T(8,128)S(1)}, f32[17,8,128]{2,1,0:T(8,128)S(1)}, u32[]{:S(2)}, u32[]{:S(2)}) collective-permute-start(f32[17,8,128]{2,1,0:T(8,128)S(1)} %pad_maximum_fusion.1.refs_0_), channel_id=1, source_target_pairs={{0,16},{1,17},{2,18},{3,19},{4,20},{5,21},{6,22},{7,23},{8,24},{9,... | collective-permute-start | bytes 208904 | tf_op jit(solution)/shard_map/ppermute | solution.py:524
  8.0 10.1 %collective-permute-start.1 = (f32[16,8,128]{2,1,0:T(8,128)S(1)}, f32[16,8,128]{2,1,0:T(8,128)S(1)}, u32[]{:S(2)}, u32[]{:S(2)}) collective-permute-start(f32[16,8,128]{2,1,0:T(8,128)S(1)} %get-tuple-element.85.refs_2_), channel_id=1, source_target_pairs={{0,16},{1,17},{2,18},{3,19},{4,20},{5,21},{6,22},{7,23},{8,24},{9,... | collective-permute-start | bytes 196616 | tf_op jit(solution)/shard_map/ppermute | solution.py:524
  9.8 0.8 copy-start
  10.5 7.6 %copy-start.6 = (f32[8,128]{1,0:T(8,128)}, f32[8,128]{1,0:T(8,128)S(1)}, u32[]{:S(2)}) copy-start(f32[8,128]{1,0:T(8,128)S(1)} %get-tuple-element.122.centre_ref) | copy-start | bytes 12292
  10.5 32.8 %copy-start.2 = (bf16[48,4096]{1,0:T(8,128)(2,1)}, bf16[48,4096]{1,0:T(8,128)(2,1)S(1)}, u32[]{:S(2)}) copy-start(bf16[48,4096]{1,0:T(8,128)(2,1)S(1)} %get-tuple-element.78.own_ref) | copy-start | bytes 1179652
  10.5 32.8 %copy-start.11 = (f32[4096,128]{1,0:T(8,128)}, f32[4096,128]{1,0:T(8,128)S(1)}, u32[]{:S(2)}) copy-start(f32[4096,128]{1,0:T(8,128)S(1)} %get-tuple-element.80.mass_ref) | copy-start | bytes 6291460
  10.5 32.8 %copy-start.13 = (bf16[4096,48]{1,0:T(8,128)(2,1)}, bf16[4096,48]{1,0:T(8,128)(2,1)S(1)}, u32[]{:S(2)}) copy-start(bf16[4096,48]{1,0:T(8,128)(2,1)S(1)} %get-tuple-element.123.near_ref) | copy-start | bytes 1179652
  10.5 32.8 %copy-start.15 = (bf16[32,4096]{1,0:T(8,128)(2,1)}, bf16[32,4096]{1,0:T(8,128)(2,1)S(1)}, u32[]{:S(2)}) copy-start(bf16[32,4096]{1,0:T(8,128)(2,1)S(1)} %get-tuple-element.79.moment_ref) | copy-start | bytes 786436
  18.5 9.6 %collective-permute-start.2 = (f32[34,8,128]{2,1,0:T(8,128)S(1)}, f32[34,8,128]{2,1,0:T(8,128)S(1)}, u32[]{:S(2)}, u32[]{:S(2)}) collective-permute-start(f32[34,8,128]{2,1,0:T(8,128)S(1)} %get-tuple-element.94.refs_0_), channel_id=1, source_target_pairs={{0,8},{1,9},{2,10},{3,11},{4,12},{5,13},{6,14},{7,15},{8,0},{9,1},... | collective-permute-start | bytes 417800 | tf_op jit(solution)/shard_map/ppermute | solution.py:524
  20.4 7.7 %collective-permute-start.3 = (f32[32,8,128]{2,1,0:T(8,128)S(1)}, f32[32,8,128]{2,1,0:T(8,128)S(1)}, u32[]{:S(2)}, u32[]{:S(2)}) collective-permute-start(f32[32,8,128]{2,1,0:T(8,128)S(1)} %get-tuple-element.96.refs_2_), channel_id=1, source_target_pairs={{0,8},{1,9},{2,10},{3,11},{4,12},{5,13},{6,14},{7,15},{8,0},{9,1},... | collective-permute-start | bytes 393224 | tf_op jit(solution)/shard_map/ppermute | solution.py:524
  28.9 13.4 %collective-permute-start.4 = (f32[68,8,128]{2,1,0:T(8,128)S(1)}, f32[68,8,128]{2,1,0:T(8,128)S(1)}, u32[]{:S(2)}, u32[]{:S(2)}) collective-permute-start(f32[68,8,128]{2,1,0:T(8,128)S(1)} %get-tuple-element.105.refs_0_), channel_id=1, source_target_pairs={{0,4},{1,5},{2,6},{3,7},{4,0},{5,1},{6,2},{7,3},{8,12},{9,13},{10,... | collective-permute-start | bytes 835592 | tf_op jit(solution)/shard_map/ppermute | solution.py:524
  30.7 11.5 %collective-permute-start.5 = (f32[64,8,128]{2,1,0:T(8,128)S(1)}, f32[64,8,128]{2,1,0:T(8,128)S(1)}, u32[]{:S(2)}, u32[]{:S(2)}) collective-permute-start(f32[64,8,128]{2,1,0:T(8,128)S(1)} %get-tuple-element.107.refs_2_), channel_id=1, source_target_pairs={{0,2},{1,3},{2,0},{3,1},{4,6},{5,7},{6,4},{7,5},{8,10},{9,11},{10,... | collective-permute-start | bytes 786440 | tf_op jit(solution)/shard_map/ppermute | solution.py:524
  42.4 12.8 %collective-permute-start.6 = (f32[136,8,128]{2,1,0:T(8,128)S(1)}, f32[136,8,128]{2,1,0:T(8,128)S(1)}, u32[]{:S(2)}, u32[]{:S(2)}) collective-permute-start(f32[136,8,128]{2,1,0:T(8,128)S(1)} %get-tuple-element.116.refs_0_), channel_id=1, source_target_pairs={{0,2},{1,3},{2,0},{3,1},{4,6},{5,7},{6,4},{7,5},{8,10},{9,11},{10,... | collective-permute-start | bytes 1671176 | tf_op jit(solution)/shard_map/ppermute | solution.py:524
  43.0 11.7 %collective-permute-start.7 = (f32[128,8,128]{2,1,0:T(8,128)S(1)}, f32[128,8,128]{2,1,0:T(8,128)S(1)}, u32[]{:S(2)}, u32[]{:S(2)}) collective-permute-start(f32[128,8,128]{2,1,0:T(8,128)S(1)} %get-tuple-element.118.refs_2_), channel_id=1, source_target_pairs={{0,4},{1,5},{2,6},{3,7},{4,0},{5,1},{6,2},{7,3},{8,12},{9,13},{10,... | collective-permute-start | bytes 1572872 | tf_op jit(solution)/shard_map/ppermute | solution.py:524
  50.9 0.7 copy-start.4
  55.5 14.6 %collective-permute-start.8 = (f32[272,8,128]{2,1,0:T(8,128)S(1)}, f32[272,8,128]{2,1,0:T(8,128)S(1)}, u32[]{:S(2)}, u32[]{:S(2)}) collective-permute-start(f32[272,8,128]{2,1,0:T(8,128)S(1)} %get-tuple-element.120.piece0), channel_id=1, source_target_pairs={{0,1},{1,0},{2,3},{3,2},{4,5},{5,4},{6,7},{7,6},{8,9},{9,8},{10,11... | collective-permute-start | bytes 3342344 | tf_op jit(solution)/shard_map/ppermute | solution.py:524
  55.6 14.5 %collective-permute-start.9 = (f32[256,8,128]{2,1,0:T(8,128)S(1)}, f32[256,8,128]{2,1,0:T(8,128)}, u32[]{:S(2)}, u32[]{:S(2)}) collective-permute-start(f32[256,8,128]{2,1,0:T(8,128)S(1)} %get-tuple-element.121.piece2), channel_id=1, source_target_pairs={{0,1},{1,0},{2,3},{3,2},{4,5},{5,4},{6,7},{7,6},{8,9},{9,8},{10,11... | collective-permute-start | bytes 3145736 | tf_op jit(solution)/shard_map/ppermute | solution.py:524
  56.9 1.0 copy-start.3
  57.9 0.9 copy-start.5
  58.8 1.6 copy-start.12
  60.3 1.2 copy-start.14
  61.6 0.9 copy-start.16
  62.5 7.6 %copy-start.7 = (f32[8,128]{1,0:T(8,128)S(1)}, f32[8,128]{1,0:T(8,128)}, u32[]{:S(2)}) copy-start(f32[8,128]{1,0:T(8,128)} %copy-done.6) | copy-start | bytes 12292
  62.5 7.6 %copy-start.8 = (f32[32,128]{1,0:T(8,128)S(1)}, f32[32,128]{1,0:T(8,128)}, u32[]{:S(2)}) copy-start(f32[32,128]{1,0:T(8,128)} %entropy_ref.1) | copy-start | bytes 49156
  62.5 7.6 %copy-start.9 = (s32[2,32]{1,0:T(2,128)S(1)}, s32[2,32]{1,0:T(2,128)}, u32[]{:S(2)}) copy-start(s32[2,32]{1,0:T(2,128)} %constant.54.clone.place_ref) | copy-start | bytes 772
  70.1 38.8 %copy-start.1 = (bf16[48,4096]{1,0:T(8,128)(2,1)S(1)}, bf16[48,4096]{1,0:T(8,128)(2,1)}, u32[]{:S(2)}) copy-start(bf16[48,4096]{1,0:T(8,128)(2,1)} %copy-done) | copy-start | bytes 1179652
  106.3 8.1 %collective-permute-start.10 = (f32[32,128]{1,0:T(8,128)S(1)}, f32[32,128]{1,0:T(8,128)S(1)}, u32[]{:S(2)}, u32[]{:S(2)}) collective-permute-start(f32[32,128]{1,0:T(8,128)S(1)} %get-tuple-element.134.weight_ref.refs_0_), channel_id=1, source_target_pairs={{0,16},{1,17},{2,18},{3,19},{4,20},{5,21},{6,22},{7,23},{8,24},{9,... | collective-permute-start | bytes 49160 | tf_op jit(solution)/shard_map/ppermute | solution.py:524
  114.5 7.1 %collective-permute-start.11 = (f32[64,128]{1,0:T(8,128)S(1)}, f32[64,128]{1,0:T(8,128)S(1)}, u32[]{:S(2)}, u32[]{:S(2)}) collective-permute-start(f32[64,128]{1,0:T(8,128)S(1)} %shard_map.125.refs_0_), channel_id=1, source_target_pairs={{0,8},{1,9},{2,10},{3,11},{4,12},{5,13},{6,14},{7,15},{8,0},{9,1},... | collective-permute-start | bytes 98312 | tf_op jit(solution)/shard_map/ppermute | solution.py:524
  121.8 7.9 %collective-permute-start.12 = (f32[128,128]{1,0:T(8,128)S(1)}, f32[128,128]{1,0:T(8,128)S(1)}, u32[]{:S(2)}, u32[]{:S(2)}) collective-permute-start(f32[128,128]{1,0:T(8,128)S(1)} %shard_map.127.refs_0_), channel_id=1, source_target_pairs={{0,4},{1,5},{2,6},{3,7},{4,0},{5,1},{6,2},{7,3},{8,12},{9,13},{10,... | collective-permute-start | bytes 196616 | tf_op jit(solution)/shard_map/ppermute | solution.py:524
  129.9 6.6 %collective-permute-start.13 = (f32[256,128]{1,0:T(8,128)S(1)}, f32[256,128]{1,0:T(8,128)S(1)}, u32[]{:S(2)}, u32[]{:S(2)}) collective-permute-start(f32[256,128]{1,0:T(8,128)S(1)} %shard_map.129.refs_0_), channel_id=1, source_target_pairs={{0,2},{1,3},{2,0},{3,1},{4,6},{5,7},{6,4},{7,5},{8,10},{9,11},{10,... | collective-permute-start | bytes 393224 | tf_op jit(solution)/shard_map/ppermute | solution.py:524
  136.8 5.6 %copy-start.10 = (s32[32]{0:T(128)S(1)}, s32[32]{0:T(128)}, u32[]{:S(2)}) copy-start(s32[32]{0:T(128)} %active_ref.1) | copy-start | bytes 388
  136.8 5.6 %collective-permute-start.14 = (f32[512,128]{1,0:T(8,128)S(1)}, f32[512,128]{1,0:T(8,128)S(1)}, u32[]{:S(2)}, u32[]{:S(2)}) collective-permute-start(f32[512,128]{1,0:T(8,128)S(1)} %shard_map.131.weight0), channel_id=1, source_target_pairs={{0,1},{1,0},{2,3},{3,2},{4,5},{5,4},{6,7},{7,6},{8,9},{9,8},{10,11... | collective-permute-start | bytes 786440 | tf_op jit(solution)/shard_map/ppermute | solution.py:524

commit v3 on v2

v3 whole, which is shorter than its diff:
```python
import functools

import jax
import jax.numpy as jnp
import numpy as np
from jax import lax
from jax.experimental import pallas as pl
from jax.experimental.pallas import tpu as pltpu
from jax.sharding import PartitionSpec as P

kernel_norm = 3.3422538049298023
LANES = 128
FEATS = 48
TILE = 256
PIECES = 8
bf16 = jnp.bfloat16
f32 = jnp.float32


def split3(value):
    high = value.astype(bf16).astype(f32)
    rest = value - high
    middle = rest.astype(bf16).astype(f32)
    return high, middle, rest - middle


def near_rows(four, last):
    high, middle, low = split3(jnp.concatenate([four, four], axis=0))
    upper = lax.broadcasted_iota(jnp.int32, high.shape, 0) < 4
    mixed = jnp.where(upper, high, middle)
    blank = jnp.zeros((FEATS - 40, LANES), f32)
    return jnp.concatenate([high, middle, low, mixed, *last, blank], axis=0)


def own_rows(four, last):
    high, middle, low = split3(four)
    pair = [high, middle]
    blank = jnp.zeros((FEATS - 35, LANES), f32)
    rows = pair * 3 + [low, low, *last, blank]
    return jnp.concatenate(rows, axis=0).astype(bf16)


def split_rows(value):
    parts = list(split3(value))
    if value.shape[0] % 8 == 0:
        parts.append(jnp.zeros_like(value))
    else:
        parts.append(jnp.zeros((16 - 3 * value.shape[0], LANES), f32))
    return jnp.concatenate(parts, axis=0).astype(bf16)


def fold_rows(moments, count):
    return moments[0:count] + (moments[count : 2 * count] + moments[2 * count : 3 * count])


def particle_rows(fields, centre):
    shifted = fields - centre
    pos = shifted[0:3]
    vel = shifted[3:6]
    square = jnp.sum(pos * pos, axis=0, keepdims=True)
    return pos, vel, square


def first_near(fields, centre):
    pos, vel, square = particle_rows(fields, centre)
    one = jnp.ones_like(square)
    cross = jnp.sum(pos * vel, axis=0, keepdims=True)
    last = [one, one, one, fields[6:7], jnp.zeros((4, LANES), f32)]
    near = near_rows(jnp.concatenate([pos, square], axis=0), last)
    moments = split_rows(jnp.concatenate([pos, vel, one, cross], axis=0))
    return near, moments


def second_near(fields, centre, weight):
    pos, _, square = particle_rows(fields, centre)
    inverse = 1.0 / fields[7:8]
    inverse = inverse * inverse
    last = [*split3(square * inverse), jnp.zeros((5, LANES), f32)]
    near = near_rows(jnp.concatenate([pos * inverse, inverse], axis=0), last)
    moments = split_rows(jnp.concatenate([pos * weight, weight], axis=0))
    return near, moments


MASS_ROW = 35


def spread(turned, column):
    return jnp.broadcast_to(turned[:, column : column + 1], (LANES, LANES))


def assemble_kernel(*refs):
    inputs, (fields_ref, first_ref, second_ref), buffers = refs[:5], refs[5:8], refs[8:13]
    semaphore = refs[13]
    copies = [
        pltpu.make_async_copy(source, target, semaphore.at[number])
        for number, (source, target) in enumerate(zip(inputs, buffers))
    ]
    for copy in copies:
        copy.start()
    for copy in copies:
        copy.wait()
    pos_ref, vel_ref, mass_ref, smooth_ref, table_ref = buffers
    blocks = fields_ref.shape[0]
    half = second_ref.shape[0]
    fields_ref[:, 0:3, :] = pos_ref[...]
    fields_ref[:, 3:6, :] = vel_ref[...]
    fields_ref[:, 6, :] = mass_ref[...]
    fields_ref[:, 7, :] = smooth_ref[...]
    first_ref[0 : blocks - half] = fields_ref[0 : blocks - half]
    second_ref[...] = fields_ref[blocks - half :]
    table = table_ref[0].astype(f32)
    devices, capacity = table.shape
    lines = [table[row : row + 8] for row in range(0, devices, 8)]
    each = LANES // capacity
    for number in range(0, len(lines), each):
        line = jnp.concatenate(lines[number : number + each], axis=1)
        first_ref[blocks - half + number // each, :, 0 : line.shape[1]] = line


def prepare_kernel(fields_ref, near_ref, moment_ref, mass_ref, own_ref, centre_ref):
    blocks = fields_ref.shape[0]
    total = jnp.sum(fields_ref[...], axis=0)
    mean = jnp.sum(total, axis=1, keepdims=True) / (blocks * LANES)
    rows = lax.broadcasted_iota(jnp.int32, (8, LANES), 0)
    centre = jnp.where(rows < 6, jnp.broadcast_to(mean, (8, LANES)), 0.0)
    centre_ref[...] = centre
    mass_ref[...] = fields_ref[:, 6, :].T

    @pl.loop(0, blocks // 4)
    def _(group):
        for part in range(4):
            index = group * 4 + part
            fields = fields_ref[index]
            at = pl.ds(pl.multiple_of(index * LANES, LANES), LANES)
            near, moment_ref[:, at] = first_near(fields, centre)
            near_ref[at, :] = near.T.astype(bf16)
            pos, _, square = particle_rows(fields, centre)
            smooth = fields[7:8]
            sigma = 16.0 / (smooth * smooth)
            four = jnp.concatenate([pos * (-2.0 * sigma), sigma], axis=0)
            own_ref[:, at] = own_rows(four, split3(square * sigma))


def halves(slope):
    high = slope.astype(bf16)
    low = (slope - high.astype(f32)).astype(bf16)
    return jnp.concatenate([high, low], axis=0)


def pair_sums(own, near_ref, moment_ref, mass_of, chunk):
    width = own.shape[1]
    steps = near_ref.shape[0] // chunk
    dense = None
    total = None

    def place(step):
        return pl.ds(step * chunk, chunk)

    def product(step):
        return jnp.dot(near_ref[place(step), :], own, preferred_element_type=f32)

    def moment(step, slope):
        fields = moment_ref[:, place(step)]
        both = jnp.concatenate([fields, fields], axis=1)
        return jnp.dot(both, slope, preferred_element_type=f32)

    square = product(0)
    slope = None
    for step in range(steps):
        following = product(step + 1) if step + 1 < steps else None
        square = jnp.maximum(square, 1e-12)
        radius = square * lax.rsqrt(square)
        if mass_of is None:
            tail = jnp.maximum(1.0 - radius, 0.0)
            cube = tail * tail * tail
        else:
            mass = mass_of(step)
            tail = jnp.maximum(4.0 - radius, 0.0)
            cube = tail * tail * tail * mass
            value = cube * (tail * (5.0 - tail))
            value = jnp.sum(value.reshape(chunk // 8, 8, width), axis=0)
            dense = value if dense is None else dense + value
        if slope is not None:
            more = moment(step - 1, slope)
            total = more if total is None else total + more
        slope = halves(cube)
        square = following
    more = moment(steps - 1, slope)
    total = more if total is None else total + more
    return dense, total


def local_first_kernel(own_ref, near_ref, moment_ref, mass_ref, *refs):
    out_ref, dense_ref = refs[-2:]
    own = own_ref[...]
    mass = mass_ref[...]
    chunk = 2 * LANES

    def mass_of(step):
        column = jnp.concatenate(
            [spread(mass, block) for block in (2 * step, 2 * step + 1)], axis=0
        )
        return jnp.concatenate([column] * (own.shape[1] // LANES), axis=1)

    dense, total = pair_sums(own, near_ref, moment_ref, mass_of, chunk)
    out_ref[...] = fold_rows(total, 8)
    dense_ref[...] = dense


def local_second_kernel(own_ref, near_ref, moment_ref, *refs):
    out_ref = refs[-1]
    own = own_ref[...]
    _, total = pair_sums(own, near_ref, moment_ref, None, 2 * LANES)
    blank = jnp.zeros((4, own.shape[1]), f32)
    out_ref[...] = jnp.concatenate([fold_rows(total, 4), blank], axis=0)


def diagonal(own):
    blank = jnp.zeros((FEATS, LANES), bf16)
    upper = jnp.concatenate([own[:, 0:LANES], blank], axis=1)
    lower = jnp.concatenate([blank, own[:, LANES:]], axis=1)
    return jnp.concatenate([upper, lower], axis=0)


def slot_place(slot, tables_ref, place_ref, me, capacity, blocks, extra):
    sender = slot // capacity
    apart = sender ^ me
    first = place_ref[0, apart]
    second = place_ref[1, apart]
    block = tables_ref[first, (me // 8 * capacity) % LANES + slot % capacity]
    half = blocks // 2
    devices = place_ref.shape[1]
    row = jnp.where(
        block < half,
        first * (half + extra) + block,
        devices * (half + extra) + second * half + block - half,
    )
    return row, first * blocks + block


def fetch(pieces, gathered, semaphore):
    start = 0
    copies = []
    for number, piece in enumerate(pieces):
        count = piece.shape[0]
        copy = pltpu.make_async_copy(
            piece, gathered.at[pl.ds(start, count)], semaphore.at[number]
        )
        copy.start()
        copies.append(copy)
        start += count
    return copies


def in_turn(pairs, build, sums):
    build(0, 0)

    @pl.loop(0, pairs // 2)
    def _(step):
        build(step * 2 + 1, 1)
        sums(step * 2, 0)
        build(jnp.minimum(step * 2 + 2, pairs - 1), 0)
        sums(step * 2 + 1, 1)


def own_tables(gathered, line_ref, tables_ref, semaphore, place, me, capacity):
    step, half, extra = place
    line = me // 8 * capacity // LANES
    devices = line_ref.shape[0]
    chosen = lax.broadcasted_iota(jnp.int32, (8, LANES), 0) == me % 8
    for device in range(devices):
        block = gathered[device * step + half + line]
        row = jnp.sum(jnp.where(chosen, block, 0.0), axis=0, keepdims=True)
        line_ref[device : device + 1, :] = row.astype(jnp.int32)
    copy = pltpu.make_async_copy(line_ref, tables_ref, semaphore)
    copy.start()
    copy.wait()


def remote_first_kernel(
    capacity,
    extra,
    place_ref,
    me_ref,
    slots_hbm,
    *refs,
):
    pieces, refs = refs[:PIECES], refs[PIECES:]
    own_ref, fields_ref, centre_ref, entropy_ref, moments_ref, dense_ref = refs[:6]
    density_ref, divergence_ref, weight_ref, gradient_ref, line_ref = refs[6:11]
    gathered, tables_ref, near0, near1, moment0, moment1, mass0, mass1 = refs[11:19]
    sums_ref, slots_ref, semaphore, table_semaphore, slots_semaphore = refs[19:]
    blocks = fields_ref.shape[0]
    partners = slots_ref.shape[1]
    copies = fetch((slots_hbm,), slots_ref, slots_semaphore)
    copies += fetch(pieces, gathered, semaphore)
    for copy in copies:
        copy.wait()
    centre = centre_ref[...]
    me = me_ref[0]
    half = blocks // 2
    place = (half + extra, half, extra)
    own_tables(gathered, line_ref, tables_ref, table_semaphore, place, me, capacity)
    sides = ((near0, moment0, mass0), (near1, moment1, mass1))

    def build(pair, side):
        near, moment, mass = sides[side]
        for k in range(partners):
            at = slice(k * LANES, (k + 1) * LANES)
            rows = []
            for odd in range(2):
                row, _ = slot_place(
                    slots_ref[pair * 2 + odd, k],
                    tables_ref, place_ref, me, capacity, blocks, extra,
                )
                values, moments = first_near(gathered[row], centre)
                rows.append(values)
                moment[odd * 32 : odd * 32 + 32, at] = moments
            turned = jnp.concatenate(rows, axis=0).T
            near[at, :] = turned.astype(bf16)
            for odd in range(2):
                mass[at, odd * LANES : (odd + 1) * LANES] = spread(turned, odd * FEATS + MASS_ROW)

    def sums(pair, side):
        near, moment, mass = sides[side]
        at = pl.ds(pl.multiple_of(pair * 2 * LANES, 2 * LANES), 2 * LANES)
        dense, total = pair_sums(
            diagonal(own_ref[:, at]), near, moment, lambda step: mass[pl.ds(step * 256, 256), :], 256
        )
        dense = dense + dense_ref[:, at]
        before = moments_ref[:, at]
        for odd in range(2):
            here = slice(odd * LANES, (odd + 1) * LANES)
            part = fold_rows(total[odd * 32 : odd * 32 + 32, here], 8)
            sums_ref[pair * 2 + odd, 0:8, :] = part + before[:, here]
            sums_ref[pair * 2 + odd, 8:16, :] = dense[:, here]

    in_turn(blocks // 2, build, sums)
    total = sums_ref[:, 8, :]
    for row in range(9, 16):
        total = total + sums_ref[:, row, :]
    moments = [sums_ref[:, row, :] for row in range(8)]
    own = [fields_ref[:, row, :] - centre[row : row + 1, :] for row in range(8)]
    inverse = 1.0 / own[7]
    cube = inverse * inverse * inverse
    density = total * cube * (kernel_norm / 256.0)
    factor = cube * inverse * inverse * (20.0 * kernel_norm / 64.0)
    cross = own[0] * own[3] + own[1] * own[4] + own[2] * own[5]
    approach = cross * moments[6] + moments[7]
    for row in range(3):
        approach = approach - own[row + 3] * moments[row] - own[row] * moments[row + 3]
    press = entropy_ref[...] * inverse_cube_root(density)
    density_ref[...] = density
    divergence_ref[...] = factor * approach / density
    weight_ref[...] = (20.0 * kernel_norm) * own[6] * press * (cube * inverse * inverse)
    for row in range(3):
        gradient = (own[row] * moments[6] - moments[row]) * (factor * press)
        gradient_ref[row] = gradient


def inverse_cube_root(value):
    guess = jnp.exp(jnp.log(value) * (-1.0 / 3.0))
    guess = guess * (4.0 - value * guess * guess * guess) * (1.0 / 3.0)
    return guess * (4.0 - value * guess * guess * guess) * (1.0 / 3.0)


def prepare_second_kernel(fields_ref, centre_ref, weight_ref, near_ref, moment_ref, own_ref):
    blocks = fields_ref.shape[0]
    centre = centre_ref[...]

    @pl.loop(0, blocks // 4)
    def _(group):
        for part in range(4):
            index = group * 4 + part
            at = pl.ds(pl.multiple_of(index * LANES, LANES), LANES)
            near, moment_ref[:, at] = second_near(
                fields_ref[index], centre, weight_ref[pl.ds(index, 1), :]
            )
            near_ref[at, :] = near.T.astype(bf16)
            pos, _, square = particle_rows(fields_ref[index], centre)
            four = jnp.concatenate([pos * -2.0, square], axis=0)
            own_ref[:, at] = own_rows(four, [jnp.ones_like(square)] * 3)


def remote_second_kernel(
    capacity,
    extra,
    tables_ref,
    place_ref,
    me_ref,
    active_ref,
    slots_hbm,
    *refs,
):
    pieces, weight_pieces, refs = refs[:PIECES], refs[PIECES : PIECES + 4], refs[PIECES + 4 :]
    own_ref, fields_ref, centre_ref, moments_ref, gradient_ref, out_ref = refs[:6]
    gathered, weights, near0, near1, moment0, moment1 = refs[6:12]
    slots_ref, semaphore, weight_semaphore, slots_semaphore = refs[12:]
    blocks = fields_ref.shape[0]
    partners = slots_ref.shape[1]
    copies = fetch((slots_hbm,), slots_ref, slots_semaphore)
    copies += fetch(pieces, gathered, semaphore)
    copies += fetch(weight_pieces, weights, weight_semaphore)
    for copy in copies:
        copy.wait()
    centre = centre_ref[...]
    me = me_ref[0]
    sides = ((near0, moment0), (near1, moment1))

    def build(pair, side):
        near, moment = sides[side]
        for k in range(partners):
            at = slice(k * LANES, (k + 1) * LANES)
            rows = []
            for odd in range(2):
                row, weight_row = slot_place(
                    slots_ref[pair * 2 + odd, k],
                    tables_ref, place_ref, me, capacity, blocks, extra,
                )
                values, moments = second_near(
                    gathered[row], centre, weights[pl.ds(weight_row, 1), :]
                )
                rows.append(values)
                moment[odd * 16 : odd * 16 + 16, at] = moments
            near[at, :] = jnp.concatenate(rows, axis=0).T.astype(bf16)

    def sums(pair, side):
        near, moment = sides[side]
        at = pl.ds(pl.multiple_of(pair * 2 * LANES, 2 * LANES), 2 * LANES)
        _, total = pair_sums(diagonal(own_ref[:, at]), near, moment, None, 256)
        before = moments_ref[0:4, at]
        for odd in range(2):
            index = pair * 2 + odd
            here = slice(odd * LANES, (odd + 1) * LANES)
            part = fold_rows(total[odd * 16 : odd * 16 + 16, here], 4) + before[:, here]
            pos, _, _ = particle_rows(fields_ref[index], centre)
            out = gradient_ref[:, index, :] + (pos * part[3:4] - part[0:3])
            out_ref[index] = jnp.where(active_ref[index] > 0, out, 0.0)

    in_turn(blocks // 2, build, sums)


def join_kernel(*refs):
    count = (len(refs) - 1) // 3
    copies = []
    for number in range(count):
        out = refs[2 * count + number]
        start = 0
        for part in range(2):
            piece = refs[2 * number + part]
            copy = pltpu.make_async_copy(
                piece, out.at[pl.ds(start, piece.shape[0])], refs[-1].at[2 * number + part]
            )
            copy.start()
            copies.append(copy)
            start += piece.shape[0]
    for copy in copies:
        copy.wait()


def in_vmem(count):
    return [pl.BlockSpec(memory_space=pltpu.VMEM)] * count


def in_smem(count):
    return [pl.BlockSpec(memory_space=pltpu.SMEM)] * count


def in_any(count):
    return [pl.BlockSpec(memory_space=pl.ANY)] * count


def shape(*dims, dtype=f32):
    return jax.ShapeDtypeStruct(dims, dtype)


def room(mebibytes):
    return pltpu.CompilerParams(vmem_limit_bytes=mebibytes * 2**20)


def join(*pairs):
    flat = [item for pair in pairs for item in pair]
    outs = [shape(2 * pair[0].shape[0], *pair[0].shape[1:]) for pair in pairs]
    return pl.pallas_call(
        join_kernel,
        out_shape=outs,
        in_specs=in_any(len(flat)),
        out_specs=in_any(len(outs)),
        scratch_shapes=[pltpu.SemaphoreType.DMA((len(flat),))],
        compiler_params=room(4),
    )(*flat)


def assemble(extra, *arrays):
    blocks = arrays[0].shape[0]
    half = blocks // 2
    return pl.pallas_call(
        assemble_kernel,
        out_shape=[
            shape(blocks, 8, LANES),
            shape(half + extra, 8, LANES),
            shape(blocks - half, 8, LANES),
        ],
        in_specs=in_any(5),
        out_specs=in_vmem(3),
        scratch_shapes=[pltpu.VMEM(item.shape, item.dtype) for item in arrays]
        + [pltpu.SemaphoreType.DMA((5,))],
        compiler_params=room(8),
    )(*arrays)


def prepare(fields):
    particles = fields.shape[0] * LANES
    return pl.pallas_call(
        prepare_kernel,
        out_shape=[
            shape(particles, FEATS, dtype=bf16),
            shape(32, particles, dtype=bf16),
            shape(LANES, fields.shape[0]),
            shape(FEATS, particles, dtype=bf16),
            shape(8, LANES),
        ],
        in_specs=in_vmem(1),
        out_specs=in_vmem(5),
        compiler_params=room(16),
    )(fields)


def prepare_second(fields, centre, weight):
    particles = fields.shape[0] * LANES
    return pl.pallas_call(
        prepare_second_kernel,
        out_shape=[
            shape(particles, FEATS, dtype=bf16),
            shape(16, particles, dtype=bf16),
            shape(FEATS, particles, dtype=bf16),
        ],
        in_specs=in_vmem(3),
        out_specs=in_vmem(3),
        compiler_params=room(16),
    )(fields, centre, weight)


def local_pass(kernel, first, count, own, whole, sums):
    particles = own.shape[1]
    here = lambda index: (0, first + index)
    height = 2 if kernel is local_first_kernel else 1
    outs = [shape(8, particles)] * height
    aliases = {}
    operands = [own, *whole]
    in_specs = [pl.BlockSpec((FEATS, TILE), here)]
    in_specs += in_vmem(len(whole))
    if sums is not None:
        aliases = {len(operands) + number: number for number in range(height)}
        operands += list(sums)
        in_specs += in_any(height)
    return pl.pallas_call(
        kernel,
        grid=(count,),
        in_specs=in_specs,
        out_specs=[pl.BlockSpec((8, TILE), here)] * height,
        out_shape=outs,
        input_output_aliases=aliases,
        cost_estimate=pl.CostEstimate(
            flops=count * TILE * particles * 2000, bytes_accessed=2**20, transcendentals=0
        ),
        compiler_params=room(24),
    )(*operands)


def swap(value, bit, devices):
    return lax.ppermute(value, "dom", [(i, i ^ bit) for i in range(devices)])


def places(order, devices):
    table = np.zeros((devices,), np.int32)
    for apart in range(devices):
        table[apart] = sum(1 << k for k, bit in enumerate(order) if apart & bit)
    return table


def shares(tiles, stages):
    weights = [3] + [2] * (stages - 4) + [3, 5, 3]
    cuts = [round(tiles * sum(weights[:k]) / sum(weights)) for k in range(stages + 1)]
    return list(zip(cuts[:-1], cuts[1:]))


def per_device(
    devices,
    positions,
    velocities,
    masses,
    smoothing,
    entropy,
    export_blocks,
    partner_slots,
    active,
):
    blocks = positions.shape[0]
    particles = blocks * LANES
    capacity = export_blocks.shape[2]
    half = blocks // 2
    me = lax.axis_index("dom")
    extra = -(-devices * capacity // (8 * LANES))
    fields, first, second = assemble(
        extra, positions, velocities, masses, smoothing, export_blocks
    )
    bits = [1 << k for k in reversed(range(devices.bit_length() - 1))]
    order0 = list(bits)
    order1 = list(bits)
    order1[-3:-1] = reversed(order1[-3:-1])
    place = jnp.asarray(np.stack([places(order0, devices), places(order1, devices)]))
    tiles = particles // TILE
    stages = len(bits)

    near, moment, mass, own, centre = prepare(fields)
    sums = None
    first, second = [first], [second]
    for number, (start, stop) in enumerate(shares(tiles, stages)):
        first_in = [swap(item, order0[number], devices) for item in first]
        second_in = [swap(item, order1[number], devices) for item in second]
        if stop > start:
            sums = local_pass(
                local_first_kernel, start, stop - start, own, (near, moment, mass), sums
            )
        first += first_in
        second += second_in
        if number < stages - 1:
            first, second, near, sums = lax.optimization_barrier((first, second, near, sums))
        if number < stages - 2:
            first, second = join(first, second)
            first, second = [first], [second]
    pieces = (*first, *second)

    me_array = me.astype(jnp.int32).reshape(1)

    rows = sum(piece.shape[0] for piece in pieces)
    partners = partner_slots.shape[1] * LANES
    near_side = [pltpu.VMEM((partners, 2 * FEATS), bf16)] * 2
    density, divergence, weight, gradient, tables = pl.pallas_call(
        functools.partial(remote_first_kernel, capacity, extra),
        out_shape=[
            shape(blocks, LANES),
            shape(blocks, LANES),
            shape(blocks, LANES),
            shape(3, blocks, LANES),
            shape(devices, LANES, dtype=jnp.int32),
        ],
        in_specs=in_smem(2) + in_any(1 + PIECES) + in_vmem(6),
        out_specs=in_vmem(5),
        scratch_shapes=[
            pltpu.VMEM((rows, 8, LANES), f32),
            pltpu.SMEM((devices, LANES), jnp.int32),
            *near_side,
            pltpu.VMEM((64, partners), bf16),
            pltpu.VMEM((64, partners), bf16),
            pltpu.VMEM((partners, 2 * LANES), f32),
            pltpu.VMEM((partners, 2 * LANES), f32),
            pltpu.VMEM((blocks, 16, LANES), f32),
            pltpu.SMEM(partner_slots.shape, jnp.int32),
            pltpu.SemaphoreType.DMA((PIECES,)),
            pltpu.SemaphoreType.DMA,
            pltpu.SemaphoreType.DMA((1,)),
        ],
        compiler_params=room(20 + rows // 256),
    )(place, me_array, partner_slots, *pieces, own, fields, centre, entropy, *sums)

    near2, moment2, own2 = prepare_second(fields, centre, weight)
    sums = None
    weights = [weight]
    for number, (start, stop) in enumerate(shares(tiles, stages)):
        weights += [swap(item, order0[number], devices) for item in weights]
        if stop > start:
            sums = local_pass(
                local_second_kernel, start, stop - start, own2, (near2, moment2), sums
            )
        if number < stages - 1:
            weights, near2, sums = lax.optimization_barrier((weights, near2, sums))
        if number < stages - 2:
            weights = list(join(weights))

    acceleration = pl.pallas_call(
        functools.partial(remote_second_kernel, capacity, extra),
        out_shape=shape(blocks, 3, LANES),
        in_specs=in_smem(4) + in_any(5 + PIECES) + in_vmem(5),
        out_specs=pl.BlockSpec(memory_space=pltpu.VMEM),
        scratch_shapes=[
            pltpu.VMEM((rows, 8, LANES), f32),
            pltpu.VMEM((devices * blocks, LANES), f32),
            *near_side,
            pltpu.VMEM((32, partners), bf16),
            pltpu.VMEM((32, partners), bf16),
            pltpu.SMEM(partner_slots.shape, jnp.int32),
            pltpu.SemaphoreType.DMA((PIECES,)),
            pltpu.SemaphoreType.DMA((4,)),
            pltpu.SemaphoreType.DMA((1,)),
        ],
        compiler_params=room(20 + rows // 256),
    )(
        tables, place, me_array, active, partner_slots, *pieces, *weights, own2,
        fields, centre, *sums, gradient,
    )
    return (density, divergence, acceleration)


def solution(mesh):
    in_specs = (
        P("dom", None, None),
        P("dom", None, None),
        P("dom", None),
        P("dom", None),
        P("dom", None),
        P("dom", None, None),
        P("dom", None),
        P("dom"),
    )
    out_specs = (P("dom", None), P("dom", None), P("dom", None, None))
    return jax.shard_map(
        functools.partial(per_device, mesh.shape["dom"]),
        mesh=mesh,
        in_specs=in_specs,
        out_specs=out_specs,
        check_vma=False,
    )
```

time: 170 us -> 151 us (0.89)
  Pallas kernels: 136 us -> 125 us
  local copies, waits for them, and re-layouts: 10.3 us -> 3.61 us
  waiting for transfers between devices: 3.81 us -> 1.01 us
  starting transfers between devices: 17 us -> 19.5 us
    unnamed x38 -> x20, local copies, waits for them, and re-layouts: 10.2 us -> 3.61 us
    pallas_call x1, Pallas kernels: 35.1 us -> 29.3 us  [per_device(): pl.pallas_call(functools.partial(remote_first_kernel, capacity, extra), o...]
    pallas_call x1, Pallas kernels: 26.2 us -> 22.2 us  [per_device(): pl.pallas_call(functools.partial(remote_second_kernel, capacity, extra),...]
    ppermute x15 -> x18, waiting for transfers between devices: 3.81 us -> 1.01 us  [swap(): return lax.ppermute(value, 'dom', [(i, i ^ bit) for i in range(devices)])]
    ppermute x15 -> x18, starting transfers between devices: 17 us -> 19.5 us  [swap(): return lax.ppermute(value, 'dom', [(i, i ^ bit) for i in range(devices)])]
  transfers between devices with their start and end apart: 15 -> 18, of which waited for: 2 -> 1; matrix products, arithmetic and copies ran while one was open for 0% -> 0% of each run, Pallas kernels for 42% -> 48%
where the time goes in v3:
time: 151 us; the launch traced here: 150 us
  Pallas kernels  125 us (83%)
  starting transfers between devices  19.5 us (13%)
  local copies, waits for them, and re-layouts  3.61 us (2%)
    pallas_call x10, Pallas kernels, local_pass(): pl.pallas_call(kernel, grid=(count,), in_specs=in_specs, out_specs=[pl.Bl...  69.4 us
    pallas_call x1, Pallas kernels, per_device(): pl.pallas_call(functools.partial(remote_first_kernel, capacity, extra), o...  29.3 us
    pallas_call x1, Pallas kernels, per_device(): pl.pallas_call(functools.partial(remote_second_kernel, capacity, extra),...  22.2 us
    ppermute x18, starting transfers between devices, swap(): return lax.ppermute(value, 'dom', [(i, i ^ bit) for i in range(devices)])  19.5 us
    unnamed x20, local copies, waits for them, and re-layouts  3.61 us
  transfers between devices with their start and end apart: 18, of which 1 were waited for; matrix products, arithmetic and copies ran while one was open for 0% of the time, Pallas kernels for 48%

profile of v3, /device:TPU:0, one launch (start us, length us, event | category | flops | bytes accessed | tf_op | source)
XLA Modules:
  0.0 150.3 jit_solution(3986976739721586630)
XLA Ops:
  0.6 0.8 copy.24.refs_0_
  1.5 0.0 copy-start.1
  1.5 0.0 copy-start.2
  1.5 0.0 copy-start.3
  1.6 0.6 copy-done.1
  2.2 0.0 copy-done.2
  2.2 0.0 copy-done.3
  2.3 0.2 shard_map.112
  2.5 4.1 %collective-permute-start.1 = (f32[16,8,128]{2,1,0:T(8,128)S(1)}, f32[16,8,128]{2,1,0:T(8,128)S(1)}, u32[]{:S(2)}, u32[]{:S(2)}) collective-permute-start(f32[16,8,128]{2,1,0:T(8,128)S(1)} %get-tuple-element.90.refs_2_), channel_id=1, source_target_pairs={{0,16},{1,17},{2,18},{3,19},{4,20},{5,21},{6,22},{7,23},{8,24},{9,... | collective-permute-start | bytes 196616 | tf_op jit(solution)/shard_map/ppermute | solution.py:572
  6.6 0.1 collective-permute-start
  6.7 1.3 shard_map.113
  8.0 0.0 copy-start.7
  8.0 7.6 %shard_map.114 = (f32[8,4096]{1,0:T(8,128)S(1)}, f32[8,4096]{1,0:T(8,128)S(1)}) custom-call(bf16[48,4096]{1,0:T(8,128)(2,1)S(1)} %get-tuple-element.83.own_ref.refs_8_, bf16[4096,48]{1,0:T(8,128)(2,1)S(1)} %get-tuple-element.126.near_ref, bf16[32,4096]{1,0:T(8,128)(2,1)S(1)} %get-tuple-element.84.moment_ref, f32[128,32]{1,0:T(8,128)S(1)} %get-tuple-element.85.mass_ref), custom_call_target="tpu_custom_call" | custom-call | flops 6291456000 | bytes 1048576 | tf_op jit(solution)/shard_map/pallas_call | solution.py:557
  15.6 0.1 copy.26.slots_hbm
  15.7 0.0 collective-permute-done.1.refs_3_
  15.7 0.0 collective-permute-done.refs_1_
  15.7 0.4 shard_map.115
  16.1 1.9 %collective-permute-start.3 = (f32[32,8,128]{2,1,0:T(8,128)S(1)}, f32[32,8,128]{2,1,0:T(8,128)S(1)}, u32[]{:S(2)}, u32[]{:S(2)}) collective-permute-start(f32[32,8,128]{2,1,0:T(8,128)S(1)} %get-tuple-element.101.refs_2_), channel_id=1, source_target_pairs={{0,8},{1,9},{2,10},{3,11},{4,12},{5,13},{6,14},{7,15},{8,0},{9,1},... | collective-permute-start | bytes 393224 | tf_op jit(solution)/shard_map/ppermute | solution.py:572
  18.0 0.2 collective-permute-start.2
  18.2 5.1 %shard_map.116 = (f32[8,4096]{1,0:T(8,128)S(1)}, f32[8,4096]{1,0:T(8,128)S(1)}) custom-call(bf16[48,4096]{1,0:T(8,128)(2,1)S(1)} %get-tuple-element.83.own_ref.refs_8_, bf16[4096,48]{1,0:T(8,128)(2,1)S(1)} %get-tuple-element.126.near_ref, bf16[32,4096]{1,0:T(8,128)(2,1)S(1)} %get-tuple-element.84.moment_ref, ...), custom_call_target="tpu_custom_call", output_to_operand_aliasing={{0}: (4, {}), {1}: (5, {})} | custom-call | flops 4194304000 | bytes 1048576 | tf_op jit(solution)/shard_map/pallas_call | solution.py:557
  23.3 0.9 collective-permute-done.2.refs_1_
  24.2 0.7 shard_map.117
  24.9 1.6 %collective-permute-start.5 = (f32[64,8,128]{2,1,0:T(8,128)S(1)}, f32[64,8,128]{2,1,0:T(8,128)S(1)}, u32[]{:S(2)}, u32[]{:S(2)}) collective-permute-start(f32[64,8,128]{2,1,0:T(8,128)S(1)} %get-tuple-element.112.refs_2_), channel_id=1, source_target_pairs={{0,2},{1,3},{2,0},{3,1},{4,6},{5,7},{6,4},{7,5},{8,10},{9,11},{10,... | collective-permute-start | bytes 786440 | tf_op jit(solution)/shard_map/ppermute | solution.py:572
  26.4 1.5 %collective-permute-start.4 = (f32[68,8,128]{2,1,0:T(8,128)S(1)}, f32[68,8,128]{2,1,0:T(8,128)S(1)}, u32[]{:S(2)}, u32[]{:S(2)}) collective-permute-start(f32[68,8,128]{2,1,0:T(8,128)S(1)} %get-tuple-element.110.refs_0_), channel_id=1, source_target_pairs={{0,4},{1,5},{2,6},{3,7},{4,0},{5,1},{6,2},{7,3},{8,12},{9,13},{10,... | collective-permute-start | bytes 835592 | tf_op jit(solution)/shard_map/ppermute | solution.py:572
  27.9 7.6 %shard_map.118 = (f32[8,4096]{1,0:T(8,128)S(1)}, f32[8,4096]{1,0:T(8,128)S(1)}) custom-call(bf16[48,4096]{1,0:T(8,128)(2,1)S(1)} %get-tuple-element.83.own_ref.refs_8_, bf16[4096,48]{1,0:T(8,128)(2,1)S(1)} %get-tuple-element.126.near_ref, bf16[32,4096]{1,0:T(8,128)(2,1)S(1)} %get-tuple-element.84.moment_ref, ...), custom_call_target="tpu_custom_call", output_to_operand_aliasing={{0}: (4, {}), {1}: (5, {})} | custom-call | flops 6291456000 | bytes 1048576 | tf_op jit(solution)/shard_map/pallas_call | solution.py:557
  35.5 0.0 collective-permute-done.4.refs_1_
  35.6 0.2 shard_map.119
  35.7 0.6 collective-permute-start.7
  36.3 0.5 collective-permute-start.6
  36.8 12.7 %shard_map.120 = (f32[8,4096]{1,0:T(8,128)S(1)}, f32[8,4096]{1,0:T(8,128)S(1)}) custom-call(bf16[48,4096]{1,0:T(8,128)(2,1)S(1)} %get-tuple-element.83.own_ref.refs_8_, bf16[4096,48]{1,0:T(8,128)(2,1)S(1)} %get-tuple-element.126.near_ref, bf16[32,4096]{1,0:T(8,128)(2,1)S(1)} %get-tuple-element.84.moment_ref, ...), custom_call_target="tpu_custom_call", output_to_operand_aliasing={{0}: (4, {}), {1}: (5, {})} | custom-call | flops 10485760000 | bytes 1048576 | tf_op jit(solution)/shard_map/pallas_call | solution.py:557
  49.5 0.0 collective-permute-done.6.refs_1_
  49.5 0.1 collective-permute-start.10
  49.6 0.5 collective-permute-start.11
  50.1 0.1 collective-permute-start.8
  50.2 0.4 collective-permute-start.9
  50.6 7.6 %shard_map.121 = (f32[8,4096]{1,0:T(8,128)S(1)}, f32[8,4096]{1,0:T(8,128)S(1)}) custom-call(bf16[48,4096]{1,0:T(8,128)(2,1)S(1)} %get-tuple-element.83.own_ref.refs_8_, bf16[4096,48]{1,0:T(8,128)(2,1)S(1)} %get-tuple-element.126.near_ref, bf16[32,4096]{1,0:T(8,128)(2,1)S(1)} %get-tuple-element.84.moment_ref, ...), custom_call_target="tpu_custom_call", output_to_operand_aliasing={{0}: (4, {}), {1}: (5, {})} | custom-call | flops 6291456000 | bytes 1048576 | tf_op jit(solution)/shard_map/pallas_call | solution.py:557
  58.2 0.0 collective-permute-done.11.refs_7_
  58.3 0.0 copy-start.4
  58.3 0.7 copy-done.4
  58.9 29.3 %shard_map.122 = (f32[32,128]{1,0:T(8,128)}, f32[32,128]{1,0:T(8,128)}, f32[32,128]{1,0:T(8,128)S(1)}, f32[3,32,128]{2,1,0:T(8,128)S(1)}, s32[32,128]{1,0:T(8,128)S(1)}) custom-call(s32[2,32]{1,0:T(2,128)S(1)} %copy-done.4, s32[1]{0:T(128)} %bitcast.me_ref, s32[32,16]{1,0:T(8,128)S(1)} %copy.26.slots_hbm, f32[136,8,128]{2,1,0:T(8,128)S(1)} %get-tuple-element.121.refs_0_, ...), custom_call_target="tpu_custom_call" | custom-call | tf_op jit(solution)/shard_map/pallas_call | solution.py:640
  88.3 2.6 %collective-permute-start.12 = (f32[32,128]{1,0:T(8,128)S(1)}, f32[32,128]{1,0:T(8,128)S(1)}, u32[]{:S(2)}, u32[]{:S(2)}) collective-permute-start(f32[32,128]{1,0:T(8,128)S(1)} %get-tuple-element.138.weight_ref.refs_0_), channel_id=1, source_target_pairs={{0,16},{1,17},{2,18},{3,19},{4,20},{5,21},{6,22},{7,23},{8,24},{9,... | collective-permute-start | bytes 49160 | tf_op jit(solution)/shard_map/ppermute | solution.py:572
  90.9 1.2 shard_map.123
  92.1 5.4 %shard_map.124.refs_0_ = f32[8,4096]{1,0:T(8,128)S(1)} custom-call(bf16[48,4096]{1,0:T(8,128)(2,1)S(1)} %get-tuple-element.136.own_ref.refs_12_, bf16[4096,48]{1,0:T(8,128)(2,1)S(1)} %get-tuple-element.152.near_ref, bf16[16,4096]{1,0:T(8,128)(2,1)S(1)} %get-tuple-element.137.moment_ref), custom_call_target="tpu_custom_call" | custom-call | flops 6291456000 | bytes 1048576 | tf_op jit(solution)/shard_map/pallas_call | solution.py:557
  97.5 0.0 collective-permute-done.12.refs_1_
  97.5 0.1 shard_map.125.refs_0_
  97.6 1.6 %collective-permute-start.13 = (f32[64,128]{1,0:T(8,128)S(1)}, f32[64,128]{1,0:T(8,128)S(1)}, u32[]{:S(2)}, u32[]{:S(2)}) collective-permute-start(f32[64,128]{1,0:T(8,128)S(1)} %shard_map.125.refs_0_), channel_id=1, source_target_pairs={{0,8},{1,9},{2,10},{3,11},{4,12},{5,13},{6,14},{7,15},{8,0},{9,1},... | collective-permute-start | bytes 98312 | tf_op jit(solution)/shard_map/ppermute | solution.py:572
  99.2 3.6 %shard_map.126.refs_0_ = f32[8,4096]{1,0:T(8,128)S(1)} custom-call(bf16[48,4096]{1,0:T(8,128)(2,1)S(1)} %get-tuple-element.136.own_ref.refs_12_, bf16[4096,48]{1,0:T(8,128)(2,1)S(1)} %get-tuple-element.152.near_ref, bf16[16,4096]{1,0:T(8,128)(2,1)S(1)} %get-tuple-element.137.moment_ref, f32[8,4096]{1,0:T(8,128)S(1)} %shard_map.124.refs_0_), custom_call_target="tpu_custom_call", output_to_operand_aliasing={{}: (3, {})} | custom-call | flops 4194304000 | bytes 1048576 | tf_op jit(solution)/shard_map/pallas_call | solution.py:557
  102.8 0.0 collective-permute-done.13.refs_1_
  102.9 0.1 shard_map.127.refs_0_
  103.0 1.6 %collective-permute-start.14 = (f32[128,128]{1,0:T(8,128)S(1)}, f32[128,128]{1,0:T(8,128)S(1)}, u32[]{:S(2)}, u32[]{:S(2)}) collective-permute-start(f32[128,128]{1,0:T(8,128)S(1)} %shard_map.127.refs_0_), channel_id=1, source_target_pairs={{0,4},{1,5},{2,6},{3,7},{4,0},{5,1},{6,2},{7,3},{8,12},{9,13},{10,... | collective-permute-start | bytes 196616 | tf_op jit(solution)/shard_map/ppermute | solution.py:572
  104.6 5.4 %shard_map.128.refs_0_ = f32[8,4096]{1,0:T(8,128)S(1)} custom-call(bf16[48,4096]{1,0:T(8,128)(2,1)S(1)} %get-tuple-element.136.own_ref.refs_12_, bf16[4096,48]{1,0:T(8,128)(2,1)S(1)} %get-tuple-element.152.near_ref, bf16[16,4096]{1,0:T(8,128)(2,1)S(1)} %get-tuple-element.137.moment_ref, f32[8,4096]{1,0:T(8,128)S(1)} %shard_map.126.refs_0_), custom_call_target="tpu_custom_call", output_to_operand_aliasing={{}: (3, {})} | custom-call | flops 6291456000 | bytes 1048576 | tf_op jit(solution)/shard_map/pallas_call | solution.py:557
  110.0 0.0 collective-permute-done.14.refs_1_
  110.0 0.2 shard_map.129.refs_8_
  110.2 1.6 %collective-permute-start.15 = (f32[256,128]{1,0:T(8,128)S(1)}, f32[256,128]{1,0:T(8,128)S(1)}, u32[]{:S(2)}, u32[]{:S(2)}) collective-permute-start(f32[256,128]{1,0:T(8,128)S(1)} %shard_map.129.refs_8_), channel_id=1, source_target_pairs={{0,2},{1,3},{2,0},{3,1},{4,6},{5,7},{6,4},{7,5},{8,10},{9,11},{10,... | collective-permute-start | bytes 393224 | tf_op jit(solution)/shard_map/ppermute | solution.py:572
  111.8 9.0 %shard_map.130.refs_0_ = f32[8,4096]{1,0:T(8,128)S(1)} custom-call(bf16[48,4096]{1,0:T(8,128)(2,1)S(1)} %get-tuple-element.136.own_ref.refs_12_, bf16[4096,48]{1,0:T(8,128)(2,1)S(1)} %get-tuple-element.152.near_ref, bf16[16,4096]{1,0:T(8,128)(2,1)S(1)} %get-tuple-element.137.moment_ref, f32[8,4096]{1,0:T(8,128)S(1)} %shard_map.128.refs_0_), custom_call_target="tpu_custom_call", output_to_operand_aliasing={{}: (3, {})} | custom-call | flops 10485760000 | bytes 1048576 | tf_op jit(solution)/shard_map/pallas_call | solution.py:557
  120.8 0.0 collective-permute-done.15.refs_9_
  120.8 0.1 collective-permute-start.16
  120.9 0.5 collective-permute-start.17
  121.4 5.4 %shard_map.131.refs_15_ = f32[8,4096]{1,0:T(8,128)S(1)} custom-call(bf16[48,4096]{1,0:T(8,128)(2,1)S(1)} %get-tuple-element.136.own_ref.refs_12_, bf16[4096,48]{1,0:T(8,128)(2,1)S(1)} %get-tuple-element.152.near_ref, bf16[16,4096]{1,0:T(8,128)(2,1)S(1)} %get-tuple-element.137.moment_ref, ...), custom_call_target="tpu_custom_call", output_to_operand_aliasing={{}: (3, {})} | custom-call | flops 6291456000 | bytes 1048576 | tf_op jit(solution)/shard_map/pallas_call | solution.py:557
  126.8 0.0 collective-permute-done.16.refs_10_
  126.8 0.0 copy-start.5
  126.9 0.6 copy-done.5
  127.5 22.2 %shard_map.132 = f32[32,3,128]{2,1,0:T(4,128)S(1)} custom-call(s32[32,128]{1,0:T(8,128)S(1)} %get-tuple-element.133.tables_ref, s32[2,32]{1,0:T(2,128)S(1)} %copy-done.4, s32[1]{0:T(128)} %bitcast.me_ref, s32[32]{0:T(128)S(1)} %copy-done.5, s32[32,16]{1,0:T(8,128)S(1)} %copy.26.slots_hbm, f32[136,8,128]{2,1,0:T(8,128)S(1)} %get-tuple-element.121.refs_0_, ...), custom_call_target="tpu_custom_call" | custom-call | tf_op jit(solution)/shard_map/pallas_call | solution.py:682
  149.7 0.6 copy.28
  (13 shorter events, 0.1 us)
Async XLA Ops:
  0.6 0.9 copy-start.6
  1.5 0.7 copy-start.1
  1.5 0.7 copy-start.2
  1.5 0.7 copy-start.3
  2.5 13.2 %collective-permute-start.1 = (f32[16,8,128]{2,1,0:T(8,128)S(1)}, f32[16,8,128]{2,1,0:T(8,128)S(1)}, u32[]{:S(2)}, u32[]{:S(2)}) collective-permute-start(f32[16,8,128]{2,1,0:T(8,128)S(1)} %get-tuple-element.90.refs_2_), channel_id=1, source_target_pairs={{0,16},{1,17},{2,18},{3,19},{4,20},{5,21},{6,22},{7,23},{8,24},{9,... | collective-permute-start | bytes 196616 | tf_op jit(solution)/shard_map/ppermute | solution.py:572
  6.6 9.1 %collective-permute-start = (f32[17,8,128]{2,1,0:T(8,128)S(1)}, f32[17,8,128]{2,1,0:T(8,128)S(1)}, u32[]{:S(2)}, u32[]{:S(2)}) collective-permute-start(f32[17,8,128]{2,1,0:T(8,128)S(1)} %get-tuple-element.88.refs_0_), channel_id=1, source_target_pairs={{0,16},{1,17},{2,18},{3,19},{4,20},{5,21},{6,22},{7,23},{8,24},{9,... | collective-permute-start | bytes 208904 | tf_op jit(solution)/shard_map/ppermute | solution.py:572
  8.0 7.6 %copy-start.7 = (s32[32,16]{0,1:T(8,128)S(1)}, s32[32,16]{0,1:T(8,128)}, u32[]{:S(2)}) copy-start(s32[32,16]{0,1:T(8,128)} %param.15) | copy-start | bytes 6148
  16.1 7.1 %collective-permute-start.3 = (f32[32,8,128]{2,1,0:T(8,128)S(1)}, f32[32,8,128]{2,1,0:T(8,128)S(1)}, u32[]{:S(2)}, u32[]{:S(2)}) collective-permute-start(f32[32,8,128]{2,1,0:T(8,128)S(1)} %get-tuple-element.101.refs_2_), channel_id=1, source_target_pairs={{0,8},{1,9},{2,10},{3,11},{4,12},{5,13},{6,14},{7,15},{8,0},{9,1},... | collective-permute-start | bytes 393224 | tf_op jit(solution)/shard_map/ppermute | solution.py:572
  18.0 6.1 %collective-permute-start.2 = (f32[34,8,128]{2,1,0:T(8,128)S(1)}, f32[34,8,128]{2,1,0:T(8,128)S(1)}, u32[]{:S(2)}, u32[]{:S(2)}) collective-permute-start(f32[34,8,128]{2,1,0:T(8,128)S(1)} %get-tuple-element.99.refs_0_), channel_id=1, source_target_pairs={{0,8},{1,9},{2,10},{3,11},{4,12},{5,13},{6,14},{7,15},{8,0},{9,1},... | collective-permute-start | bytes 417800 | tf_op jit(solution)/shard_map/ppermute | solution.py:572
  24.9 10.7 %collective-permute-start.5 = (f32[64,8,128]{2,1,0:T(8,128)S(1)}, f32[64,8,128]{2,1,0:T(8,128)S(1)}, u32[]{:S(2)}, u32[]{:S(2)}) collective-permute-start(f32[64,8,128]{2,1,0:T(8,128)S(1)} %get-tuple-element.112.refs_2_), channel_id=1, source_target_pairs={{0,2},{1,3},{2,0},{3,1},{4,6},{5,7},{6,4},{7,5},{8,10},{9,11},{10,... | collective-permute-start | bytes 786440 | tf_op jit(solution)/shard_map/ppermute | solution.py:572
  26.4 9.1 %collective-permute-start.4 = (f32[68,8,128]{2,1,0:T(8,128)S(1)}, f32[68,8,128]{2,1,0:T(8,128)S(1)}, u32[]{:S(2)}, u32[]{:S(2)}) collective-permute-start(f32[68,8,128]{2,1,0:T(8,128)S(1)} %get-tuple-element.110.refs_0_), channel_id=1, source_target_pairs={{0,4},{1,5},{2,6},{3,7},{4,0},{5,1},{6,2},{7,3},{8,12},{9,13},{10,... | collective-permute-start | bytes 835592 | tf_op jit(solution)/shard_map/ppermute | solution.py:572
  35.7 13.8 %collective-permute-start.7 = (f32[128,8,128]{2,1,0:T(8,128)S(1)}, f32[128,8,128]{2,1,0:T(8,128)S(1)}, u32[]{:S(2)}, u32[]{:S(2)}) collective-permute-start(f32[128,8,128]{2,1,0:T(8,128)S(1)} %get-tuple-element.123.refs_4_), channel_id=1, source_target_pairs={{0,4},{1,5},{2,6},{3,7},{4,0},{5,1},{6,2},{7,3},{8,12},{9,13},{10,... | collective-permute-start | bytes 1572872 | tf_op jit(solution)/shard_map/ppermute | solution.py:572
  36.3 13.2 %collective-permute-start.6 = (f32[136,8,128]{2,1,0:T(8,128)S(1)}, f32[136,8,128]{2,1,0:T(8,128)S(1)}, u32[]{:S(2)}, u32[]{:S(2)}) collective-permute-start(f32[136,8,128]{2,1,0:T(8,128)S(1)} %get-tuple-element.121.refs_0_), channel_id=1, source_target_pairs={{0,2},{1,3},{2,0},{3,1},{4,6},{5,7},{6,4},{7,5},{8,10},{9,11},{10,... | collective-permute-start | bytes 1671176 | tf_op jit(solution)/shard_map/ppermute | solution.py:572
  49.5 8.7 %collective-permute-start.10 = (f32[128,8,128]{2,1,0:T(8,128)S(1)}, f32[128,8,128]{2,1,0:T(8,128)S(1)}, u32[]{:S(2)}, u32[]{:S(2)}) collective-permute-start(f32[128,8,128]{2,1,0:T(8,128)S(1)} %get-tuple-element.123.refs_4_), channel_id=1, source_target_pairs={{0,1},{1,0},{2,3},{3,2},{4,5},{5,4},{6,7},{7,6},{8,9},{9,8},{10,11... | collective-permute-start | bytes 1572872 | tf_op jit(solution)/shard_map/ppermute | solution.py:572
  49.6 8.6 %collective-permute-start.11 = (f32[128,8,128]{2,1,0:T(8,128)S(1)}, f32[128,8,128]{2,1,0:T(8,128)S(1)}, u32[]{:S(2)}, u32[]{:S(2)}) collective-permute-start(f32[128,8,128]{2,1,0:T(8,128)S(1)} %collective-permute-done.7.refs_5_), channel_id=1, source_target_pairs={{0,1},{1,0},{2,3},{3,2},{4,5},{5,4},{6,7},{7,6},{8,9},{9,8},{10,11... | collective-permute-start | bytes 1572872 | tf_op jit(solution)/shard_map/ppermute | solution.py:572
  50.1 8.1 %collective-permute-start.8 = (f32[136,8,128]{2,1,0:T(8,128)S(1)}, f32[136,8,128]{2,1,0:T(8,128)S(1)}, u32[]{:S(2)}, u32[]{:S(2)}) collective-permute-start(f32[136,8,128]{2,1,0:T(8,128)S(1)} %get-tuple-element.121.refs_0_), channel_id=1, source_target_pairs={{0,1},{1,0},{2,3},{3,2},{4,5},{5,4},{6,7},{7,6},{8,9},{9,8},{10,11... | collective-permute-start | bytes 1671176 | tf_op jit(solution)/shard_map/ppermute | solution.py:572
  50.2 8.1 %collective-permute-start.9 = (f32[136,8,128]{2,1,0:T(8,128)S(1)}, f32[136,8,128]{2,1,0:T(8,128)S(1)}, u32[]{:S(2)}, u32[]{:S(2)}) collective-permute-start(f32[136,8,128]{2,1,0:T(8,128)S(1)} %collective-permute-done.6.refs_1_), channel_id=1, source_target_pairs={{0,1},{1,0},{2,3},{3,2},{4,5},{5,4},{6,7},{7,6},{8,9},{9,8},{10,11... | collective-permute-start | bytes 1671176 | tf_op jit(solution)/shard_map/ppermute | solution.py:572
  50.6 7.7 %copy-start = (f32[32,128]{1,0:T(8,128)S(1)}, f32[32,128]{1,0:T(8,128)}, u32[]{:S(2)}) copy-start(f32[32,128]{1,0:T(8,128)} %refs_11_.1) | copy-start | bytes 49156
  58.3 0.7 copy-start.4
  88.3 9.3 %collective-permute-start.12 = (f32[32,128]{1,0:T(8,128)S(1)}, f32[32,128]{1,0:T(8,128)S(1)}, u32[]{:S(2)}, u32[]{:S(2)}) collective-permute-start(f32[32,128]{1,0:T(8,128)S(1)} %get-tuple-element.138.weight_ref.refs_0_), channel_id=1, source_target_pairs={{0,16},{1,17},{2,18},{3,19},{4,20},{5,21},{6,22},{7,23},{8,24},{9,... | collective-permute-start | bytes 49160 | tf_op jit(solution)/shard_map/ppermute | solution.py:572
  97.6 5.3 %collective-permute-start.13 = (f32[64,128]{1,0:T(8,128)S(1)}, f32[64,128]{1,0:T(8,128)S(1)}, u32[]{:S(2)}, u32[]{:S(2)}) collective-permute-start(f32[64,128]{1,0:T(8,128)S(1)} %shard_map.125.refs_0_), channel_id=1, source_target_pairs={{0,8},{1,9},{2,10},{3,11},{4,12},{5,13},{6,14},{7,15},{8,0},{9,1},... | collective-permute-start | bytes 98312 | tf_op jit(solution)/shard_map/ppermute | solution.py:572
  103.0 7.0 %collective-permute-start.14 = (f32[128,128]{1,0:T(8,128)S(1)}, f32[128,128]{1,0:T(8,128)S(1)}, u32[]{:S(2)}, u32[]{:S(2)}) collective-permute-start(f32[128,128]{1,0:T(8,128)S(1)} %shard_map.127.refs_0_), channel_id=1, source_target_pairs={{0,4},{1,5},{2,6},{3,7},{4,0},{5,1},{6,2},{7,3},{8,12},{9,13},{10,... | collective-permute-start | bytes 196616 | tf_op jit(solution)/shard_map/ppermute | solution.py:572
  110.2 10.6 %collective-permute-start.15 = (f32[256,128]{1,0:T(8,128)S(1)}, f32[256,128]{1,0:T(8,128)S(1)}, u32[]{:S(2)}, u32[]{:S(2)}) collective-permute-start(f32[256,128]{1,0:T(8,128)S(1)} %shard_map.129.refs_8_), channel_id=1, source_target_pairs={{0,2},{1,3},{2,0},{3,1},{4,6},{5,7},{6,4},{7,5},{8,10},{9,11},{10,... | collective-permute-start | bytes 393224 | tf_op jit(solution)/shard_map/ppermute | solution.py:572
  120.8 6.0 %collective-permute-start.16 = (f32[256,128]{1,0:T(8,128)S(1)}, f32[256,128]{1,0:T(8,128)S(1)}, u32[]{:S(2)}, u32[]{:S(2)}) collective-permute-start(f32[256,128]{1,0:T(8,128)S(1)} %shard_map.129.refs_8_), channel_id=1, source_target_pairs={{0,1},{1,0},{2,3},{3,2},{4,5},{5,4},{6,7},{7,6},{8,9},{9,8},{10,11... | collective-permute-start | bytes 393224 | tf_op jit(solution)/shard_map/ppermute | solution.py:572
  120.9 5.9 %collective-permute-start.17 = (f32[256,128]{1,0:T(8,128)S(1)}, f32[256,128]{1,0:T(8,128)S(1)}, u32[]{:S(2)}, u32[]{:S(2)}) collective-permute-start(f32[256,128]{1,0:T(8,128)S(1)} %collective-permute-done.15.refs_9_), channel_id=1, source_target_pairs={{0,1},{1,0},{2,3},{3,2},{4,5},{5,4},{6,7},{7,6},{8,9},{9,8},{10,11... | collective-permute-start | bytes 393224 | tf_op jit(solution)/shard_map/ppermute | solution.py:572
  126.8 0.7 copy-start.5

commit v4 on v3

v4 whole, which is shorter than its diff:
```python
import functools

import jax
import jax.numpy as jnp
import numpy as np
from jax import lax
from jax.experimental import pallas as pl
from jax.experimental.pallas import tpu as pltpu
from jax.sharding import PartitionSpec as P

kernel_norm = 3.3422538049298023
LANES = 128
FEATS = 48
TILE = 256
PIECES = 8
bf16 = jnp.bfloat16
f32 = jnp.float32


def split3(value):
    high = value.astype(bf16).astype(f32)
    rest = value - high
    middle = rest.astype(bf16).astype(f32)
    return high, middle, rest - middle


def near_rows(four, fifth):
    high, middle, low = split3(jnp.concatenate([four, four], axis=0))
    upper = lax.broadcasted_iota(jnp.int32, high.shape, 0) < 4
    mixed = jnp.where(upper, high, middle)
    parts = split3(fifth)
    rows = [high, middle, low, mixed, *parts, *parts, *parts[:2], jnp.zeros((8, LANES), f32)]
    return jnp.concatenate(rows, axis=0).astype(bf16)


def own_rows(four, fifth):
    high, middle, low = split3(four)
    parts = split3(fifth)
    rows = [high, middle] * 3 + [low, low]
    rows += [parts[0]] * 3 + [parts[1]] * 3 + [parts[2]] * 2
    rows.append(jnp.zeros((8, LANES), f32))
    return jnp.concatenate(rows, axis=0).astype(bf16)


def fold_rows(moments, count):
    return moments[0:count] + (moments[count : 2 * count] + moments[2 * count : 3 * count])


def particle_rows(fields, centre):
    shifted = fields - centre
    pos = shifted[0:3]
    vel = shifted[3:6]
    square = jnp.sum(pos * pos, axis=0, keepdims=True)
    return pos, vel, square


def first_near(fields, centre):
    pos, vel, square = particle_rows(fields, centre)
    root = fields[6:7]
    scale = root * root
    cross = jnp.sum(pos * vel, axis=0, keepdims=True)
    near = near_rows(jnp.concatenate([pos * scale, scale], axis=0), square * scale)
    value = jnp.concatenate([pos, vel, jnp.ones_like(square), cross], axis=0) * root
    blank = jnp.zeros((5, LANES), f32)
    moments = jnp.concatenate([*split3(value), *split3(square * root), blank], axis=0)
    return near, moments.astype(bf16)


def second_near(fields, centre, weight):
    pos, _, square = particle_rows(fields, centre)
    scale = fields[7:8]
    near = near_rows(jnp.concatenate([pos * scale, scale], axis=0), square * scale)
    value = jnp.concatenate([pos * weight, weight], axis=0)
    moments = jnp.concatenate([*split3(value), jnp.zeros((4, LANES), f32)], axis=0)
    return near, moments.astype(bf16)


def spread(columns, number):
    return jnp.broadcast_to(columns[:, number : number + 1], (LANES, LANES))


def assemble_kernel(devices, capacity, stack_ref, fields_ref, first_ref, second_ref):
    blocks = fields_ref.shape[0]
    half = second_ref.shape[0]
    for row in range(6):
        fields_ref[:, row, :] = stack_ref[row]
    fields_ref[:, 6, :] = jnp.sqrt(jnp.sqrt(stack_ref[6]))
    smooth = stack_ref[7]
    fields_ref[:, 7, :] = 1.0 / (smooth * smooth)
    first_ref[0 : blocks - half] = fields_ref[0 : blocks - half]
    second_ref[...] = fields_ref[blocks - half :]
    each = LANES // capacity
    for number, start in enumerate(range(0, devices, 8 * each)):
        lines = [
            stack_ref[8 + row // blocks, row % blocks : row % blocks + 8, 0:capacity]
            for row in range(start, min(start + 8 * each, devices), 8)
        ]
        line = jnp.concatenate(lines, axis=1)
        first_ref[blocks - half + number, :, 0 : line.shape[1]] = line


def prepare_kernel(fields_ref, near_ref, moment_ref, root_ref, own_ref, centre_ref):
    blocks = fields_ref.shape[0]
    total = jnp.sum(fields_ref[...], axis=0)
    mean = jnp.sum(total, axis=1, keepdims=True) / (blocks * LANES)
    rows = lax.broadcasted_iota(jnp.int32, (8, LANES), 0)
    centre = jnp.where(rows < 6, jnp.broadcast_to(mean, (8, LANES)), 0.0)
    centre_ref[...] = centre
    root_ref[...] = fields_ref[:, 6, :].T

    @pl.loop(0, blocks // 4)
    def _(group):
        for part in range(4):
            index = group * 4 + part
            fields = fields_ref[index]
            at = pl.ds(pl.multiple_of(index * LANES, LANES), LANES)
            near, moment_ref[:, at] = first_near(fields, centre)
            near_ref[at, :] = near.T
            pos, _, square = particle_rows(fields, centre)
            scale = fields[7:8]
            four = jnp.concatenate([pos * (-2.0 * scale), square * scale], axis=0)
            own_ref[:, at] = own_rows(four, scale)


def halves(slope):
    high = slope.astype(bf16)
    low = (slope - high.astype(f32)).astype(bf16)
    return jnp.concatenate([high, low], axis=0)


def pair_sums(own, near_ref, moment_ref, root_of, chunk, beside=None):
    steps = near_ref.shape[0] // chunk
    dense = None
    total = None

    def place(step):
        return pl.ds(step * chunk, chunk)

    def product(step):
        return jnp.dot(near_ref[place(step), :], own, preferred_element_type=f32)

    def moment(step, slope):
        fields = moment_ref[:, place(step)]
        both = jnp.concatenate([fields, fields], axis=1)
        return jnp.dot(both, slope, preferred_element_type=f32)

    square = product(0)
    slope = None
    for step in range(steps):
        following = product(step + 1) if step + 1 < steps else None
        if beside is not None:
            beside(step, steps)
        square = jnp.maximum(square, 1e-12)
        radius = square * lax.rsqrt(square)
        if root_of is None:
            tail = jnp.maximum(1.0 - radius, 0.0)
            cube = tail * tail * tail
        else:
            tail = jnp.maximum(root_of(step) - radius, 0.0)
            cube = tail * tail * tail
            value = cube * radius
            value = jnp.sum(value.reshape(chunk // 8, 8, value.shape[1]), axis=0)
            dense = value if dense is None else dense + value
        if slope is not None:
            more = moment(step - 1, slope)
            total = more if total is None else total + more
        slope = halves(cube)
        square = following
    more = moment(steps - 1, slope)
    total = more if total is None else total + more
    return dense, total


def all_rows(dense, total):
    square = total[24:25] + (total[25:26] + total[26:27])
    last = [square, jnp.sum(dense, axis=0, keepdims=True), jnp.zeros((6, dense.shape[1]), f32)]
    return jnp.concatenate([fold_rows(total, 8), *last], axis=0)


def columns_of(columns, tiles):
    def root_of(step):
        rows = []
        for part in range(2):
            line = [spread(columns, tile(2 * step + part)) for tile in tiles]
            rows.append(jnp.concatenate(line, axis=1))
        return jnp.concatenate(rows, axis=0)

    return root_of


def local_first_kernel(own_ref, near_ref, moment_ref, root_ref, *refs):
    out_ref = refs[-1]
    own = own_ref[...]
    root_of = columns_of(root_ref[...], [lambda block: block] * (own.shape[1] // LANES))
    out_ref[...] = all_rows(*pair_sums(own, near_ref, moment_ref, root_of, 2 * LANES))


def local_second_kernel(own_ref, near_ref, moment_ref, *refs):
    out_ref = refs[-1]
    own = own_ref[...]
    _, total = pair_sums(own, near_ref, moment_ref, None, 2 * LANES)
    blank = jnp.zeros((4, own.shape[1]), f32)
    out_ref[...] = jnp.concatenate([fold_rows(total, 4), blank], axis=0)


def diagonal(own):
    blank = jnp.zeros((FEATS, LANES), bf16)
    upper = jnp.concatenate([own[:, 0:LANES], blank], axis=1)
    lower = jnp.concatenate([blank, own[:, LANES:]], axis=1)
    return jnp.concatenate([upper, lower], axis=0)


def slot_rows(slot, rows_ref, me, capacity):
    if capacity & (capacity - 1) == 0:
        sender = lax.shift_right_logical(slot, capacity.bit_length() - 1)
        within = slot & (capacity - 1)
    else:
        sender, within = lax.div(slot, capacity), lax.rem(slot, capacity)
    both = rows_ref[sender, me // 8 * capacity % LANES + within]
    return both & 0xFFFF, lax.shift_right_logical(both, 16)


def fetch(pieces, gathered, semaphore):
    start = 0
    copies = []
    for number, piece in enumerate(pieces):
        count = piece.shape[0]
        copy = pltpu.make_async_copy(
            piece, gathered.at[pl.ds(start, count)], semaphore.at[number]
        )
        copy.start()
        copies.append(copy)
        start += count
    return copies


def in_turn(pairs, partners, take, build, sums):
    def beside(pair, side):
        def part(step, steps):
            some = range(step * partners // steps, (step + 1) * partners // steps)
            taken = [take(pair, k) for k in some]
            for k, fields in zip(some, taken):
                build(fields, side, k)

        return part

    beside(0, 0)(0, 1)

    @pl.loop(0, pairs // 2 - 1)
    def _(step):
        sums(step * 2, 0, beside(step * 2 + 1, 1))
        sums(step * 2 + 1, 1, beside(step * 2 + 2, 0))

    sums(pairs - 2, 0, beside(pairs - 1, 1))
    sums(pairs - 1, 1, None)


def own_tables(gathered, line_ref, step, place_ref, me, capacity, blocks):
    half = blocks // 2
    line = me // 8 * capacity // LANES
    devices = line_ref.shape[0]
    chosen = lax.broadcasted_iota(jnp.int32, (8, LANES), 0) == me % 8
    for sender in range(devices):
        first = place_ref[0, sender ^ me]
        second = place_ref[1, sender ^ me]
        block = gathered[first * step + half + line]
        row = jnp.sum(jnp.where(chosen, block, 0.0), axis=0, keepdims=True).astype(jnp.int32)
        place = jnp.where(
            row < half, first * step + row, devices * step + second * half + row - half
        )
        line_ref[sender : sender + 1, :] = place + ((first * blocks + row) << 16)


def remote_first_kernel(capacity, extra, me_ref, *refs):
    pieces, (slots_hbm, place_hbm, entropy_hbm) = refs[:PIECES], refs[PIECES : PIECES + 3]
    refs = refs[PIECES + 3 :]
    own_ref, fields_ref, centre_ref, moments_ref = refs[:4]
    density_ref, divergence_ref, weight_ref, gradient_ref, line_ref, gathered = refs[4:10]
    tables_ref, near0, near1, moment0, moment1, root0, root1 = refs[10:17]
    sums_ref, slots_ref, place_ref, entropy_ref, semaphore, table_semaphore, small = refs[17:]
    blocks = fields_ref.shape[0]
    partners = slots_ref.shape[0]
    copies = fetch(pieces, gathered, semaphore)
    for number, (source, target) in enumerate(
        ((slots_hbm, slots_ref), (place_hbm, place_ref), (entropy_hbm, entropy_ref))
    ):
        copies += fetch((source,), target, small.at[pl.ds(number, 1)])
    for copy in copies:
        copy.wait()
    centre = centre_ref[...]
    me = me_ref[0]
    own_tables(gathered, line_ref, blocks // 2 + extra, place_ref, me, capacity, blocks)
    copy = pltpu.make_async_copy(line_ref, tables_ref, table_semaphore)
    copy.start()
    copy.wait()
    sides = ((near0, moment0, root0), (near1, moment1, root1))

    def take(pair, k):
        rows = [
            slot_rows(slots_ref[k, pair * 2 + odd], tables_ref, me, capacity)[0]
            for odd in range(2)
        ]
        return [gathered[row] for row in rows]

    def build(fields, side, k):
        near, moment, root = sides[side]
        at = slice(k * LANES, (k + 1) * LANES)
        rows = []
        for odd in range(2):
            values, moments = first_near(fields[odd], centre)
            rows.append(values)
            moment[odd * 32 : odd * 32 + 32, at] = moments
            line = odd * partners + k
            root[line : line + 1, :] = fields[odd][6:7]
        near[at, :] = jnp.concatenate(rows, axis=0).T

    def sums(pair, side, beside):
        near, moment, root = sides[side]
        at = pl.ds(pl.multiple_of(pair * 2 * LANES, 2 * LANES), 2 * LANES)
        root_of = columns_of(root[...].T, [lambda k: k, lambda k: partners + k])
        dense, total = pair_sums(
            diagonal(own_ref[:, at]), near, moment, root_of, 2 * LANES, beside
        )
        before = moments_ref[:, at]
        for odd in range(2):
            here = slice(odd * LANES, (odd + 1) * LANES)
            part = all_rows(dense[:, here], total[odd * 32 : odd * 32 + 32, here])
            sums_ref[pair * 2 + odd] = part + before[:, here]

    in_turn(blocks // 2, partners, take, build, sums)
    moments = [sums_ref[:, row, :] for row in range(10)]
    own = [fields_ref[:, row, :] - centre[row : row + 1, :] for row in range(8)]
    inverse_square = own[7]
    cube = inverse_square * jnp.sqrt(inverse_square)
    square = own[0] * own[0] + own[1] * own[1] + own[2] * own[2]
    cross = own[0] * own[3] + own[1] * own[4] + own[2] * own[5]
    shift = own[0] * moments[0] + own[1] * moments[1] + own[2] * moments[2]
    spread_out = (square * moments[6] + moments[8] - 2.0 * shift) * inverse_square
    density = kernel_norm * cube * (moments[6] + 3.0 * moments[9] - 4.0 * spread_out)
    factor = (20.0 * kernel_norm) * cube * inverse_square
    approach = cross * moments[6] + moments[7]
    for row in range(3):
        approach = approach - own[row + 3] * moments[row] - own[row] * moments[row + 3]
    press = entropy_ref[...] * inverse_cube_root(density)
    mass = own[6] * own[6]
    density_ref[...] = density
    divergence_ref[...] = factor * approach / density
    weight_ref[...] = factor * (mass * mass) * press
    for row in range(3):
        gradient = (own[row] * moments[6] - moments[row]) * (factor * press)
        gradient_ref[row] = gradient


def inverse_cube_root(value):
    guess = jnp.exp(jnp.log(value) * (-1.0 / 3.0))
    guess = guess * (4.0 - value * guess * guess * guess) * (1.0 / 3.0)
    return guess * (4.0 - value * guess * guess * guess) * (1.0 / 3.0)


def prepare_second_kernel(fields_ref, centre_ref, weight_ref, near_ref, moment_ref, own_ref):
    blocks = fields_ref.shape[0]
    centre = centre_ref[...]

    @pl.loop(0, blocks // 4)
    def _(group):
        for part in range(4):
            index = group * 4 + part
            at = pl.ds(pl.multiple_of(index * LANES, LANES), LANES)
            near, moment_ref[:, at] = second_near(
                fields_ref[index], centre, weight_ref[pl.ds(index, 1), :]
            )
            near_ref[at, :] = near.T
            pos, _, square = particle_rows(fields_ref[index], centre)
            four = jnp.concatenate([pos * -2.0, square], axis=0)
            own_ref[:, at] = own_rows(four, jnp.ones_like(square))


def remote_second_kernel(capacity, me_ref, *refs):
    pieces, (slots_hbm, tables_hbm, active_hbm) = refs[:4], refs[4:7]
    gathered, own_ref, fields_ref, centre_ref, moments_ref, gradient_ref, out_ref = refs[7:14]
    weights, near0, near1, moment0, moment1, slots_ref, tables_ref, active_ref = refs[14:22]
    semaphore, small = refs[22:]
    blocks = fields_ref.shape[0]
    partners = slots_ref.shape[0]
    copies = fetch(pieces, weights, semaphore)
    for number, (source, target) in enumerate(
        ((slots_hbm, slots_ref), (tables_hbm, tables_ref), (active_hbm, active_ref))
    ):
        copies += fetch((source,), target, small.at[pl.ds(number, 1)])
    for copy in copies:
        copy.wait()
    centre = centre_ref[...]
    me = me_ref[0]
    sides = ((near0, moment0), (near1, moment1))

    def take(pair, k):
        rows = [
            slot_rows(slots_ref[k, pair * 2 + odd], tables_ref, me, capacity) for odd in range(2)
        ]
        return [(gathered[row], weights[pl.ds(line, 1), :]) for row, line in rows]

    def build(fields, side, k):
        near, moment = sides[side]
        at = slice(k * LANES, (k + 1) * LANES)
        rows = []
        for odd in range(2):
            values, moments = second_near(fields[odd][0], centre, fields[odd][1])
            rows.append(values)
            moment[odd * 16 : odd * 16 + 16, at] = moments
        near[at, :] = jnp.concatenate(rows, axis=0).T

    def sums(pair, side, beside):
        near, moment = sides[side]
        at = pl.ds(pl.multiple_of(pair * 2 * LANES, 2 * LANES), 2 * LANES)
        _, total = pair_sums(diagonal(own_ref[:, at]), near, moment, None, 256, beside)
        before = moments_ref[0:4, at]
        for odd in range(2):
            index = pair * 2 + odd
            here = slice(odd * LANES, (odd + 1) * LANES)
            part = fold_rows(total[odd * 16 : odd * 16 + 16, here], 4) + before[:, here]
            pos, _, _ = particle_rows(fields_ref[index], centre)
            out = gradient_ref[:, index, :] + (pos * part[3:4] - part[0:3])
            out_ref[:, index, :] = jnp.where(active_ref[index] > 0, out, 0.0)

    in_turn(blocks // 2, partners, take, build, sums)


def join_kernel(*refs):
    count = (len(refs) - 1) // 3
    copies = []
    for number in range(count):
        out = refs[2 * count + number]
        start = 0
        for part in range(2):
            piece = refs[2 * number + part]
            copy = pltpu.make_async_copy(
                piece, out.at[pl.ds(start, piece.shape[0])], refs[-1].at[2 * number + part]
            )
            copy.start()
            copies.append(copy)
            start += piece.shape[0]
    for copy in copies:
        copy.wait()


def in_vmem(count):
    return [pl.BlockSpec(memory_space=pltpu.VMEM)] * count


def in_smem(count):
    return [pl.BlockSpec(memory_space=pltpu.SMEM)] * count


def in_any(count):
    return [pl.BlockSpec(memory_space=pl.ANY)] * count


def shape(*dims, dtype=f32):
    return jax.ShapeDtypeStruct(dims, dtype)


def room(mebibytes):
    return pltpu.CompilerParams(vmem_limit_bytes=mebibytes * 2**20)


def join(*pairs):
    flat = [item for pair in pairs for item in pair]
    outs = [shape(2 * pair[0].shape[0], *pair[0].shape[1:]) for pair in pairs]
    return pl.pallas_call(
        join_kernel,
        out_shape=outs,
        in_specs=in_any(len(flat)),
        out_specs=in_any(len(outs)),
        scratch_shapes=[pltpu.SemaphoreType.DMA((len(flat),))],
        compiler_params=room(4),
    )(*flat)


def assemble(extra, stack, devices, capacity):
    blocks = stack.shape[1]
    half = blocks // 2
    return pl.pallas_call(
        functools.partial(assemble_kernel, devices, capacity),
        out_shape=[
            shape(blocks, 8, LANES),
            shape(half + extra, 8, LANES),
            shape(blocks - half, 8, LANES),
        ],
        in_specs=in_vmem(1),
        out_specs=in_vmem(3),
        compiler_params=room(8),
    )(stack)


def prepare(fields):
    particles = fields.shape[0] * LANES
    return pl.pallas_call(
        prepare_kernel,
        out_shape=[
            shape(particles, FEATS, dtype=bf16),
            shape(32, particles, dtype=bf16),
            shape(LANES, fields.shape[0]),
            shape(FEATS, particles, dtype=bf16),
            shape(8, LANES),
        ],
        in_specs=in_vmem(1),
        out_specs=in_vmem(5),
        compiler_params=room(16),
    )(fields)


def prepare_second(fields, centre, weight):
    particles = fields.shape[0] * LANES
    return pl.pallas_call(
        prepare_second_kernel,
        out_shape=[
            shape(particles, FEATS, dtype=bf16),
            shape(16, particles, dtype=bf16),
            shape(FEATS, particles, dtype=bf16),
        ],
        in_specs=in_vmem(3),
        out_specs=in_vmem(3),
        compiler_params=room(16),
    )(fields, centre, weight)


def local_pass(kernel, first, count, own, whole, sums):
    particles = own.shape[1]
    here = lambda index: (0, first + index)
    height = 16 if kernel is local_first_kernel else 8
    aliases = {}
    operands = [own, *whole]
    in_specs = [pl.BlockSpec((FEATS, TILE), here)]
    in_specs += in_vmem(len(whole))
    if sums is not None:
        aliases = {len(operands): 0}
        operands.append(sums)
        in_specs += in_any(1)
    return pl.pallas_call(
        kernel,
        grid=(count,),
        in_specs=in_specs,
        out_specs=pl.BlockSpec((height, TILE), here),
        out_shape=shape(height, particles),
        input_output_aliases=aliases,
        cost_estimate=pl.CostEstimate(
            flops=count * TILE * particles * 2000, bytes_accessed=2**20, transcendentals=0
        ),
        compiler_params=room(24),
    )(*operands)


def swap(value, bit, devices):
    return lax.ppermute(value, "dom", [(i, i ^ bit) for i in range(devices)])


def places(order, devices):
    table = np.zeros((devices,), np.int32)
    for apart in range(devices):
        table[apart] = sum(1 << k for k, bit in enumerate(order) if apart & bit)
    return table


def shares(tiles, stages):
    weights = [3] + [2] * (stages - 4) + [3, 5, 3]
    cuts = [round(tiles * sum(weights[:k]) / sum(weights)) for k in range(stages + 1)]
    return list(zip(cuts[:-1], cuts[1:]))


def per_device(
    devices,
    positions,
    velocities,
    masses,
    smoothing,
    entropy,
    export_blocks,
    partner_slots,
    active,
):
    blocks = positions.shape[0]
    particles = blocks * LANES
    capacity = export_blocks.shape[2]
    half = blocks // 2
    me = lax.axis_index("dom")
    extra = -(-devices * capacity // (8 * LANES))
    table = export_blocks.reshape(devices // blocks, blocks, capacity)
    layers = [
        jnp.transpose(positions, (1, 0, 2)),
        jnp.transpose(velocities, (1, 0, 2)),
        masses[None],
        smoothing[None],
    ]
    height = 8 + table.shape[0]
    stack = jnp.pad(table, ((8, 0), (0, 0), (0, LANES - capacity))).astype(f32)
    start = 0
    for layer in layers:
        after = height - start - layer.shape[0]
        stack = stack + jnp.pad(layer, ((start, after), (0, 0), (0, 0)))
        start += layer.shape[0]
    fields, first, second = assemble(extra, stack, devices, capacity)
    bits = [1 << k for k in reversed(range(devices.bit_length() - 1))]
    order0 = list(bits)
    order1 = list(bits)
    order1[-3:-1] = reversed(order1[-3:-1])
    place = jnp.asarray(np.stack([places(order0, devices), places(order1, devices)]))
    tiles = particles // TILE
    stages = len(bits)

    near, moment, root, own, centre = prepare(fields)
    sums = None
    first, second = [first], [second]
    for number, (start, stop) in enumerate(shares(tiles, stages)):
        first_in = [swap(item, order0[number], devices) for item in first]
        second_in = [swap(item, order1[number], devices) for item in second]
        if stop > start:
            sums = local_pass(
                local_first_kernel, start, stop - start, own, (near, moment, root), sums
            )
        first += first_in
        second += second_in
        if number < stages - 1:
            first, second, near, sums = lax.optimization_barrier((first, second, near, sums))
        if number < stages - 2:
            first, second = join(first, second)
            first, second = [first], [second]
    pieces = (*first, *second)

    me_array = me.astype(jnp.int32).reshape(1)

    rows = sum(piece.shape[0] for piece in pieces)
    slots = jnp.transpose(partner_slots)
    partners = slots.shape[0] * LANES
    near_side = [pltpu.VMEM((partners, 2 * FEATS), bf16)] * 2
    density, divergence, weight, gradient, tables, gathered = pl.pallas_call(
        functools.partial(remote_first_kernel, capacity, extra),
        out_shape=[
            shape(blocks, LANES),
            shape(blocks, LANES),
            shape(blocks, LANES),
            shape(3, blocks, LANES),
            shape(devices, LANES, dtype=jnp.int32),
            shape(rows, 8, LANES),
        ],
        in_specs=in_smem(1) + in_any(PIECES + 3) + in_vmem(4),
        out_specs=in_vmem(6),
        scratch_shapes=[
            pltpu.SMEM((devices, LANES), jnp.int32),
            *near_side,
            pltpu.VMEM((64, partners), bf16),
            pltpu.VMEM((64, partners), bf16),
            pltpu.VMEM((partners // LANES * 2, LANES), f32),
            pltpu.VMEM((partners // LANES * 2, LANES), f32),
            pltpu.VMEM((blocks, 16, LANES), f32),
            pltpu.SMEM(slots.shape, jnp.int32),
            pltpu.SMEM(place.shape, jnp.int32),
            pltpu.VMEM(entropy.shape, f32),
            pltpu.SemaphoreType.DMA((PIECES,)),
            pltpu.SemaphoreType.DMA,
            pltpu.SemaphoreType.DMA((3,)),
        ],
        compiler_params=room(20 + rows // 256),
    )(me_array, *pieces, slots, place, entropy, own, fields, centre, sums)

    near2, moment2, own2 = prepare_second(fields, centre, weight)
    sums = None
    weights = [weight]
    for number, (start, stop) in enumerate(shares(tiles, stages)):
        weights += [swap(item, order0[number], devices) for item in weights]
        if stop > start:
            sums = local_pass(
                local_second_kernel, start, stop - start, own2, (near2, moment2), sums
            )
        if number < stages - 1:
            weights, near2, sums = lax.optimization_barrier((weights, near2, sums))
        if number < stages - 2:
            weights = list(join(weights))

    acceleration = pl.pallas_call(
        functools.partial(remote_second_kernel, capacity),
        out_shape=shape(3, blocks, LANES),
        in_specs=in_smem(1) + in_any(7) + in_vmem(6),
        out_specs=pl.BlockSpec(memory_space=pltpu.VMEM),
        scratch_shapes=[
            pltpu.VMEM((devices * blocks, LANES), f32),
            *near_side,
            pltpu.VMEM((32, partners), bf16),
            pltpu.VMEM((32, partners), bf16),
            pltpu.SMEM(slots.shape, jnp.int32),
            pltpu.SMEM(tables.shape, jnp.int32),
            pltpu.SMEM(active.shape, jnp.int32),
            pltpu.SemaphoreType.DMA((4,)),
            pltpu.SemaphoreType.DMA((3,)),
        ],
        compiler_params=room(20 + rows // 256),
    )(
        me_array, *weights, slots, tables, active, gathered, own2, fields, centre,
        sums, gradient,
    )
    return (density, divergence, jnp.transpose(acceleration, (1, 0, 2)))


def solution(mesh):
    in_specs = (
        P("dom", None, None),
        P("dom", None, None),
        P("dom", None),
        P("dom", None),
        P("dom", None),
        P("dom", None, None),
        P("dom", None),
        P("dom"),
    )
    out_specs = (P("dom", None), P("dom", None), P("dom", None, None))
    return jax.shard_map(
        functools.partial(per_device, mesh.shape["dom"]),
        mesh=mesh,
        in_specs=in_specs,
        out_specs=out_specs,
        check_vma=False,
    )
```

time: 151 us -> 141 us (0.934)
  Pallas kernels: 125 us -> 118 us
  local copies, waits for them, and re-layouts: 3.61 us -> 0.02 us
    pallas_call x12, Pallas kernels: 91.8 us -> 87.3 us  [the longest x10 64.9 us: local_pass(): pl.pallas_call(kernel, grid=(count,), in_specs=in_specs, out_specs=pl.Blo...]
    unnamed x20 -> x8, local copies, waits for them, and re-layouts: 3.61 us -> 0.02 us
    pallas_call x1, Pallas kernels: 29.3 us -> 26.6 us  [per_device(): pl.pallas_call(functools.partial(remote_first_kernel, capacity, extra), o...]
  transfers between devices with their start and end apart: 18 -> 18, of which waited for: 1 -> 2; matrix products, arithmetic and copies ran while one was open for 0% -> 0% of each run, Pallas kernels for 48% -> 48%
where the time goes in v4:
time: 141 us
  Pallas kernels  118 us (84%)
  starting transfers between devices  19.3 us (14%)
  waiting for transfers between devices  1.72 us (1%)
    pallas_call x10, Pallas kernels, local_pass(): pl.pallas_call(kernel, grid=(count,), in_specs=in_specs, out_specs=pl.Blo...  64.9 us
    pallas_call x1, Pallas kernels, per_device(): pl.pallas_call(functools.partial(remote_first_kernel, capacity, extra), o...  26.6 us
    pallas_call x1, Pallas kernels, per_device(): pl.pallas_call(functools.partial(remote_second_kernel, capacity), out_sha...  22.3 us
    ppermute x18, starting transfers between devices, swap(): return lax.ppermute(value, 'dom', [(i, i ^ bit) for i in range(devices)])  19.3 us
  transfers between devices with their start and end apart: 18, of which 2 were waited for; matrix products, arithmetic and copies ran while one was open for 0% of the time, Pallas kernels for 48%

profile of v4, /device:TPU:0, one launch (start us, length us, event | category | flops | bytes accessed | tf_op | source)
XLA Modules:
  0.0 140.9 jit_solution(4761146022529923142)
XLA Ops:
  0.6 0.9 pad_add_fusion.stack_ref
  1.5 0.1 shard_map.112
  1.6 4.1 %collective-permute-start.1 = (f32[16,8,128]{2,1,0:T(8,128)S(1)}, f32[16,8,128]{2,1,0:T(8,128)S(1)}, u32[]{:S(2)}, u32[]{:S(2)}) collective-permute-start(f32[16,8,128]{2,1,0:T(8,128)S(1)} %get-tuple-element.75.refs_2_), channel_id=1, source_target_pairs={{0,16},{1,17},{2,18},{3,19},{4,20},{5,21},{6,22},{7,23},{8,24},{9,... | collective-permute-start | bytes 196616 | tf_op jit(solution)/shard_map/ppermute | solution.py:554
  5.7 0.1 collective-permute-start
  5.8 1.2 shard_map.113
  7.0 6.8 %shard_map.114.refs_0_ = f32[16,4096]{1,0:T(8,128)S(1)} custom-call(bf16[48,4096]{1,0:T(8,128)(2,1)S(1)} %get-tuple-element.70.own_ref.refs_11_, bf16[4096,48]{1,0:T(8,128)(2,1)S(1)} %get-tuple-element.102.near_ref, bf16[32,4096]{1,0:T(8,128)(2,1)S(1)} %get-tuple-element.71.moment_ref, f32[128,32]{1,0:T(8,128)S(1)} %get-tuple-element.72.root_ref), custom_call_target="tpu_custom_call" | custom-call | flops 6291456000 | bytes 1048576 | tf_op jit(solution)/shard_map/pallas_call | solution.py:539
  13.8 0.0 collective-permute-done.1.refs_3_
  13.8 0.0 collective-permute-done.refs_1_
  13.8 0.4 shard_map.115
  14.2 1.9 %collective-permute-start.3 = (f32[32,8,128]{2,1,0:T(8,128)S(1)}, f32[32,8,128]{2,1,0:T(8,128)S(1)}, u32[]{:S(2)}, u32[]{:S(2)}) collective-permute-start(f32[32,8,128]{2,1,0:T(8,128)S(1)} %get-tuple-element.83.refs_2_), channel_id=1, source_target_pairs={{0,8},{1,9},{2,10},{3,11},{4,12},{5,13},{6,14},{7,15},{8,0},{9,1},... | collective-permute-start | bytes 393224 | tf_op jit(solution)/shard_map/ppermute | solution.py:554
  16.2 0.2 collective-permute-start.2
  16.3 4.5 %shard_map.116.refs_0_ = f32[16,4096]{1,0:T(8,128)S(1)} custom-call(bf16[48,4096]{1,0:T(8,128)(2,1)S(1)} %get-tuple-element.70.own_ref.refs_11_, bf16[4096,48]{1,0:T(8,128)(2,1)S(1)} %get-tuple-element.102.near_ref, bf16[32,4096]{1,0:T(8,128)(2,1)S(1)} %get-tuple-element.71.moment_ref, ...), custom_call_target="tpu_custom_call", output_to_operand_aliasing={{}: (4, {})} | custom-call | flops 4194304000 | bytes 1048576 | tf_op jit(solution)/shard_map/pallas_call | solution.py:539
  20.9 0.0 collective-permute-done.3.refs_3_
  20.9 1.4 collective-permute-done.2.refs_1_
  22.3 0.7 shard_map.117
  23.0 1.6 %collective-permute-start.5 = (f32[64,8,128]{2,1,0:T(8,128)S(1)}, f32[64,8,128]{2,1,0:T(8,128)S(1)}, u32[]{:S(2)}, u32[]{:S(2)}) collective-permute-start(f32[64,8,128]{2,1,0:T(8,128)S(1)} %get-tuple-element.91.refs_2_), channel_id=1, source_target_pairs={{0,2},{1,3},{2,0},{3,1},{4,6},{5,7},{6,4},{7,5},{8,10},{9,11},{10,... | collective-permute-start | bytes 786440 | tf_op jit(solution)/shard_map/ppermute | solution.py:554
  24.5 1.5 %collective-permute-start.4 = (f32[68,8,128]{2,1,0:T(8,128)S(1)}, f32[68,8,128]{2,1,0:T(8,128)S(1)}, u32[]{:S(2)}, u32[]{:S(2)}) collective-permute-start(f32[68,8,128]{2,1,0:T(8,128)S(1)} %get-tuple-element.89.refs_0_), channel_id=1, source_target_pairs={{0,4},{1,5},{2,6},{3,7},{4,0},{5,1},{6,2},{7,3},{8,12},{9,13},{10,... | collective-permute-start | bytes 835592 | tf_op jit(solution)/shard_map/ppermute | solution.py:554
  26.0 6.8 %shard_map.118.refs_0_ = f32[16,4096]{1,0:T(8,128)S(1)} custom-call(bf16[48,4096]{1,0:T(8,128)(2,1)S(1)} %get-tuple-element.70.own_ref.refs_11_, bf16[4096,48]{1,0:T(8,128)(2,1)S(1)} %get-tuple-element.102.near_ref, bf16[32,4096]{1,0:T(8,128)(2,1)S(1)} %get-tuple-element.71.moment_ref, ...), custom_call_target="tpu_custom_call", output_to_operand_aliasing={{}: (4, {})} | custom-call | flops 6291456000 | bytes 1048576 | tf_op jit(solution)/shard_map/pallas_call | solution.py:539
  32.8 0.0 collective-permute-done.5.refs_3_
  32.8 0.0 collective-permute-done.4.refs_1_
  32.8 0.2 shard_map.119
  33.0 0.6 collective-permute-start.7
  33.6 0.5 collective-permute-start.6
  34.1 11.2 %shard_map.120.refs_0_ = f32[16,4096]{1,0:T(8,128)S(1)} custom-call(bf16[48,4096]{1,0:T(8,128)(2,1)S(1)} %get-tuple-element.70.own_ref.refs_11_, bf16[4096,48]{1,0:T(8,128)(2,1)S(1)} %get-tuple-element.102.near_ref, bf16[32,4096]{1,0:T(8,128)(2,1)S(1)} %get-tuple-element.71.moment_ref, ...), custom_call_target="tpu_custom_call", output_to_operand_aliasing={{}: (4, {})} | custom-call | flops 10485760000 | bytes 1048576 | tf_op jit(solution)/shard_map/pallas_call | solution.py:539
  45.4 0.0 copy-start
  45.4 0.0 copy-start.1
  45.4 0.0 copy-start.2
  45.4 0.0 collective-permute-done.7.refs_5_
  45.4 0.2 collective-permute-done.6.refs_1_
  45.6 0.0 collective-permute-start.10
  45.6 0.5 collective-permute-start.11
  46.2 0.0 collective-permute-start.8
  46.2 0.5 collective-permute-start.9
  46.7 6.8 %shard_map.121.refs_14_ = f32[16,4096]{1,0:T(8,128)S(1)} custom-call(bf16[48,4096]{1,0:T(8,128)(2,1)S(1)} %get-tuple-element.70.own_ref.refs_11_, bf16[4096,48]{1,0:T(8,128)(2,1)S(1)} %get-tuple-element.102.near_ref, bf16[32,4096]{1,0:T(8,128)(2,1)S(1)} %get-tuple-element.71.moment_ref, ...), custom_call_target="tpu_custom_call", output_to_operand_aliasing={{}: (4, {})} | custom-call | flops 6291456000 | bytes 1048576 | tf_op jit(solution)/shard_map/pallas_call | solution.py:539
  53.4 0.0 collective-permute-done.10.refs_6_
  53.4 0.0 collective-permute-done.11.refs_7_
  53.4 0.0 collective-permute-done.8.refs_2_
  53.5 0.0 collective-permute-done.9.refs_3_
  53.5 0.0 copy-done
  53.5 0.0 copy-done.1
  53.5 0.0 copy-done.2
  53.5 26.6 %shard_map.122 = (f32[32,128]{1,0:T(8,128)}, f32[32,128]{1,0:T(8,128)}, f32[32,128]{1,0:T(8,128)S(1)}, f32[3,32,128]{2,1,0:T(8,128)S(1)}, s32[32,128]{1,0:T(8,128)S(1)}, /*index=5*/f32[1056,8,128]{2,1,0:T(8,128)S(1)}) custom-call(s32[1]{0:T(128)} %bitcast.me_ref, f32[136,8,128]{2,1,0:T(8,128)S(1)} %get-tuple-element.97.refs_0_, ...), custom_call_target="tpu_custom_call" | custom-call | tf_op jit(solution)/shard_map/pallas_call | solution.py:635
  80.1 2.6 %collective-permute-start.12 = (f32[32,128]{1,0:T(8,128)S(1)}, f32[32,128]{1,0:T(8,128)S(1)}, u32[]{:S(2)}, u32[]{:S(2)}) collective-permute-start(f32[32,128]{1,0:T(8,128)S(1)} %get-tuple-element.110.weight_ref.refs_0_), channel_id=1, source_target_pairs={{0,16},{1,17},{2,18},{3,19},{4,20},{5,21},{6,22},{7,23},{8,24},{9,... | collective-permute-start | bytes 49160 | tf_op jit(solution)/shard_map/ppermute | solution.py:554
  82.7 1.0 shard_map.123
  83.7 5.4 %shard_map.124.refs_0_ = f32[8,4096]{1,0:T(8,128)S(1)} custom-call(bf16[48,4096]{1,0:T(8,128)(2,1)S(1)} %get-tuple-element.108.own_ref.refs_8_, bf16[4096,48]{1,0:T(8,128)(2,1)S(1)} %get-tuple-element.126.near_ref, bf16[16,4096]{1,0:T(8,128)(2,1)S(1)} %get-tuple-element.109.moment_ref), custom_call_target="tpu_custom_call" | custom-call | flops 6291456000 | bytes 1048576 | tf_op jit(solution)/shard_map/pallas_call | solution.py:539
  89.2 0.0 collective-permute-done.12.refs_1_
  89.2 0.1 shard_map.125.refs_0_
  89.2 1.7 %collective-permute-start.13 = (f32[64,128]{1,0:T(8,128)S(1)}, f32[64,128]{1,0:T(8,128)S(1)}, u32[]{:S(2)}, u32[]{:S(2)}) collective-permute-start(f32[64,128]{1,0:T(8,128)S(1)} %shard_map.125.refs_0_), channel_id=1, source_target_pairs={{0,8},{1,9},{2,10},{3,11},{4,12},{5,13},{6,14},{7,15},{8,0},{9,1},... | collective-permute-start | bytes 98312 | tf_op jit(solution)/shard_map/ppermute | solution.py:554
  90.9 3.6 %shard_map.126.refs_0_ = f32[8,4096]{1,0:T(8,128)S(1)} custom-call(bf16[48,4096]{1,0:T(8,128)(2,1)S(1)} %get-tuple-element.108.own_ref.refs_8_, bf16[4096,48]{1,0:T(8,128)(2,1)S(1)} %get-tuple-element.126.near_ref, bf16[16,4096]{1,0:T(8,128)(2,1)S(1)} %get-tuple-element.109.moment_ref, f32[8,4096]{1,0:T(8,128)S(1)} %shard_map.124.refs_0_), custom_call_target="tpu_custom_call", output_to_operand_aliasing={{}: (3, {})} | custom-call | flops 4194304000 | bytes 1048576 | tf_op jit(solution)/shard_map/pallas_call | solution.py:539
  94.5 0.0 collective-permute-done.13.refs_1_
  94.5 0.1 shard_map.127.refs_0_
  94.6 1.6 %collective-permute-start.14 = (f32[128,128]{1,0:T(8,128)S(1)}, f32[128,128]{1,0:T(8,128)S(1)}, u32[]{:S(2)}, u32[]{:S(2)}) collective-permute-start(f32[128,128]{1,0:T(8,128)S(1)} %shard_map.127.refs_0_), channel_id=1, source_target_pairs={{0,4},{1,5},{2,6},{3,7},{4,0},{5,1},{6,2},{7,3},{8,12},{9,13},{10,... | collective-permute-start | bytes 196616 | tf_op jit(solution)/shard_map/ppermute | solution.py:554
  96.2 5.4 %shard_map.128.refs_0_ = f32[8,4096]{1,0:T(8,128)S(1)} custom-call(bf16[48,4096]{1,0:T(8,128)(2,1)S(1)} %get-tuple-element.108.own_ref.refs_8_, bf16[4096,48]{1,0:T(8,128)(2,1)S(1)} %get-tuple-element.126.near_ref, bf16[16,4096]{1,0:T(8,128)(2,1)S(1)} %get-tuple-element.109.moment_ref, f32[8,4096]{1,0:T(8,128)S(1)} %shard_map.126.refs_0_), custom_call_target="tpu_custom_call", output_to_operand_aliasing={{}: (3, {})} | custom-call | flops 6291456000 | bytes 1048576 | tf_op jit(solution)/shard_map/pallas_call | solution.py:539
  101.6 0.0 collective-permute-done.14.refs_1_
  101.7 0.2 shard_map.129.refs_0_
  101.9 1.5 %collective-permute-start.15 = (f32[256,128]{1,0:T(8,128)S(1)}, f32[256,128]{1,0:T(8,128)S(1)}, u32[]{:S(2)}, u32[]{:S(2)}) collective-permute-start(f32[256,128]{1,0:T(8,128)S(1)} %shard_map.129.refs_0_), channel_id=1, source_target_pairs={{0,2},{1,3},{2,0},{3,1},{4,6},{5,7},{6,4},{7,5},{8,10},{9,11},{10,... | collective-permute-start | bytes 393224 | tf_op jit(solution)/shard_map/ppermute | solution.py:554
  103.3 9.0 %shard_map.130.refs_0_ = f32[8,4096]{1,0:T(8,128)S(1)} custom-call(bf16[48,4096]{1,0:T(8,128)(2,1)S(1)} %get-tuple-element.108.own_ref.refs_8_, bf16[4096,48]{1,0:T(8,128)(2,1)S(1)} %get-tuple-element.126.near_ref, bf16[16,4096]{1,0:T(8,128)(2,1)S(1)} %get-tuple-element.109.moment_ref, f32[8,4096]{1,0:T(8,128)S(1)} %shard_map.128.refs_0_), custom_call_target="tpu_custom_call", output_to_operand_aliasing={{}: (3, {})} | custom-call | flops 10485760000 | bytes 1048576 | tf_op jit(solution)/shard_map/pallas_call | solution.py:539
  112.4 0.0 collective-permute-done.15.refs_1_
  112.4 0.1 collective-permute-start.16
  112.4 0.5 collective-permute-start.17
  112.9 5.4 %shard_map.131.refs_11_ = f32[8,4096]{1,0:T(8,128)S(1)} custom-call(bf16[48,4096]{1,0:T(8,128)(2,1)S(1)} %get-tuple-element.108.own_ref.refs_8_, bf16[4096,48]{1,0:T(8,128)(2,1)S(1)} %get-tuple-element.126.near_ref, bf16[16,4096]{1,0:T(8,128)(2,1)S(1)} %get-tuple-element.109.moment_ref, f32[8,4096]{1,0:T(8,128)S(1)} %shard_map.130.refs_0_), custom_call_target="tpu_custom_call", output_to_operand_aliasing={{}: (3, {})} | custom-call | flops 6291456000 | bytes 1048576 | tf_op jit(solution)/shard_map/pallas_call | solution.py:539
  118.4 0.0 collective-permute-done.16.refs_2_
  118.4 0.0 collective-permute-done.17.refs_3_
  118.4 22.3 %shard_map.132 = f32[3,32,128]{2,1,0:T(8,128)} custom-call(s32[1]{0:T(128)} %bitcast.me_ref, f32[256,128]{1,0:T(8,128)S(1)} %shard_map.129.refs_0_, f32[256,128]{1,0:T(8,128)S(1)} %collective-permute-done.15.refs_1_, f32[256,128]{1,0:T(8,128)S(1)} %collective-permute-done.16.refs_2_, f32[256,128]{1,0:T(8,128)S(1)} %collective-permute-done.17.refs_3_, ...), custom_call_target="tpu_custom_call" | custom-call | tf_op jit(solution)/shard_map/pallas_call | solution.py:679
  (2 shorter events, 0.0 us)
Async XLA Ops:
  1.6 12.2 %collective-permute-start.1 = (f32[16,8,128]{2,1,0:T(8,128)S(1)}, f32[16,8,128]{2,1,0:T(8,128)S(1)}, u32[]{:S(2)}, u32[]{:S(2)}) collective-permute-start(f32[16,8,128]{2,1,0:T(8,128)S(1)} %get-tuple-element.75.refs_2_), channel_id=1, source_target_pairs={{0,16},{1,17},{2,18},{3,19},{4,20},{5,21},{6,22},{7,23},{8,24},{9,... | collective-permute-start | bytes 196616 | tf_op jit(solution)/shard_map/ppermute | solution.py:554
  5.7 8.1 %collective-permute-start = (f32[17,8,128]{2,1,0:T(8,128)S(1)}, f32[17,8,128]{2,1,0:T(8,128)S(1)}, u32[]{:S(2)}, u32[]{:S(2)}) collective-permute-start(f32[17,8,128]{2,1,0:T(8,128)S(1)} %get-tuple-element.73.refs_0_), channel_id=1, source_target_pairs={{0,16},{1,17},{2,18},{3,19},{4,20},{5,21},{6,22},{7,23},{8,24},{9,... | collective-permute-start | bytes 208904 | tf_op jit(solution)/shard_map/ppermute | solution.py:554
  14.2 6.6 %collective-permute-start.3 = (f32[32,8,128]{2,1,0:T(8,128)S(1)}, f32[32,8,128]{2,1,0:T(8,128)S(1)}, u32[]{:S(2)}, u32[]{:S(2)}) collective-permute-start(f32[32,8,128]{2,1,0:T(8,128)S(1)} %get-tuple-element.83.refs_2_), channel_id=1, source_target_pairs={{0,8},{1,9},{2,10},{3,11},{4,12},{5,13},{6,14},{7,15},{8,0},{9,1},... | collective-permute-start | bytes 393224 | tf_op jit(solution)/shard_map/ppermute | solution.py:554
  16.2 6.1 %collective-permute-start.2 = (f32[34,8,128]{2,1,0:T(8,128)S(1)}, f32[34,8,128]{2,1,0:T(8,128)S(1)}, u32[]{:S(2)}, u32[]{:S(2)}) collective-permute-start(f32[34,8,128]{2,1,0:T(8,128)S(1)} %get-tuple-element.81.refs_0_), channel_id=1, source_target_pairs={{0,8},{1,9},{2,10},{3,11},{4,12},{5,13},{6,14},{7,15},{8,0},{9,1},... | collective-permute-start | bytes 417800 | tf_op jit(solution)/shard_map/ppermute | solution.py:554
  23.0 9.8 %collective-permute-start.5 = (f32[64,8,128]{2,1,0:T(8,128)S(1)}, f32[64,8,128]{2,1,0:T(8,128)S(1)}, u32[]{:S(2)}, u32[]{:S(2)}) collective-permute-start(f32[64,8,128]{2,1,0:T(8,128)S(1)} %get-tuple-element.91.refs_2_), channel_id=1, source_target_pairs={{0,2},{1,3},{2,0},{3,1},{4,6},{5,7},{6,4},{7,5},{8,10},{9,11},{10,... | collective-permute-start | bytes 786440 | tf_op jit(solution)/shard_map/ppermute | solution.py:554
  24.5 8.3 %collective-permute-start.4 = (f32[68,8,128]{2,1,0:T(8,128)S(1)}, f32[68,8,128]{2,1,0:T(8,128)S(1)}, u32[]{:S(2)}, u32[]{:S(2)}) collective-permute-start(f32[68,8,128]{2,1,0:T(8,128)S(1)} %get-tuple-element.89.refs_0_), channel_id=1, source_target_pairs={{0,4},{1,5},{2,6},{3,7},{4,0},{5,1},{6,2},{7,3},{8,12},{9,13},{10,... | collective-permute-start | bytes 835592 | tf_op jit(solution)/shard_map/ppermute | solution.py:554
  33.0 12.4 %collective-permute-start.7 = (f32[128,8,128]{2,1,0:T(8,128)S(1)}, f32[128,8,128]{2,1,0:T(8,128)S(1)}, u32[]{:S(2)}, u32[]{:S(2)}) collective-permute-start(f32[128,8,128]{2,1,0:T(8,128)S(1)} %get-tuple-element.99.refs_4_), channel_id=1, source_target_pairs={{0,4},{1,5},{2,6},{3,7},{4,0},{5,1},{6,2},{7,3},{8,12},{9,13},{10,... | collective-permute-start | bytes 1572872 | tf_op jit(solution)/shard_map/ppermute | solution.py:554
  33.6 12.1 %collective-permute-start.6 = (f32[136,8,128]{2,1,0:T(8,128)S(1)}, f32[136,8,128]{2,1,0:T(8,128)S(1)}, u32[]{:S(2)}, u32[]{:S(2)}) collective-permute-start(f32[136,8,128]{2,1,0:T(8,128)S(1)} %get-tuple-element.97.refs_0_), channel_id=1, source_target_pairs={{0,2},{1,3},{2,0},{3,1},{4,6},{5,7},{6,4},{7,5},{8,10},{9,11},{10,... | collective-permute-start | bytes 1671176 | tf_op jit(solution)/shard_map/ppermute | solution.py:554
  45.4 8.1 %copy-start = (s32[32,16]{0,1:T(8,128)S(1)}, s32[32,16]{0,1:T(8,128)}, u32[]{:S(2)}) copy-start(s32[32,16]{0,1:T(8,128)} %param.15) | copy-start | bytes 6148
  45.4 8.1 %copy-start.1 = (f32[32,128]{1,0:T(8,128)S(1)}, f32[32,128]{1,0:T(8,128)}, u32[]{:S(2)}) copy-start(f32[32,128]{1,0:T(8,128)} %refs_10_.1) | copy-start | bytes 49156
  45.4 8.1 %copy-start.2 = (s32[2,32]{1,0:T(2,128)S(1)}, s32[2,32]{1,0:T(2,128)}, u32[]{:S(2)}) copy-start(s32[2,32]{1,0:T(2,128)} %constant.10.clone.refs_9_) | copy-start | bytes 772
  45.6 7.8 %collective-permute-start.10 = (f32[128,8,128]{2,1,0:T(8,128)S(1)}, f32[128,8,128]{2,1,0:T(8,128)S(1)}, u32[]{:S(2)}, u32[]{:S(2)}) collective-permute-start(f32[128,8,128]{2,1,0:T(8,128)S(1)} %get-tuple-element.99.refs_4_), channel_id=1, source_target_pairs={{0,1},{1,0},{2,3},{3,2},{4,5},{5,4},{6,7},{7,6},{8,9},{9,8},{10,11... | collective-permute-start | bytes 1572872 | tf_op jit(solution)/shard_map/ppermute | solution.py:554
  45.6 7.8 %collective-permute-start.11 = (f32[128,8,128]{2,1,0:T(8,128)S(1)}, f32[128,8,128]{2,1,0:T(8,128)S(1)}, u32[]{:S(2)}, u32[]{:S(2)}) collective-permute-start(f32[128,8,128]{2,1,0:T(8,128)S(1)} %collective-permute-done.7.refs_5_), channel_id=1, source_target_pairs={{0,1},{1,0},{2,3},{3,2},{4,5},{5,4},{6,7},{7,6},{8,9},{9,8},{10,11... | collective-permute-start | bytes 1572872 | tf_op jit(solution)/shard_map/ppermute | solution.py:554
  46.2 7.3 %collective-permute-start.8 = (f32[136,8,128]{2,1,0:T(8,128)S(1)}, f32[136,8,128]{2,1,0:T(8,128)S(1)}, u32[]{:S(2)}, u32[]{:S(2)}) collective-permute-start(f32[136,8,128]{2,1,0:T(8,128)S(1)} %get-tuple-element.97.refs_0_), channel_id=1, source_target_pairs={{0,1},{1,0},{2,3},{3,2},{4,5},{5,4},{6,7},{7,6},{8,9},{9,8},{10,11... | collective-permute-start | bytes 1671176 | tf_op jit(solution)/shard_map/ppermute | solution.py:554
  46.2 7.3 %collective-permute-start.9 = (f32[136,8,128]{2,1,0:T(8,128)S(1)}, f32[136,8,128]{2,1,0:T(8,128)S(1)}, u32[]{:S(2)}, u32[]{:S(2)}) collective-permute-start(f32[136,8,128]{2,1,0:T(8,128)S(1)} %collective-permute-done.6.refs_1_), channel_id=1, source_target_pairs={{0,1},{1,0},{2,3},{3,2},{4,5},{5,4},{6,7},{7,6},{8,9},{9,8},{10,11... | collective-permute-start | bytes 1671176 | tf_op jit(solution)/shard_map/ppermute | solution.py:554
  80.1 9.0 %collective-permute-start.12 = (f32[32,128]{1,0:T(8,128)S(1)}, f32[32,128]{1,0:T(8,128)S(1)}, u32[]{:S(2)}, u32[]{:S(2)}) collective-permute-start(f32[32,128]{1,0:T(8,128)S(1)} %get-tuple-element.110.weight_ref.refs_0_), channel_id=1, source_target_pairs={{0,16},{1,17},{2,18},{3,19},{4,20},{5,21},{6,22},{7,23},{8,24},{9,... | collective-permute-start | bytes 49160 | tf_op jit(solution)/shard_map/ppermute | solution.py:554
  89.2 5.3 %collective-permute-start.13 = (f32[64,128]{1,0:T(8,128)S(1)}, f32[64,128]{1,0:T(8,128)S(1)}, u32[]{:S(2)}, u32[]{:S(2)}) collective-permute-start(f32[64,128]{1,0:T(8,128)S(1)} %shard_map.125.refs_0_), channel_id=1, source_target_pairs={{0,8},{1,9},{2,10},{3,11},{4,12},{5,13},{6,14},{7,15},{8,0},{9,1},... | collective-permute-start | bytes 98312 | tf_op jit(solution)/shard_map/ppermute | solution.py:554
  94.6 7.0 %collective-permute-start.14 = (f32[128,128]{1,0:T(8,128)S(1)}, f32[128,128]{1,0:T(8,128)S(1)}, u32[]{:S(2)}, u32[]{:S(2)}) collective-permute-start(f32[128,128]{1,0:T(8,128)S(1)} %shard_map.127.refs_0_), channel_id=1, source_target_pairs={{0,4},{1,5},{2,6},{3,7},{4,0},{5,1},{6,2},{7,3},{8,12},{9,13},{10,... | collective-permute-start | bytes 196616 | tf_op jit(solution)/shard_map/ppermute | solution.py:554
  101.9 10.5 %collective-permute-start.15 = (f32[256,128]{1,0:T(8,128)S(1)}, f32[256,128]{1,0:T(8,128)S(1)}, u32[]{:S(2)}, u32[]{:S(2)}) collective-permute-start(f32[256,128]{1,0:T(8,128)S(1)} %shard_map.129.refs_0_), channel_id=1, source_target_pairs={{0,2},{1,3},{2,0},{3,1},{4,6},{5,7},{6,4},{7,5},{8,10},{9,11},{10,... | collective-permute-start | bytes 393224 | tf_op jit(solution)/shard_map/ppermute | solution.py:554
  112.3 6.0 %copy-start.3 = (s32[32]{0:T(128)S(1)}, s32[32]{0:T(128)}, u32[]{:S(2)}) copy-start(s32[32]{0:T(128)} %refs_6_.1) | copy-start | bytes 388
  112.4 6.0 %collective-permute-start.16 = (f32[256,128]{1,0:T(8,128)S(1)}, f32[256,128]{1,0:T(8,128)S(1)}, u32[]{:S(2)}, u32[]{:S(2)}) collective-permute-start(f32[256,128]{1,0:T(8,128)S(1)} %shard_map.129.refs_0_), channel_id=1, source_target_pairs={{0,1},{1,0},{2,3},{3,2},{4,5},{5,4},{6,7},{7,6},{8,9},{9,8},{10,11... | collective-permute-start | bytes 393224 | tf_op jit(solution)/shard_map/ppermute | solution.py:554
  112.4 5.9 %collective-permute-start.17 = (f32[256,128]{1,0:T(8,128)S(1)}, f32[256,128]{1,0:T(8,128)S(1)}, u32[]{:S(2)}, u32[]{:S(2)}) collective-permute-start(f32[256,128]{1,0:T(8,128)S(1)} %collective-permute-done.15.refs_1_), channel_id=1, source_target_pairs={{0,1},{1,0},{2,3},{3,2},{4,5},{5,4},{6,7},{7,6},{8,9},{9,8},{10,11... | collective-permute-start | bytes 393224 | tf_op jit(solution)/shard_map/ppermute | solution.py:554

commit v5 on v4

--- a/solution.py
+++ b/solution.py
@@ -24,11 +24,10 @@
     return high, middle, rest - middle
 
 
-def near_rows(four, fifth):
+def near_rows(four, parts):
     high, middle, low = split3(jnp.concatenate([four, four], axis=0))
     upper = lax.broadcasted_iota(jnp.int32, high.shape, 0) < 4
     mixed = jnp.where(upper, high, middle)
-    parts = split3(fifth)
     rows = [high, middle, low, mixed, *parts, *parts, *parts[:2], jnp.zeros((8, LANES), f32)]
     return jnp.concatenate(rows, axis=0).astype(bf16)
 
@@ -59,19 +58,23 @@
     root = fields[6:7]
     scale = root * root
     cross = jnp.sum(pos * vel, axis=0, keepdims=True)
-    near = near_rows(jnp.concatenate([pos * scale, scale], axis=0), square * scale)
+    squares = split3(jnp.concatenate([square * scale, square * root], axis=0))
+    fifth, weighted = ([part[row : row + 1] for part in squares] for row in range(2))
+    near = near_rows(jnp.concatenate([pos * scale, scale], axis=0), fifth)
     value = jnp.concatenate([pos, vel, jnp.ones_like(square), cross], axis=0) * root
     blank = jnp.zeros((5, LANES), f32)
-    moments = jnp.concatenate([*split3(value), *split3(square * root), blank], axis=0)
+    moments = jnp.concatenate([*split3(value), *weighted, blank], axis=0)
     return near, moments.astype(bf16)
 
 
 def second_near(fields, centre, weight):
     pos, _, square = particle_rows(fields, centre)
     scale = fields[7:8]
-    near = near_rows(jnp.concatenate([pos * scale, scale], axis=0), square * scale)
-    value = jnp.concatenate([pos * weight, weight], axis=0)
-    moments = jnp.concatenate([*split3(value), jnp.zeros((4, LANES), f32)], axis=0)
+    value = split3(jnp.concatenate([pos * weight, weight, square * scale], axis=0))
+    fifth = [part[4:5] for part in value]
+    near = near_rows(jnp.concatenate([pos * scale, scale], axis=0), fifth)
+    value = [part[0:4] for part in value]
+    moments = jnp.concatenate([*value, jnp.zeros((4, LANES), f32)], axis=0)
     return near, moments.astype(bf16)
 
 
@@ -544,7 +547,7 @@
         out_shape=shape(height, particles),
         input_output_aliases=aliases,
         cost_estimate=pl.CostEstimate(
-            flops=count * TILE * particles * 2000, bytes_accessed=2**20, transcendentals=0
+            flops=3 * TILE * particles * 2000, bytes_accessed=2**20, transcendentals=0
         ),
         compiler_params=room(24),
     )(*operands)
@@ -562,7 +565,7 @@
 
 
 def shares(tiles, stages):
-    weights = [3] + [2] * (stages - 4) + [3, 5, 3]
+    weights = [3] * (stages - 2) + [5, 2]
     cuts = [round(tiles * sum(weights[:k]) / sum(weights)) for k in range(stages + 1)]
     return list(zip(cuts[:-1], cuts[1:]))
 

time: 141 us -> 139 us (0.986)
  transfers between devices with their start and end apart: 18 -> 18, of which waited for: 2 -> 1; matrix products, arithmetic and copies ran while one was open for 0% -> 0% of each run, Pallas kernels for 48% -> 48%
where the time goes in v5:
time: 139 us
  Pallas kernels  117 us (84%)
  starting transfers between devices  19 us (14%)
    pallas_call x10, Pallas kernels, local_pass(): pl.pallas_call(kernel, grid=(count,), in_specs=in_specs, out_specs=pl.Blo...  64.9 us
    pallas_call x1, Pallas kernels, per_device(): pl.pallas_call(functools.partial(remote_first_kernel, capacity, extra), o...  26.3 us
    pallas_call x1, Pallas kernels, per_device(): pl.pallas_call(functools.partial(remote_second_kernel, capacity), out_sha...  22 us
    ppermute x18, starting transfers between devices, swap(): return lax.ppermute(value, 'dom', [(i, i ^ bit) for i in range(devices)])  19 us
  transfers between devices with their start and end apart: 18, of which 1 were waited for; matrix products, arithmetic and copies ran while one was open for 0% of the time, Pallas kernels for 48%

profile of v5, /device:TPU:0, one launch (start us, length us, event | category | flops | bytes accessed | tf_op | source)
XLA Modules:
  0.0 139.2 jit_solution(2616065008537500759)
XLA Ops:
  0.6 0.9 pad_add_fusion.stack_ref
  1.5 0.1 shard_map.112
  1.6 4.1 %collective-permute-start.1 = (f32[16,8,128]{2,1,0:T(8,128)S(1)}, f32[16,8,128]{2,1,0:T(8,128)S(1)}, u32[]{:S(2)}, u32[]{:S(2)}) collective-permute-start(f32[16,8,128]{2,1,0:T(8,128)S(1)} %get-tuple-element.75.refs_2_), channel_id=1, source_target_pairs={{0,16},{1,17},{2,18},{3,19},{4,20},{5,21},{6,22},{7,23},{8,24},{9,... | collective-permute-start | bytes 196616 | tf_op jit(solution)/shard_map/ppermute | solution.py:557
  5.7 0.1 collective-permute-start
  5.8 1.2 shard_map.113
  7.0 6.8 %shard_map.114.refs_0_ = f32[16,4096]{1,0:T(8,128)S(1)} custom-call(bf16[48,4096]{1,0:T(8,128)(2,1)S(1)} %get-tuple-element.70.own_ref.refs_11_, bf16[4096,48]{1,0:T(8,128)(2,1)S(1)} %get-tuple-element.102.near_ref, bf16[32,4096]{1,0:T(8,128)(2,1)S(1)} %get-tuple-element.71.moment_ref, f32[128,32]{1,0:T(8,128)S(1)} %get-tuple-element.72.root_ref), custom_call_target="tpu_custom_call" | custom-call | flops 6291456000 | bytes 1048576 | tf_op jit(solution)/shard_map/pallas_call | solution.py:542
  13.8 0.0 collective-permute-done.1.refs_3_
  13.8 0.0 collective-permute-done.refs_1_
  13.9 0.4 shard_map.115
  14.3 1.9 %collective-permute-start.3 = (f32[32,8,128]{2,1,0:T(8,128)S(1)}, f32[32,8,128]{2,1,0:T(8,128)S(1)}, u32[]{:S(2)}, u32[]{:S(2)}) collective-permute-start(f32[32,8,128]{2,1,0:T(8,128)S(1)} %get-tuple-element.83.refs_2_), channel_id=1, source_target_pairs={{0,8},{1,9},{2,10},{3,11},{4,12},{5,13},{6,14},{7,15},{8,0},{9,1},... | collective-permute-start | bytes 393224 | tf_op jit(solution)/shard_map/ppermute | solution.py:557
  16.2 0.2 collective-permute-start.2
  16.4 6.8 %shard_map.116.refs_0_ = f32[16,4096]{1,0:T(8,128)S(1)} custom-call(bf16[48,4096]{1,0:T(8,128)(2,1)S(1)} %get-tuple-element.70.own_ref.refs_11_, bf16[4096,48]{1,0:T(8,128)(2,1)S(1)} %get-tuple-element.102.near_ref, bf16[32,4096]{1,0:T(8,128)(2,1)S(1)} %get-tuple-element.71.moment_ref, ...), custom_call_target="tpu_custom_call", output_to_operand_aliasing={{}: (4, {})} | custom-call | flops 6291456000 | bytes 1048576 | tf_op jit(solution)/shard_map/pallas_call | solution.py:542
  23.1 0.0 collective-permute-done.3.refs_3_
  23.1 0.0 collective-permute-done.2.refs_1_
  23.1 0.7 shard_map.117
  23.9 1.8 %collective-permute-start.5 = (f32[64,8,128]{2,1,0:T(8,128)S(1)}, f32[64,8,128]{2,1,0:T(8,128)S(1)}, u32[]{:S(2)}, u32[]{:S(2)}) collective-permute-start(f32[64,8,128]{2,1,0:T(8,128)S(1)} %get-tuple-element.91.refs_2_), channel_id=1, source_target_pairs={{0,2},{1,3},{2,0},{3,1},{4,6},{5,7},{6,4},{7,5},{8,10},{9,11},{10,... | collective-permute-start | bytes 786440 | tf_op jit(solution)/shard_map/ppermute | solution.py:557
  25.7 1.5 %collective-permute-start.4 = (f32[68,8,128]{2,1,0:T(8,128)S(1)}, f32[68,8,128]{2,1,0:T(8,128)S(1)}, u32[]{:S(2)}, u32[]{:S(2)}) collective-permute-start(f32[68,8,128]{2,1,0:T(8,128)S(1)} %get-tuple-element.89.refs_0_), channel_id=1, source_target_pairs={{0,4},{1,5},{2,6},{3,7},{4,0},{5,1},{6,2},{7,3},{8,12},{9,13},{10,... | collective-permute-start | bytes 835592 | tf_op jit(solution)/shard_map/ppermute | solution.py:557
  27.2 6.8 %shard_map.118.refs_0_ = f32[16,4096]{1,0:T(8,128)S(1)} custom-call(bf16[48,4096]{1,0:T(8,128)(2,1)S(1)} %get-tuple-element.70.own_ref.refs_11_, bf16[4096,48]{1,0:T(8,128)(2,1)S(1)} %get-tuple-element.102.near_ref, bf16[32,4096]{1,0:T(8,128)(2,1)S(1)} %get-tuple-element.71.moment_ref, ...), custom_call_target="tpu_custom_call", output_to_operand_aliasing={{}: (4, {})} | custom-call | flops 6291456000 | bytes 1048576 | tf_op jit(solution)/shard_map/pallas_call | solution.py:542
  34.0 0.0 collective-permute-done.5.refs_3_
  34.0 0.0 collective-permute-done.4.refs_1_
  34.0 0.2 shard_map.119
  34.2 0.6 collective-permute-start.7
  34.7 0.3 collective-permute-start.6
  35.0 11.2 %shard_map.120.refs_0_ = f32[16,4096]{1,0:T(8,128)S(1)} custom-call(bf16[48,4096]{1,0:T(8,128)(2,1)S(1)} %get-tuple-element.70.own_ref.refs_11_, bf16[4096,48]{1,0:T(8,128)(2,1)S(1)} %get-tuple-element.102.near_ref, bf16[32,4096]{1,0:T(8,128)(2,1)S(1)} %get-tuple-element.71.moment_ref, ...), custom_call_target="tpu_custom_call", output_to_operand_aliasing={{}: (4, {})} | custom-call | flops 6291456000 | bytes 1048576 | tf_op jit(solution)/shard_map/pallas_call | solution.py:542
  46.3 0.0 copy-start
  46.3 0.0 copy-start.1
  46.3 0.0 copy-start.2
  46.3 0.0 collective-permute-done.7.refs_5_
  46.3 0.8 collective-permute-done.6.refs_1_
  47.2 0.0 collective-permute-start.10
  47.2 0.5 collective-permute-start.11
  47.7 0.0 collective-permute-start.8
  47.7 0.5 collective-permute-start.9
  48.2 4.5 %shard_map.121.refs_14_ = f32[16,4096]{1,0:T(8,128)S(1)} custom-call(bf16[48,4096]{1,0:T(8,128)(2,1)S(1)} %get-tuple-element.70.own_ref.refs_11_, bf16[4096,48]{1,0:T(8,128)(2,1)S(1)} %get-tuple-element.102.near_ref, bf16[32,4096]{1,0:T(8,128)(2,1)S(1)} %get-tuple-element.71.moment_ref, ...), custom_call_target="tpu_custom_call", output_to_operand_aliasing={{}: (4, {})} | custom-call | flops 6291456000 | bytes 1048576 | tf_op jit(solution)/shard_map/pallas_call | solution.py:542
  52.7 0.0 collective-permute-done.10.refs_6_
  52.7 0.0 collective-permute-done.11.refs_7_
  52.7 0.0 collective-permute-done.8.refs_2_
  52.7 0.0 collective-permute-done.9.refs_3_
  52.7 0.0 copy-done
  52.8 0.0 copy-done.1
  52.8 0.0 copy-done.2
  52.8 26.3 %shard_map.122 = (f32[32,128]{1,0:T(8,128)}, f32[32,128]{1,0:T(8,128)}, f32[32,128]{1,0:T(8,128)S(1)}, f32[3,32,128]{2,1,0:T(8,128)S(1)}, s32[32,128]{1,0:T(8,128)S(1)}, /*index=5*/f32[1056,8,128]{2,1,0:T(8,128)S(1)}) custom-call(s32[1]{0:T(128)} %bitcast.me_ref, f32[136,8,128]{2,1,0:T(8,128)S(1)} %get-tuple-element.97.refs_0_, ...), custom_call_target="tpu_custom_call" | custom-call | tf_op jit(solution)/shard_map/pallas_call | solution.py:638
  79.1 2.6 %collective-permute-start.12 = (f32[32,128]{1,0:T(8,128)S(1)}, f32[32,128]{1,0:T(8,128)S(1)}, u32[]{:S(2)}, u32[]{:S(2)}) collective-permute-start(f32[32,128]{1,0:T(8,128)S(1)} %get-tuple-element.110.weight_ref.refs_0_), channel_id=1, source_target_pairs={{0,16},{1,17},{2,18},{3,19},{4,20},{5,21},{6,22},{7,23},{8,24},{9,... | collective-permute-start | bytes 49160 | tf_op jit(solution)/shard_map/ppermute | solution.py:557
  81.7 0.9 shard_map.123
  82.7 5.4 %shard_map.124.refs_0_ = f32[8,4096]{1,0:T(8,128)S(1)} custom-call(bf16[48,4096]{1,0:T(8,128)(2,1)S(1)} %get-tuple-element.108.own_ref.refs_8_, bf16[4096,48]{1,0:T(8,128)(2,1)S(1)} %get-tuple-element.126.near_ref, bf16[16,4096]{1,0:T(8,128)(2,1)S(1)} %get-tuple-element.109.moment_ref), custom_call_target="tpu_custom_call" | custom-call | flops 6291456000 | bytes 1048576 | tf_op jit(solution)/shard_map/pallas_call | solution.py:542
  88.1 0.0 collective-permute-done.12.refs_1_
  88.1 0.1 shard_map.125.refs_0_
  88.2 1.6 %collective-permute-start.13 = (f32[64,128]{1,0:T(8,128)S(1)}, f32[64,128]{1,0:T(8,128)S(1)}, u32[]{:S(2)}, u32[]{:S(2)}) collective-permute-start(f32[64,128]{1,0:T(8,128)S(1)} %shard_map.125.refs_0_), channel_id=1, source_target_pairs={{0,8},{1,9},{2,10},{3,11},{4,12},{5,13},{6,14},{7,15},{8,0},{9,1},... | collective-permute-start | bytes 98312 | tf_op jit(solution)/shard_map/ppermute | solution.py:557
  89.8 5.4 %shard_map.126.refs_0_ = f32[8,4096]{1,0:T(8,128)S(1)} custom-call(bf16[48,4096]{1,0:T(8,128)(2,1)S(1)} %get-tuple-element.108.own_ref.refs_8_, bf16[4096,48]{1,0:T(8,128)(2,1)S(1)} %get-tuple-element.126.near_ref, bf16[16,4096]{1,0:T(8,128)(2,1)S(1)} %get-tuple-element.109.moment_ref, f32[8,4096]{1,0:T(8,128)S(1)} %shard_map.124.refs_0_), custom_call_target="tpu_custom_call", output_to_operand_aliasing={{}: (3, {})} | custom-call | flops 6291456000 | bytes 1048576 | tf_op jit(solution)/shard_map/pallas_call | solution.py:542
  95.3 0.0 collective-permute-done.13.refs_1_
  95.3 0.1 shard_map.127.refs_0_
  95.4 1.6 %collective-permute-start.14 = (f32[128,128]{1,0:T(8,128)S(1)}, f32[128,128]{1,0:T(8,128)S(1)}, u32[]{:S(2)}, u32[]{:S(2)}) collective-permute-start(f32[128,128]{1,0:T(8,128)S(1)} %shard_map.127.refs_0_), channel_id=1, source_target_pairs={{0,4},{1,5},{2,6},{3,7},{4,0},{5,1},{6,2},{7,3},{8,12},{9,13},{10,... | collective-permute-start | bytes 196616 | tf_op jit(solution)/shard_map/ppermute | solution.py:557
  97.0 5.4 %shard_map.128.refs_0_ = f32[8,4096]{1,0:T(8,128)S(1)} custom-call(bf16[48,4096]{1,0:T(8,128)(2,1)S(1)} %get-tuple-element.108.own_ref.refs_8_, bf16[4096,48]{1,0:T(8,128)(2,1)S(1)} %get-tuple-element.126.near_ref, bf16[16,4096]{1,0:T(8,128)(2,1)S(1)} %get-tuple-element.109.moment_ref, f32[8,4096]{1,0:T(8,128)S(1)} %shard_map.126.refs_0_), custom_call_target="tpu_custom_call", output_to_operand_aliasing={{}: (3, {})} | custom-call | flops 6291456000 | bytes 1048576 | tf_op jit(solution)/shard_map/pallas_call | solution.py:542
  102.4 0.0 collective-permute-done.14.refs_1_
  102.4 0.2 shard_map.129.refs_0_
  102.6 1.1 collective-permute-start.15
  103.7 9.0 %shard_map.130.refs_0_ = f32[8,4096]{1,0:T(8,128)S(1)} custom-call(bf16[48,4096]{1,0:T(8,128)(2,1)S(1)} %get-tuple-element.108.own_ref.refs_8_, bf16[4096,48]{1,0:T(8,128)(2,1)S(1)} %get-tuple-element.126.near_ref, bf16[16,4096]{1,0:T(8,128)(2,1)S(1)} %get-tuple-element.109.moment_ref, f32[8,4096]{1,0:T(8,128)S(1)} %shard_map.128.refs_0_), custom_call_target="tpu_custom_call", output_to_operand_aliasing={{}: (3, {})} | custom-call | flops 6291456000 | bytes 1048576 | tf_op jit(solution)/shard_map/pallas_call | solution.py:542
  112.7 0.0 collective-permute-done.15.refs_1_
  112.7 0.1 collective-permute-start.16
  112.8 0.5 collective-permute-start.17
  113.3 3.6 %shard_map.131.refs_11_ = f32[8,4096]{1,0:T(8,128)S(1)} custom-call(bf16[48,4096]{1,0:T(8,128)(2,1)S(1)} %get-tuple-element.108.own_ref.refs_8_, bf16[4096,48]{1,0:T(8,128)(2,1)S(1)} %get-tuple-element.126.near_ref, bf16[16,4096]{1,0:T(8,128)(2,1)S(1)} %get-tuple-element.109.moment_ref, f32[8,4096]{1,0:T(8,128)S(1)} %shard_map.130.refs_0_), custom_call_target="tpu_custom_call", output_to_operand_aliasing={{}: (3, {})} | custom-call | flops 6291456000 | bytes 1048576 | tf_op jit(solution)/shard_map/pallas_call | solution.py:542
  116.9 0.0 collective-permute-done.16.refs_2_
  116.9 0.0 collective-permute-done.17.refs_3_
  117.0 22.0 %shard_map.132 = f32[3,32,128]{2,1,0:T(8,128)} custom-call(s32[1]{0:T(128)} %bitcast.me_ref, f32[256,128]{1,0:T(8,128)S(1)} %shard_map.129.refs_0_, f32[256,128]{1,0:T(8,128)S(1)} %collective-permute-done.15.refs_1_, f32[256,128]{1,0:T(8,128)S(1)} %collective-permute-done.16.refs_2_, f32[256,128]{1,0:T(8,128)S(1)} %collective-permute-done.17.refs_3_, ...), custom_call_target="tpu_custom_call" | custom-call | tf_op jit(solution)/shard_map/pallas_call | solution.py:682
  (2 shorter events, 0.0 us)
Async XLA Ops:
  1.6 12.2 %collective-permute-start.1 = (f32[16,8,128]{2,1,0:T(8,128)S(1)}, f32[16,8,128]{2,1,0:T(8,128)S(1)}, u32[]{:S(2)}, u32[]{:S(2)}) collective-permute-start(f32[16,8,128]{2,1,0:T(8,128)S(1)} %get-tuple-element.75.refs_2_), channel_id=1, source_target_pairs={{0,16},{1,17},{2,18},{3,19},{4,20},{5,21},{6,22},{7,23},{8,24},{9,... | collective-permute-start | bytes 196616 | tf_op jit(solution)/shard_map/ppermute | solution.py:557
  5.7 8.1 %collective-permute-start = (f32[17,8,128]{2,1,0:T(8,128)S(1)}, f32[17,8,128]{2,1,0:T(8,128)S(1)}, u32[]{:S(2)}, u32[]{:S(2)}) collective-permute-start(f32[17,8,128]{2,1,0:T(8,128)S(1)} %get-tuple-element.73.refs_0_), channel_id=1, source_target_pairs={{0,16},{1,17},{2,18},{3,19},{4,20},{5,21},{6,22},{7,23},{8,24},{9,... | collective-permute-start | bytes 208904 | tf_op jit(solution)/shard_map/ppermute | solution.py:557
  14.3 8.9 %collective-permute-start.3 = (f32[32,8,128]{2,1,0:T(8,128)S(1)}, f32[32,8,128]{2,1,0:T(8,128)S(1)}, u32[]{:S(2)}, u32[]{:S(2)}) collective-permute-start(f32[32,8,128]{2,1,0:T(8,128)S(1)} %get-tuple-element.83.refs_2_), channel_id=1, source_target_pairs={{0,8},{1,9},{2,10},{3,11},{4,12},{5,13},{6,14},{7,15},{8,0},{9,1},... | collective-permute-start | bytes 393224 | tf_op jit(solution)/shard_map/ppermute | solution.py:557
  16.2 7.0 %collective-permute-start.2 = (f32[34,8,128]{2,1,0:T(8,128)S(1)}, f32[34,8,128]{2,1,0:T(8,128)S(1)}, u32[]{:S(2)}, u32[]{:S(2)}) collective-permute-start(f32[34,8,128]{2,1,0:T(8,128)S(1)} %get-tuple-element.81.refs_0_), channel_id=1, source_target_pairs={{0,8},{1,9},{2,10},{3,11},{4,12},{5,13},{6,14},{7,15},{8,0},{9,1},... | collective-permute-start | bytes 417800 | tf_op jit(solution)/shard_map/ppermute | solution.py:557
  23.9 10.1 %collective-permute-start.5 = (f32[64,8,128]{2,1,0:T(8,128)S(1)}, f32[64,8,128]{2,1,0:T(8,128)S(1)}, u32[]{:S(2)}, u32[]{:S(2)}) collective-permute-start(f32[64,8,128]{2,1,0:T(8,128)S(1)} %get-tuple-element.91.refs_2_), channel_id=1, source_target_pairs={{0,2},{1,3},{2,0},{3,1},{4,6},{5,7},{6,4},{7,5},{8,10},{9,11},{10,... | collective-permute-start | bytes 786440 | tf_op jit(solution)/shard_map/ppermute | solution.py:557
  25.7 8.3 %collective-permute-start.4 = (f32[68,8,128]{2,1,0:T(8,128)S(1)}, f32[68,8,128]{2,1,0:T(8,128)S(1)}, u32[]{:S(2)}, u32[]{:S(2)}) collective-permute-start(f32[68,8,128]{2,1,0:T(8,128)S(1)} %get-tuple-element.89.refs_0_), channel_id=1, source_target_pairs={{0,4},{1,5},{2,6},{3,7},{4,0},{5,1},{6,2},{7,3},{8,12},{9,13},{10,... | collective-permute-start | bytes 835592 | tf_op jit(solution)/shard_map/ppermute | solution.py:557
  34.2 12.1 %collective-permute-start.7 = (f32[128,8,128]{2,1,0:T(8,128)S(1)}, f32[128,8,128]{2,1,0:T(8,128)S(1)}, u32[]{:S(2)}, u32[]{:S(2)}) collective-permute-start(f32[128,8,128]{2,1,0:T(8,128)S(1)} %get-tuple-element.99.refs_4_), channel_id=1, source_target_pairs={{0,4},{1,5},{2,6},{3,7},{4,0},{5,1},{6,2},{7,3},{8,12},{9,13},{10,... | collective-permute-start | bytes 1572872 | tf_op jit(solution)/shard_map/ppermute | solution.py:557
  34.7 12.4 %collective-permute-start.6 = (f32[136,8,128]{2,1,0:T(8,128)S(1)}, f32[136,8,128]{2,1,0:T(8,128)S(1)}, u32[]{:S(2)}, u32[]{:S(2)}) collective-permute-start(f32[136,8,128]{2,1,0:T(8,128)S(1)} %get-tuple-element.97.refs_0_), channel_id=1, source_target_pairs={{0,2},{1,3},{2,0},{3,1},{4,6},{5,7},{6,4},{7,5},{8,10},{9,11},{10,... | collective-permute-start | bytes 1671176 | tf_op jit(solution)/shard_map/ppermute | solution.py:557
  46.3 6.5 %copy-start = (s32[32,16]{0,1:T(8,128)S(1)}, s32[32,16]{0,1:T(8,128)}, u32[]{:S(2)}) copy-start(s32[32,16]{0,1:T(8,128)} %param.15) | copy-start | bytes 6148
  46.3 6.5 %copy-start.1 = (f32[32,128]{1,0:T(8,128)S(1)}, f32[32,128]{1,0:T(8,128)}, u32[]{:S(2)}) copy-start(f32[32,128]{1,0:T(8,128)} %refs_10_.1) | copy-start | bytes 49156
  46.3 6.5 %copy-start.2 = (s32[2,32]{1,0:T(2,128)S(1)}, s32[2,32]{1,0:T(2,128)}, u32[]{:S(2)}) copy-start(s32[2,32]{1,0:T(2,128)} %constant.10.clone.refs_9_) | copy-start | bytes 772
  47.2 5.5 %collective-permute-start.10 = (f32[128,8,128]{2,1,0:T(8,128)S(1)}, f32[128,8,128]{2,1,0:T(8,128)S(1)}, u32[]{:S(2)}, u32[]{:S(2)}) collective-permute-start(f32[128,8,128]{2,1,0:T(8,128)S(1)} %get-tuple-element.99.refs_4_), channel_id=1, source_target_pairs={{0,1},{1,0},{2,3},{3,2},{4,5},{5,4},{6,7},{7,6},{8,9},{9,8},{10,11... | collective-permute-start | bytes 1572872 | tf_op jit(solution)/shard_map/ppermute | solution.py:557
  47.2 5.5 %collective-permute-start.11 = (f32[128,8,128]{2,1,0:T(8,128)S(1)}, f32[128,8,128]{2,1,0:T(8,128)S(1)}, u32[]{:S(2)}, u32[]{:S(2)}) collective-permute-start(f32[128,8,128]{2,1,0:T(8,128)S(1)} %collective-permute-done.7.refs_5_), channel_id=1, source_target_pairs={{0,1},{1,0},{2,3},{3,2},{4,5},{5,4},{6,7},{7,6},{8,9},{9,8},{10,11... | collective-permute-start | bytes 1572872 | tf_op jit(solution)/shard_map/ppermute | solution.py:557
  47.7 5.0 %collective-permute-start.8 = (f32[136,8,128]{2,1,0:T(8,128)S(1)}, f32[136,8,128]{2,1,0:T(8,128)S(1)}, u32[]{:S(2)}, u32[]{:S(2)}) collective-permute-start(f32[136,8,128]{2,1,0:T(8,128)S(1)} %get-tuple-element.97.refs_0_), channel_id=1, source_target_pairs={{0,1},{1,0},{2,3},{3,2},{4,5},{5,4},{6,7},{7,6},{8,9},{9,8},{10,11... | collective-permute-start | bytes 1671176 | tf_op jit(solution)/shard_map/ppermute | solution.py:557
  47.7 5.1 %collective-permute-start.9 = (f32[136,8,128]{2,1,0:T(8,128)S(1)}, f32[136,8,128]{2,1,0:T(8,128)S(1)}, u32[]{:S(2)}, u32[]{:S(2)}) collective-permute-start(f32[136,8,128]{2,1,0:T(8,128)S(1)} %collective-permute-done.6.refs_1_), channel_id=1, source_target_pairs={{0,1},{1,0},{2,3},{3,2},{4,5},{5,4},{6,7},{7,6},{8,9},{9,8},{10,11... | collective-permute-start | bytes 1671176 | tf_op jit(solution)/shard_map/ppermute | solution.py:557
  79.1 9.0 %collective-permute-start.12 = (f32[32,128]{1,0:T(8,128)S(1)}, f32[32,128]{1,0:T(8,128)S(1)}, u32[]{:S(2)}, u32[]{:S(2)}) collective-permute-start(f32[32,128]{1,0:T(8,128)S(1)} %get-tuple-element.110.weight_ref.refs_0_), channel_id=1, source_target_pairs={{0,16},{1,17},{2,18},{3,19},{4,20},{5,21},{6,22},{7,23},{8,24},{9,... | collective-permute-start | bytes 49160 | tf_op jit(solution)/shard_map/ppermute | solution.py:557
  88.2 7.1 %collective-permute-start.13 = (f32[64,128]{1,0:T(8,128)S(1)}, f32[64,128]{1,0:T(8,128)S(1)}, u32[]{:S(2)}, u32[]{:S(2)}) collective-permute-start(f32[64,128]{1,0:T(8,128)S(1)} %shard_map.125.refs_0_), channel_id=1, source_target_pairs={{0,8},{1,9},{2,10},{3,11},{4,12},{5,13},{6,14},{7,15},{8,0},{9,1},... | collective-permute-start | bytes 98312 | tf_op jit(solution)/shard_map/ppermute | solution.py:557
  95.4 7.0 %collective-permute-start.14 = (f32[128,128]{1,0:T(8,128)S(1)}, f32[128,128]{1,0:T(8,128)S(1)}, u32[]{:S(2)}, u32[]{:S(2)}) collective-permute-start(f32[128,128]{1,0:T(8,128)S(1)} %shard_map.127.refs_0_), channel_id=1, source_target_pairs={{0,4},{1,5},{2,6},{3,7},{4,0},{5,1},{6,2},{7,3},{8,12},{9,13},{10,... | collective-permute-start | bytes 196616 | tf_op jit(solution)/shard_map/ppermute | solution.py:557
  102.6 10.1 %collective-permute-start.15 = (f32[256,128]{1,0:T(8,128)S(1)}, f32[256,128]{1,0:T(8,128)S(1)}, u32[]{:S(2)}, u32[]{:S(2)}) collective-permute-start(f32[256,128]{1,0:T(8,128)S(1)} %shard_map.129.refs_0_), channel_id=1, source_target_pairs={{0,2},{1,3},{2,0},{3,1},{4,6},{5,7},{6,4},{7,5},{8,10},{9,11},{10,... | collective-permute-start | bytes 393224 | tf_op jit(solution)/shard_map/ppermute | solution.py:557
  112.7 4.2 %copy-start.3 = (s32[32]{0:T(128)S(1)}, s32[32]{0:T(128)}, u32[]{:S(2)}) copy-start(s32[32]{0:T(128)} %refs_6_.1) | copy-start | bytes 388
  112.7 4.2 %collective-permute-start.16 = (f32[256,128]{1,0:T(8,128)S(1)}, f32[256,128]{1,0:T(8,128)S(1)}, u32[]{:S(2)}, u32[]{:S(2)}) collective-permute-start(f32[256,128]{1,0:T(8,128)S(1)} %shard_map.129.refs_0_), channel_id=1, source_target_pairs={{0,1},{1,0},{2,3},{3,2},{4,5},{5,4},{6,7},{7,6},{8,9},{9,8},{10,11... | collective-permute-start | bytes 393224 | tf_op jit(solution)/shard_map/ppermute | solution.py:557
  112.8 4.1 %collective-permute-start.17 = (f32[256,128]{1,0:T(8,128)S(1)}, f32[256,128]{1,0:T(8,128)S(1)}, u32[]{:S(2)}, u32[]{:S(2)}) collective-permute-start(f32[256,128]{1,0:T(8,128)S(1)} %collective-permute-done.15.refs_1_), channel_id=1, source_target_pairs={{0,1},{1,0},{2,3},{3,2},{4,5},{5,4},{6,7},{7,6},{8,9},{9,8},{10,11... | collective-permute-start | bytes 393224 | tf_op jit(solution)/shard_map/ppermute | solution.py:557

commit v6 on v5

--- a/solution.py
+++ b/solution.py
@@ -82,16 +82,14 @@
     return jnp.broadcast_to(columns[:, number : number + 1], (LANES, LANES))
 
 
-def assemble_kernel(devices, capacity, stack_ref, fields_ref, first_ref, second_ref):
+def assemble_kernel(devices, capacity, stack_ref, fields_ref, payload_ref):
     blocks = fields_ref.shape[0]
-    half = second_ref.shape[0]
     for row in range(6):
         fields_ref[:, row, :] = stack_ref[row]
     fields_ref[:, 6, :] = jnp.sqrt(jnp.sqrt(stack_ref[6]))
     smooth = stack_ref[7]
     fields_ref[:, 7, :] = 1.0 / (smooth * smooth)
-    first_ref[0 : blocks - half] = fields_ref[0 : blocks - half]
-    second_ref[...] = fields_ref[blocks - half :]
+    payload_ref[0:blocks] = fields_ref[...]
     each = LANES // capacity
     for number, start in enumerate(range(0, devices, 8 * each)):
         lines = [
@@ -99,7 +97,7 @@
             for row in range(start, min(start + 8 * each, devices), 8)
         ]
         line = jnp.concatenate(lines, axis=1)
-        first_ref[blocks - half + number, :, 0 : line.shape[1]] = line
+        payload_ref[blocks + number, :, 0 : line.shape[1]] = line
 
 
 def prepare_kernel(fields_ref, near_ref, moment_ref, root_ref, own_ref, centre_ref):
@@ -259,19 +257,17 @@
 
 
 def own_tables(gathered, line_ref, step, place_ref, me, capacity, blocks):
-    half = blocks // 2
     line = me // 8 * capacity // LANES
     devices = line_ref.shape[0]
     chosen = lax.broadcasted_iota(jnp.int32, (8, LANES), 0) == me % 8
     for sender in range(devices):
         first = place_ref[0, sender ^ me]
         second = place_ref[1, sender ^ me]
-        block = gathered[first * step + half + line]
+        block = gathered[first * step + blocks + line]
         row = jnp.sum(jnp.where(chosen, block, 0.0), axis=0, keepdims=True).astype(jnp.int32)
-        place = jnp.where(
-            row < half, first * step + row, devices * step + second * half + row - half
+        line_ref[sender : sender + 1, :] = (
+            first * step + row + ((second * blocks + row) << 16)
         )
-        line_ref[sender : sender + 1, :] = place + ((first * blocks + row) << 16)
 
 
 def remote_first_kernel(capacity, extra, me_ref, *refs):
@@ -292,7 +288,7 @@
         copy.wait()
     centre = centre_ref[...]
     me = me_ref[0]
-    own_tables(gathered, line_ref, blocks // 2 + extra, place_ref, me, capacity, blocks)
+    own_tables(gathered, line_ref, blocks + extra, place_ref, me, capacity, blocks)
     copy = pltpu.make_async_copy(line_ref, tables_ref, table_semaphore)
     copy.start()
     copy.wait()
@@ -428,20 +424,13 @@
     in_turn(blocks // 2, partners, take, build, sums)
 
 
-def join_kernel(*refs):
-    count = (len(refs) - 1) // 3
+def join_kernel(parts, *refs):
+    pieces, outs, semaphore = refs[: sum(parts)], refs[sum(parts) : -1], refs[-1]
     copies = []
-    for number in range(count):
-        out = refs[2 * count + number]
-        start = 0
-        for part in range(2):
-            piece = refs[2 * number + part]
-            copy = pltpu.make_async_copy(
-                piece, out.at[pl.ds(start, piece.shape[0])], refs[-1].at[2 * number + part]
-            )
-            copy.start()
-            copies.append(copy)
-            start += piece.shape[0]
+    first = 0
+    for out, count in zip(outs, parts):
+        copies += fetch(pieces[first : first + count], out, semaphore.at[pl.ds(first, count)])
+        first += count
     for copy in copies:
         copy.wait()
 
@@ -466,11 +455,13 @@
     return pltpu.CompilerParams(vmem_limit_bytes=mebibytes * 2**20)
 
 
-def join(*pairs):
-    flat = [item for pair in pairs for item in pair]
-    outs = [shape(2 * pair[0].shape[0], *pair[0].shape[1:]) for pair in pairs]
+def join(*groups):
+    flat = [item for group in groups for item in group]
+    outs = [
+        shape(sum(item.shape[0] for item in group), *group[0].shape[1:]) for group in groups
+    ]
     return pl.pallas_call(
-        join_kernel,
+        functools.partial(join_kernel, [len(group) for group in groups]),
         out_shape=outs,
         in_specs=in_any(len(flat)),
         out_specs=in_any(len(outs)),
@@ -481,16 +472,14 @@
 
 def assemble(extra, stack, devices, capacity):
     blocks = stack.shape[1]
-    half = blocks // 2
     return pl.pallas_call(
         functools.partial(assemble_kernel, devices, capacity),
         out_shape=[
             shape(blocks, 8, LANES),
-            shape(half + extra, 8, LANES),
-            shape(blocks - half, 8, LANES),
+            shape(blocks + extra, 8, LANES),
         ],
         in_specs=in_vmem(1),
-        out_specs=in_vmem(3),
+        out_specs=in_vmem(2),
         compiler_params=room(8),
     )(stack)
 
@@ -564,9 +553,14 @@
     return table
 
 
-def shares(tiles, stages):
-    weights = [3] * (stages - 2) + [5, 2]
-    cuts = [round(tiles * sum(weights[:k]) / sum(weights)) for k in range(stages + 1)]
+def combinations(group):
+    return group if len(group) == 1 else [group[0], group[1], group[0] | group[1]]
+
+
+def shares(tiles, weights):
+    cuts = [
+        round(tiles * sum(weights[:stage]) / sum(weights)) for stage in range(len(weights) + 1)
+    ]
     return list(zip(cuts[:-1], cuts[1:]))
 
 
@@ -601,30 +595,49 @@
         after = height - start - layer.shape[0]
         stack = stack + jnp.pad(layer, ((start, after), (0, 0), (0, 0)))
         start += layer.shape[0]
-    fields, first, second = assemble(extra, stack, devices, capacity)
-    bits = [1 << k for k in reversed(range(devices.bit_length() - 1))]
-    order0 = list(bits)
-    order1 = list(bits)
-    order1[-3:-1] = reversed(order1[-3:-1])
-    place = jnp.asarray(np.stack([places(order0, devices), places(order1, devices)]))
+    fields, payload = assemble(extra, stack, devices, capacity)
+    bits = [1 << k for k in range(devices.bit_length() - 1)]
+    groups = [bits[k : k + 2] for k in range(3, len(bits), 2)][::-1]
+    split = groups[-1][-1]
+    far = [bit for group in groups for bit in group]
+    near_first = [bit for bit in far if bit != split] + [bits[2], bits[1], bits[0]]
+    near_second = [bit for bit in far if bit != split] + [bits[1], bits[2], bits[0]]
+    in_second = np.arange(devices) & split > 0
+    payload_place = np.where(
+        in_second, devices // 2 + places(near_second, devices), places(near_first, devices)
+    )
+    place = jnp.asarray(
+        np.stack([payload_place, places(far + [bits[2], bits[1], bits[0]], devices)]), jnp.int32
+    )
     tiles = particles // TILE
-    stages = len(bits)
+    stages = len(groups) + 3
+    far_stages = [5] * len(groups)
 
     near, moment, root, own, centre = prepare(fields)
     sums = None
-    first, second = [first], [second]
-    for number, (start, stop) in enumerate(shares(tiles, stages)):
-        first_in = [swap(item, order0[number], devices) for item in first]
-        second_in = [swap(item, order1[number], devices) for item in second]
+    first, second = [payload], []
+    for number, (start, stop) in enumerate(shares(tiles, far_stages + [3, 6, 2])):
+        if number < len(groups):
+            group = groups[number]
+            first += [swap(payload, bit, devices) for bit in combinations(group)]
+        else:
+            last = number - len(groups)
+            first += [swap(item, [bits[2], bits[1], bits[0]][last], devices) for item in first]
+            second += [swap(item, [bits[1], bits[2], bits[0]][last], devices) for item in second]
         if stop > start:
             sums = local_pass(
                 local_first_kernel, start, stop - start, own, (near, moment, root), sums
             )
-        first += first_in
-        second += second_in
         if number < stages - 1:
             first, second, near, sums = lax.optimization_barrier((first, second, near, sums))
-        if number < stages - 2:
+        if number < len(groups) - 1:
+            (payload,) = join(first)
+            first = [payload]
+        elif number == len(groups) - 1:
+            middle = len(first) // 2
+            first, second = join(first[:middle], first[middle:])
+            first, second = [first], [second]
+        elif number < stages - 2:
             first, second = join(first, second)
             first, second = [first], [second]
     pieces = (*first, *second)
@@ -668,15 +681,16 @@
     near2, moment2, own2 = prepare_second(fields, centre, weight)
     sums = None
     weights = [weight]
-    for number, (start, stop) in enumerate(shares(tiles, stages)):
-        weights += [swap(item, order0[number], devices) for item in weights]
+    order = far + [bits[2], bits[1], bits[0]]
+    for number, (start, stop) in enumerate(shares(tiles, [3] * (len(order) - 2) + [5, 2])):
+        weights += [swap(item, order[number], devices) for item in weights]
         if stop > start:
             sums = local_pass(
                 local_second_kernel, start, stop - start, own2, (near2, moment2), sums
             )
-        if number < stages - 1:
+        if number < len(order) - 1:
             weights, near2, sums = lax.optimization_barrier((weights, near2, sums))
-        if number < stages - 2:
+        if number < len(order) - 2:
             weights = list(join(weights))
 
     acceleration = pl.pallas_call(

time: 139 us -> 139 us (level)
    ppermute x18 -> x17, starting transfers between devices: 19 us -> 19.2 us  [swap(): return lax.ppermute(value, 'dom', [(i, i ^ bit) for i in range(devices)])]
    pallas_call x10 -> x9, Pallas kernels: 64.9 us -> 65 us  [local_pass(): pl.pallas_call(kernel, grid=(count,), in_specs=in_specs, out_specs=pl.Blo...]
  transfers between devices with their start and end apart: 18 -> 17, of which waited for: 1 -> 0; matrix products, arithmetic and copies ran while one was open for 0% -> 0% of each run, Pallas kernels for 48% -> 49%
where the time goes in v6:
time: 139 us; the launch traced here: 138 us
  Pallas kernels  117 us (84%)
  starting transfers between devices  19.2 us (14%)
    pallas_call x9, Pallas kernels, local_pass(): pl.pallas_call(kernel, grid=(count,), in_specs=in_specs, out_specs=pl.Blo...  65 us
    pallas_call x1, Pallas kernels, per_device(): pl.pallas_call(functools.partial(remote_first_kernel, capacity, extra), o...  26.5 us
    pallas_call x1, Pallas kernels, per_device(): pl.pallas_call(functools.partial(remote_second_kernel, capacity), out_sha...  22 us
    ppermute x17, starting transfers between devices, swap(): return lax.ppermute(value, 'dom', [(i, i ^ bit) for i in range(devices)])  19.2 us
  transfers between devices with their start and end apart: 17, of which 0 were waited for; matrix products, arithmetic and copies ran while one was open for 0% of the time, Pallas kernels for 49%

profile of v6, /device:TPU:0, one launch (start us, length us, event | category | flops | bytes accessed | tf_op | source)
XLA Modules:
  0.0 138.3 jit_solution(8152309154870349774)
XLA Ops:
  0.6 0.9 pad_add_fusion.stack_ref
  1.5 0.1 shard_map.112
  1.6 5.1 %collective-permute-start.2 = (f32[33,8,128]{2,1,0:T(8,128)S(1)}, f32[33,8,128]{2,1,0:T(8,128)S(1)}, u32[]{:S(2)}, u32[]{:S(2)}) collective-permute-start(f32[33,8,128]{2,1,0:T(8,128)S(1)} %get-tuple-element.63.refs_0_), channel_id=1, source_target_pairs={{0,24},{1,25},{2,26},{3,27},{4,28},{5,29},{6,30},{7,31},{8,16},{9,... | collective-permute-start | bytes 405512 | tf_op jit(solution)/shard_map/ppermute | solution.py:546
  6.7 0.0 collective-permute-start.1
  6.7 0.6 collective-permute-start
  7.4 1.2 shard_map.113
  8.6 11.3 %shard_map.114.refs_0_ = f32[16,4096]{1,0:T(8,128)S(1)} custom-call(bf16[48,4096]{1,0:T(8,128)(2,1)S(1)} %get-tuple-element.60.own_ref.refs_11_, bf16[4096,48]{1,0:T(8,128)(2,1)S(1)} %get-tuple-element.84.near_ref, bf16[32,4096]{1,0:T(8,128)(2,1)S(1)} %get-tuple-element.61.moment_ref, f32[128,32]{1,0:T(8,128)S(1)} %get-tuple-element.62.root_ref), custom_call_target="tpu_custom_call" | custom-call | flops 6291456000 | bytes 1048576 | tf_op jit(solution)/shard_map/pallas_call | solution.py:531
  19.9 0.0 collective-permute-done.2.refs_3_
  19.9 0.0 collective-permute-done.1.refs_2_
  20.0 0.0 collective-permute-done.refs_1_
  20.0 0.7 shard_map.115
  20.7 1.7 %collective-permute-start.3 = (f32[66,8,128]{2,1,0:T(8,128)S(1)}, f32[66,8,128]{2,1,0:T(8,128)S(1)}, u32[]{:S(2)}, u32[]{:S(2)}) collective-permute-start(f32[66,8,128]{2,1,0:T(8,128)S(1)} %get-tuple-element.71.refs_0_), channel_id=1, source_target_pairs={{0,4},{1,5},{2,6},{3,7},{4,0},{5,1},{6,2},{7,3},{8,12},{9,13},{10,... | collective-permute-start | bytes 811016 | tf_op jit(solution)/shard_map/ppermute | solution.py:546
  22.4 1.5 %collective-permute-start.4 = (f32[66,8,128]{2,1,0:T(8,128)S(1)}, f32[66,8,128]{2,1,0:T(8,128)S(1)}, u32[]{:S(2)}, u32[]{:S(2)}) collective-permute-start(f32[66,8,128]{2,1,0:T(8,128)S(1)} %get-tuple-element.73.refs_2_), channel_id=1, source_target_pairs={{0,2},{1,3},{2,0},{3,1},{4,6},{5,7},{6,4},{7,5},{8,10},{9,11},{10,... | collective-permute-start | bytes 811016 | tf_op jit(solution)/shard_map/ppermute | solution.py:546
  23.9 6.8 %shard_map.116.refs_0_ = f32[16,4096]{1,0:T(8,128)S(1)} custom-call(bf16[48,4096]{1,0:T(8,128)(2,1)S(1)} %get-tuple-element.60.own_ref.refs_11_, bf16[4096,48]{1,0:T(8,128)(2,1)S(1)} %get-tuple-element.84.near_ref, bf16[32,4096]{1,0:T(8,128)(2,1)S(1)} %get-tuple-element.61.moment_ref, ...), custom_call_target="tpu_custom_call", output_to_operand_aliasing={{}: (4, {})} | custom-call | flops 6291456000 | bytes 1048576 | tf_op jit(solution)/shard_map/pallas_call | solution.py:531
  30.7 0.0 collective-permute-done.3.refs_1_
  30.7 0.0 collective-permute-done.4.refs_3_
  30.7 0.2 shard_map.117
  30.9 0.6 collective-permute-start.5
  31.5 0.4 collective-permute-start.6
  31.9 13.5 %shard_map.118.refs_0_ = f32[16,4096]{1,0:T(8,128)S(1)} custom-call(bf16[48,4096]{1,0:T(8,128)(2,1)S(1)} %get-tuple-element.60.own_ref.refs_11_, bf16[4096,48]{1,0:T(8,128)(2,1)S(1)} %get-tuple-element.84.near_ref, bf16[32,4096]{1,0:T(8,128)(2,1)S(1)} %get-tuple-element.61.moment_ref, ...), custom_call_target="tpu_custom_call", output_to_operand_aliasing={{}: (4, {})} | custom-call | flops 6291456000 | bytes 1048576 | tf_op jit(solution)/shard_map/pallas_call | solution.py:531
  45.4 0.0 copy-start
  45.4 0.0 copy-start.1
  45.5 0.0 copy-start.2
  45.5 0.0 collective-permute-done.5.refs_1_
  45.5 0.0 collective-permute-done.6.refs_5_
  45.5 0.1 collective-permute-start.7
  45.6 0.5 collective-permute-start.8
  46.1 0.1 collective-permute-start.9
  46.1 0.4 collective-permute-start.10
  46.6 4.5 %shard_map.119.refs_14_ = f32[16,4096]{1,0:T(8,128)S(1)} custom-call(bf16[48,4096]{1,0:T(8,128)(2,1)S(1)} %get-tuple-element.60.own_ref.refs_11_, bf16[4096,48]{1,0:T(8,128)(2,1)S(1)} %get-tuple-element.84.near_ref, bf16[32,4096]{1,0:T(8,128)(2,1)S(1)} %get-tuple-element.61.moment_ref, ...), custom_call_target="tpu_custom_call", output_to_operand_aliasing={{}: (4, {})} | custom-call | flops 6291456000 | bytes 1048576 | tf_op jit(solution)/shard_map/pallas_call | solution.py:531
  51.1 0.0 collective-permute-done.7.refs_2_
  51.1 0.0 collective-permute-done.8.refs_3_
  51.1 0.0 collective-permute-done.9.refs_6_
  51.1 0.0 collective-permute-done.10.refs_7_
  51.1 0.0 copy-done
  51.2 0.0 copy-done.1
  51.2 0.0 copy-done.2
  51.2 26.5 %shard_map.120 = (f32[32,128]{1,0:T(8,128)}, f32[32,128]{1,0:T(8,128)}, f32[32,128]{1,0:T(8,128)S(1)}, f32[3,32,128]{2,1,0:T(8,128)S(1)}, s32[32,128]{1,0:T(8,128)S(1)}, /*index=5*/f32[1056,8,128]{2,1,0:T(8,128)S(1)}) custom-call(s32[1]{0:T(128)} %bitcast.me_ref, f32[132,8,128]{2,1,0:T(8,128)S(1)} %get-tuple-element.79.refs_0_, ...), custom_call_target="tpu_custom_call" | custom-call | tf_op jit(solution)/shard_map/pallas_call | solution.py:651
  77.6 1.4 %collective-permute-start.11 = (f32[32,128]{1,0:T(8,128)S(1)}, f32[32,128]{1,0:T(8,128)S(1)}, u32[]{:S(2)}, u32[]{:S(2)}) collective-permute-start(f32[32,128]{1,0:T(8,128)S(1)} %get-tuple-element.92.weight_ref.refs_0_), channel_id=1, source_target_pairs={{0,8},{1,9},{2,10},{3,11},{4,12},{5,13},{6,14},{7,15},{8,0},{9,1},... | collective-permute-start | bytes 49160 | tf_op jit(solution)/shard_map/ppermute | solution.py:546
  79.1 0.9 shard_map.121
  80.0 5.4 %shard_map.122.refs_0_ = f32[8,4096]{1,0:T(8,128)S(1)} custom-call(bf16[48,4096]{1,0:T(8,128)(2,1)S(1)} %get-tuple-element.90.own_ref.refs_8_, bf16[4096,48]{1,0:T(8,128)(2,1)S(1)} %get-tuple-element.108.near_ref, bf16[16,4096]{1,0:T(8,128)(2,1)S(1)} %get-tuple-element.91.moment_ref), custom_call_target="tpu_custom_call" | custom-call | flops 6291456000 | bytes 1048576 | tf_op jit(solution)/shard_map/pallas_call | solution.py:531
  85.5 0.0 collective-permute-done.11.refs_1_
  85.5 0.1 shard_map.123.refs_0_
  85.6 2.9 %collective-permute-start.12 = (f32[64,128]{1,0:T(8,128)S(1)}, f32[64,128]{1,0:T(8,128)S(1)}, u32[]{:S(2)}, u32[]{:S(2)}) collective-permute-start(f32[64,128]{1,0:T(8,128)S(1)} %shard_map.123.refs_0_), channel_id=1, source_target_pairs={{0,16},{1,17},{2,18},{3,19},{4,20},{5,21},{6,22},{7,23},{8,24},{9,... | collective-permute-start | bytes 98312 | tf_op jit(solution)/shard_map/ppermute | solution.py:546
  88.5 5.4 %shard_map.124.refs_0_ = f32[8,4096]{1,0:T(8,128)S(1)} custom-call(bf16[48,4096]{1,0:T(8,128)(2,1)S(1)} %get-tuple-element.90.own_ref.refs_8_, bf16[4096,48]{1,0:T(8,128)(2,1)S(1)} %get-tuple-element.108.near_ref, bf16[16,4096]{1,0:T(8,128)(2,1)S(1)} %get-tuple-element.91.moment_ref, f32[8,4096]{1,0:T(8,128)S(1)} %shard_map.122.refs_0_), custom_call_target="tpu_custom_call", output_to_operand_aliasing={{}: (3, {})} | custom-call | flops 6291456000 | bytes 1048576 | tf_op jit(solution)/shard_map/pallas_call | solution.py:531
  93.9 0.0 collective-permute-done.12.refs_1_
  93.9 0.1 shard_map.125.refs_0_
  94.1 1.6 %collective-permute-start.13 = (f32[128,128]{1,0:T(8,128)S(1)}, f32[128,128]{1,0:T(8,128)S(1)}, u32[]{:S(2)}, u32[]{:S(2)}) collective-permute-start(f32[128,128]{1,0:T(8,128)S(1)} %shard_map.125.refs_0_), channel_id=1, source_target_pairs={{0,4},{1,5},{2,6},{3,7},{4,0},{5,1},{6,2},{7,3},{8,12},{9,13},{10,... | collective-permute-start | bytes 196616 | tf_op jit(solution)/shard_map/ppermute | solution.py:546
  95.6 5.4 %shard_map.126.refs_0_ = f32[8,4096]{1,0:T(8,128)S(1)} custom-call(bf16[48,4096]{1,0:T(8,128)(2,1)S(1)} %get-tuple-element.90.own_ref.refs_8_, bf16[4096,48]{1,0:T(8,128)(2,1)S(1)} %get-tuple-element.108.near_ref, bf16[16,4096]{1,0:T(8,128)(2,1)S(1)} %get-tuple-element.91.moment_ref, f32[8,4096]{1,0:T(8,128)S(1)} %shard_map.124.refs_0_), custom_call_target="tpu_custom_call", output_to_operand_aliasing={{}: (3, {})} | custom-call | flops 6291456000 | bytes 1048576 | tf_op jit(solution)/shard_map/pallas_call | solution.py:531
  101.1 0.0 collective-permute-done.13.refs_1_
  101.1 0.2 shard_map.127.refs_0_
  101.3 1.6 %collective-permute-start.14 = (f32[256,128]{1,0:T(8,128)S(1)}, f32[256,128]{1,0:T(8,128)S(1)}, u32[]{:S(2)}, u32[]{:S(2)}) collective-permute-start(f32[256,128]{1,0:T(8,128)S(1)} %shard_map.127.refs_0_), channel_id=1, source_target_pairs={{0,2},{1,3},{2,0},{3,1},{4,6},{5,7},{6,4},{7,5},{8,10},{9,11},{10,... | collective-permute-start | bytes 393224 | tf_op jit(solution)/shard_map/ppermute | solution.py:546
  102.8 9.0 %shard_map.128.refs_0_ = f32[8,4096]{1,0:T(8,128)S(1)} custom-call(bf16[48,4096]{1,0:T(8,128)(2,1)S(1)} %get-tuple-element.90.own_ref.refs_8_, bf16[4096,48]{1,0:T(8,128)(2,1)S(1)} %get-tuple-element.108.near_ref, bf16[16,4096]{1,0:T(8,128)(2,1)S(1)} %get-tuple-element.91.moment_ref, f32[8,4096]{1,0:T(8,128)S(1)} %shard_map.126.refs_0_), custom_call_target="tpu_custom_call", output_to_operand_aliasing={{}: (3, {})} | custom-call | flops 6291456000 | bytes 1048576 | tf_op jit(solution)/shard_map/pallas_call | solution.py:531
  111.9 0.0 copy-start.3
  111.9 0.0 collective-permute-done.14.refs_1_
  111.9 0.1 collective-permute-start.15
  112.0 0.5 collective-permute-start.16
  112.5 3.6 %shard_map.129.refs_11_ = f32[8,4096]{1,0:T(8,128)S(1)} custom-call(bf16[48,4096]{1,0:T(8,128)(2,1)S(1)} %get-tuple-element.90.own_ref.refs_8_, bf16[4096,48]{1,0:T(8,128)(2,1)S(1)} %get-tuple-element.108.near_ref, bf16[16,4096]{1,0:T(8,128)(2,1)S(1)} %get-tuple-element.91.moment_ref, f32[8,4096]{1,0:T(8,128)S(1)} %shard_map.128.refs_0_), custom_call_target="tpu_custom_call", output_to_operand_aliasing={{}: (3, {})} | custom-call | flops 6291456000 | bytes 1048576 | tf_op jit(solution)/shard_map/pallas_call | solution.py:531
  116.1 0.0 collective-permute-done.15.refs_2_
  116.1 0.0 collective-permute-done.16.refs_3_
  116.1 0.0 copy-done.3
  116.1 22.0 %shard_map.130 = f32[3,32,128]{2,1,0:T(8,128)} custom-call(s32[1]{0:T(128)} %bitcast.me_ref, f32[256,128]{1,0:T(8,128)S(1)} %shard_map.127.refs_0_, f32[256,128]{1,0:T(8,128)S(1)} %collective-permute-done.14.refs_1_, f32[256,128]{1,0:T(8,128)S(1)} %collective-permute-done.15.refs_2_, f32[256,128]{1,0:T(8,128)S(1)} %collective-permute-done.16.refs_3_, ...), custom_call_target="tpu_custom_call" | custom-call | tf_op jit(solution)/shard_map/pallas_call | solution.py:696
Async XLA Ops:
  1.6 18.3 %collective-permute-start.2 = (f32[33,8,128]{2,1,0:T(8,128)S(1)}, f32[33,8,128]{2,1,0:T(8,128)S(1)}, u32[]{:S(2)}, u32[]{:S(2)}) collective-permute-start(f32[33,8,128]{2,1,0:T(8,128)S(1)} %get-tuple-element.63.refs_0_), channel_id=1, source_target_pairs={{0,24},{1,25},{2,26},{3,27},{4,28},{5,29},{6,30},{7,31},{8,16},{9,... | collective-permute-start | bytes 405512 | tf_op jit(solution)/shard_map/ppermute | solution.py:546
  6.7 13.2 %collective-permute-start.1 = (f32[33,8,128]{2,1,0:T(8,128)S(1)}, f32[33,8,128]{2,1,0:T(8,128)S(1)}, u32[]{:S(2)}, u32[]{:S(2)}) collective-permute-start(f32[33,8,128]{2,1,0:T(8,128)S(1)} %get-tuple-element.63.refs_0_), channel_id=1, source_target_pairs={{0,16},{1,17},{2,18},{3,19},{4,20},{5,21},{6,22},{7,23},{8,24},{9,... | collective-permute-start | bytes 405512 | tf_op jit(solution)/shard_map/ppermute | solution.py:546
  6.7 13.2 %collective-permute-start = (f32[33,8,128]{2,1,0:T(8,128)S(1)}, f32[33,8,128]{2,1,0:T(8,128)S(1)}, u32[]{:S(2)}, u32[]{:S(2)}) collective-permute-start(f32[33,8,128]{2,1,0:T(8,128)S(1)} %get-tuple-element.63.refs_0_), channel_id=1, source_target_pairs={{0,8},{1,9},{2,10},{3,11},{4,12},{5,13},{6,14},{7,15},{8,0},{9,1},... | collective-permute-start | bytes 405512 | tf_op jit(solution)/shard_map/ppermute | solution.py:546
  20.7 10.0 %collective-permute-start.3 = (f32[66,8,128]{2,1,0:T(8,128)S(1)}, f32[66,8,128]{2,1,0:T(8,128)S(1)}, u32[]{:S(2)}, u32[]{:S(2)}) collective-permute-start(f32[66,8,128]{2,1,0:T(8,128)S(1)} %get-tuple-element.71.refs_0_), channel_id=1, source_target_pairs={{0,4},{1,5},{2,6},{3,7},{4,0},{5,1},{6,2},{7,3},{8,12},{9,13},{10,... | collective-permute-start | bytes 811016 | tf_op jit(solution)/shard_map/ppermute | solution.py:546
  22.4 8.3 %collective-permute-start.4 = (f32[66,8,128]{2,1,0:T(8,128)S(1)}, f32[66,8,128]{2,1,0:T(8,128)S(1)}, u32[]{:S(2)}, u32[]{:S(2)}) collective-permute-start(f32[66,8,128]{2,1,0:T(8,128)S(1)} %get-tuple-element.73.refs_2_), channel_id=1, source_target_pairs={{0,2},{1,3},{2,0},{3,1},{4,6},{5,7},{6,4},{7,5},{8,10},{9,11},{10,... | collective-permute-start | bytes 811016 | tf_op jit(solution)/shard_map/ppermute | solution.py:546
  30.9 14.6 %collective-permute-start.5 = (f32[132,8,128]{2,1,0:T(8,128)S(1)}, f32[132,8,128]{2,1,0:T(8,128)S(1)}, u32[]{:S(2)}, u32[]{:S(2)}) collective-permute-start(f32[132,8,128]{2,1,0:T(8,128)S(1)} %get-tuple-element.79.refs_0_), channel_id=1, source_target_pairs={{0,2},{1,3},{2,0},{3,1},{4,6},{5,7},{6,4},{7,5},{8,10},{9,11},{10,... | collective-permute-start | bytes 1622024 | tf_op jit(solution)/shard_map/ppermute | solution.py:546
  31.5 14.0 %collective-permute-start.6 = (f32[132,8,128]{2,1,0:T(8,128)S(1)}, f32[132,8,128]{2,1,0:T(8,128)S(1)}, u32[]{:S(2)}, u32[]{:S(2)}) collective-permute-start(f32[132,8,128]{2,1,0:T(8,128)S(1)} %get-tuple-element.81.refs_4_), channel_id=1, source_target_pairs={{0,4},{1,5},{2,6},{3,7},{4,0},{5,1},{6,2},{7,3},{8,12},{9,13},{10,... | collective-permute-start | bytes 1622024 | tf_op jit(solution)/shard_map/ppermute | solution.py:546
  45.4 5.7 %copy-start = (s32[32,16]{0,1:T(8,128)S(1)}, s32[32,16]{0,1:T(8,128)}, u32[]{:S(2)}) copy-start(s32[32,16]{0,1:T(8,128)} %param.15) | copy-start | bytes 6148
  45.4 5.7 %copy-start.1 = (f32[32,128]{1,0:T(8,128)S(1)}, f32[32,128]{1,0:T(8,128)}, u32[]{:S(2)}) copy-start(f32[32,128]{1,0:T(8,128)} %refs_10_.1) | copy-start | bytes 49156
  45.5 5.7 %copy-start.2 = (s32[2,32]{1,0:T(2,128)S(1)}, s32[2,32]{1,0:T(2,128)}, u32[]{:S(2)}) copy-start(s32[2,32]{1,0:T(2,128)} %constant.10.clone.refs_9_) | copy-start | bytes 772
  45.5 5.6 %collective-permute-start.7 = (f32[132,8,128]{2,1,0:T(8,128)S(1)}, f32[132,8,128]{2,1,0:T(8,128)S(1)}, u32[]{:S(2)}, u32[]{:S(2)}) collective-permute-start(f32[132,8,128]{2,1,0:T(8,128)S(1)} %get-tuple-element.79.refs_0_), channel_id=1, source_target_pairs={{0,1},{1,0},{2,3},{3,2},{4,5},{5,4},{6,7},{7,6},{8,9},{9,8},{10,11... | collective-permute-start | bytes 1622024 | tf_op jit(solution)/shard_map/ppermute | solution.py:546
  45.6 5.5 %collective-permute-start.8 = (f32[132,8,128]{2,1,0:T(8,128)S(1)}, f32[132,8,128]{2,1,0:T(8,128)S(1)}, u32[]{:S(2)}, u32[]{:S(2)}) collective-permute-start(f32[132,8,128]{2,1,0:T(8,128)S(1)} %collective-permute-done.5.refs_1_), channel_id=1, source_target_pairs={{0,1},{1,0},{2,3},{3,2},{4,5},{5,4},{6,7},{7,6},{8,9},{9,8},{10,11... | collective-permute-start | bytes 1622024 | tf_op jit(solution)/shard_map/ppermute | solution.py:546
  46.1 5.1 %collective-permute-start.9 = (f32[132,8,128]{2,1,0:T(8,128)S(1)}, f32[132,8,128]{2,1,0:T(8,128)S(1)}, u32[]{:S(2)}, u32[]{:S(2)}) collective-permute-start(f32[132,8,128]{2,1,0:T(8,128)S(1)} %get-tuple-element.81.refs_4_), channel_id=1, source_target_pairs={{0,1},{1,0},{2,3},{3,2},{4,5},{5,4},{6,7},{7,6},{8,9},{9,8},{10,11... | collective-permute-start | bytes 1622024 | tf_op jit(solution)/shard_map/ppermute | solution.py:546
  46.1 5.0 %collective-permute-start.10 = (f32[132,8,128]{2,1,0:T(8,128)S(1)}, f32[132,8,128]{2,1,0:T(8,128)S(1)}, u32[]{:S(2)}, u32[]{:S(2)}) collective-permute-start(f32[132,8,128]{2,1,0:T(8,128)S(1)} %collective-permute-done.6.refs_5_), channel_id=1, source_target_pairs={{0,1},{1,0},{2,3},{3,2},{4,5},{5,4},{6,7},{7,6},{8,9},{9,8},{10,11... | collective-permute-start | bytes 1622024 | tf_op jit(solution)/shard_map/ppermute | solution.py:546
  77.6 7.8 %collective-permute-start.11 = (f32[32,128]{1,0:T(8,128)S(1)}, f32[32,128]{1,0:T(8,128)S(1)}, u32[]{:S(2)}, u32[]{:S(2)}) collective-permute-start(f32[32,128]{1,0:T(8,128)S(1)} %get-tuple-element.92.weight_ref.refs_0_), channel_id=1, source_target_pairs={{0,8},{1,9},{2,10},{3,11},{4,12},{5,13},{6,14},{7,15},{8,0},{9,1},... | collective-permute-start | bytes 49160 | tf_op jit(solution)/shard_map/ppermute | solution.py:546
  85.6 8.4 %collective-permute-start.12 = (f32[64,128]{1,0:T(8,128)S(1)}, f32[64,128]{1,0:T(8,128)S(1)}, u32[]{:S(2)}, u32[]{:S(2)}) collective-permute-start(f32[64,128]{1,0:T(8,128)S(1)} %shard_map.123.refs_0_), channel_id=1, source_target_pairs={{0,16},{1,17},{2,18},{3,19},{4,20},{5,21},{6,22},{7,23},{8,24},{9,... | collective-permute-start | bytes 98312 | tf_op jit(solution)/shard_map/ppermute | solution.py:546
  94.1 7.0 %collective-permute-start.13 = (f32[128,128]{1,0:T(8,128)S(1)}, f32[128,128]{1,0:T(8,128)S(1)}, u32[]{:S(2)}, u32[]{:S(2)}) collective-permute-start(f32[128,128]{1,0:T(8,128)S(1)} %shard_map.125.refs_0_), channel_id=1, source_target_pairs={{0,4},{1,5},{2,6},{3,7},{4,0},{5,1},{6,2},{7,3},{8,12},{9,13},{10,... | collective-permute-start | bytes 196616 | tf_op jit(solution)/shard_map/ppermute | solution.py:546
  101.3 10.6 %collective-permute-start.14 = (f32[256,128]{1,0:T(8,128)S(1)}, f32[256,128]{1,0:T(8,128)S(1)}, u32[]{:S(2)}, u32[]{:S(2)}) collective-permute-start(f32[256,128]{1,0:T(8,128)S(1)} %shard_map.127.refs_0_), channel_id=1, source_target_pairs={{0,2},{1,3},{2,0},{3,1},{4,6},{5,7},{6,4},{7,5},{8,10},{9,11},{10,... | collective-permute-start | bytes 393224 | tf_op jit(solution)/shard_map/ppermute | solution.py:546
  111.9 4.2 %copy-start.3 = (s32[32]{0:T(128)S(1)}, s32[32]{0:T(128)}, u32[]{:S(2)}) copy-start(s32[32]{0:T(128)} %refs_6_.1) | copy-start | bytes 388
  111.9 4.2 %collective-permute-start.15 = (f32[256,128]{1,0:T(8,128)S(1)}, f32[256,128]{1,0:T(8,128)S(1)}, u32[]{:S(2)}, u32[]{:S(2)}) collective-permute-start(f32[256,128]{1,0:T(8,128)S(1)} %shard_map.127.refs_0_), channel_id=1, source_target_pairs={{0,1},{1,0},{2,3},{3,2},{4,5},{5,4},{6,7},{7,6},{8,9},{9,8},{10,11... | collective-permute-start | bytes 393224 | tf_op jit(solution)/shard_map/ppermute | solution.py:546
  112.0 4.1 %collective-permute-start.16 = (f32[256,128]{1,0:T(8,128)S(1)}, f32[256,128]{1,0:T(8,128)S(1)}, u32[]{:S(2)}, u32[]{:S(2)}) collective-permute-start(f32[256,128]{1,0:T(8,128)S(1)} %collective-permute-done.14.refs_1_), channel_id=1, source_target_pairs={{0,1},{1,0},{2,3},{3,2},{4,5},{5,4},{6,7},{7,6},{8,9},{9,8},{10,11... | collective-permute-start | bytes 393224 | tf_op jit(solution)/shard_map/ppermute | solution.py:546
